TPU v7x, 32 devices: a whole 2x2x4 slice. The times are simulated.
32 devices in a mesh: atoms: 16 (over z, y, x), rep: 2 (over core).
Axes of the slice: x: 2, y: 2, z: 4, core: 2. Of those that a mesh axis runs over, the one named last changes fastest.
Arguments:
- scalars_in: float32 [16384, 128], P(('atoms', 'rep')), may hold values from -6 to 6
- vectors_in: float32 [3, 16384, 128], P(None, ('atoms', 'rep')), may hold values from -6 to 6
- positions: float32 [3, 16384], P(None, ('atoms', 'rep')), may hold values from 0 to 3
- cotan_scalar: float32 [16384, 128], P(('atoms', 'rep')), may hold values from -6 to 6
- cotan_vector: float32 [3, 16384, 128], P(None, ('atoms', 'rep')), may hold values from -6 to 6
- target_energy: float32 [16384], P(('atoms', 'rep'))
- forces: float32 [3, 16384], P(None, ('atoms', 'rep'))
- elements: int32 [16384], P(('atoms', 'rep')), may hold values from 0 to 99
- crystal: int32 [16384], P(('atoms', 'rep')), may hold values from 0 to 511, never falling along the last dimension, each value on 1 to 64 neighbouring positions
- lattice: float32 [512, 9], replicated, may hold values from -0.5 to 4.5, as said below
- edge_src: int32 [262144], P(('atoms', 'rep')), may hold values from 0 to 1023, as said below
- edge_dst: int32 [262144], P(('atoms', 'rep')), may hold values from 0 to 511, as said below
- edge_shift: int32 [3, 262144], P(None, ('atoms', 'rep')), may hold values from -1 to 1
- edge_count: int32 [32], P(('atoms', 'rep')), may hold values from 4096 to 8192, as said below
- send_rows: int32 [32, 8, 64], P(('atoms', 'rep')), may hold values from 0 to 511, as said below
- params: float32 [189440], P(('atoms', 'rep'))
- first_moment: float32 [189440], P(('atoms', 'rep')), may hold values from -40 to 40
- second_moment: float32 [189440], P(('atoms', 'rep')), may hold values from 41.3696 to 165.4784
Outputs:
- scalars_out: float32 [16384, 128], P(('atoms', 'rep'))
- vectors_out: float32 [3, 16384, 128], P(None, ('atoms', 'rep'))
- grad_scalars: float32 [16384, 128], P(('atoms', 'rep'))
- grad_vectors: float32 [3, 16384, 128], P(None, ('atoms', 'rep'))
- grad_positions: float32 [3, 16384], P(None, ('atoms', 'rep'))
- element_mean: float32 [100], replicated
- force_scale: float32 [], replicated
- grad_params: float32 [189440], P(('atoms', 'rep'))
- moment_one: float32 [189440], P(('atoms', 'rep'))
- moment_two: float32 [189440], P(('atoms', 'rep'))
- params_new: float32 [189440], P(('atoms', 'rep'))
- params_low: bfloat16 [189440], P(('atoms', 'rep'))
- weight_norms: float32 [7], replicated
- update_norms: float32 [7], replicated
Inputs may be any that keep to these rules, and one draw needn't show every extreme that they name: Rows of one list send_rows[p, j] are distinct. `edge_src`: A value of 512 or more names a received slot whose sending device exists. `edge_dst`: within the slots of one device the values never fall. `edge_count`: some device uses all its 8192 slots. `lattice`: the diagonal lies between 3 and 4.5, the other entries between -0.5 and 0.5.
All inputs are finite; a program needn't handle non-finite values.
Results may differ from a plain program's by a relative error of at most 0.001.
Values sent between devices are 32-bit elements; how exact they have to be, the bound alone decides.
A program may use at most 128 MiB of HBM per device.

v0:
```python
import math

import jax
import jax.numpy as jnp
from jax import lax
from jax.sharding import PartitionSpec as P

F = 128
R = 20
HOPS = 4
ELEMS = 100
STEP = 10
GROUPS = 7


CUTOFF = 5.0
BETA_ONE = 0.9
BETA_TWO = 0.99
RATE = 0.3
DECAY = 0.01
EPSILON = 1e-06
PRECISION_MAX = lax.Precision.HIGHEST


def passed_along(shard, axis, by):
    devices = lax.axis_size(axis)
    pairs = [(i, i + by) for i in range(devices) if 0 <= i + by < devices]
    return lax.ppermute(shard, axis, pairs)


def product(left, right):
    return jnp.dot(left, right, precision=PRECISION_MAX, preferred_element_type=jnp.float32)


def layout():
    shapes = [(F, F), (F, 3 * F), (R, 3 * F), (F, 2 * F), (2 * F, F), (F, 3 * F)]
    lengths = [F, 3 * F, 3 * F, F, 3 * F, F]
    return (shapes, lengths)


def unpack(all_params):
    shapes, lengths = layout()
    result = []
    start = 0
    for shape in shapes:
        count = shape[0] * shape[1]
        result.append(all_params[start : start + count].reshape(shape))
        start += count
    for length in lengths:
        result.append(all_params[start : start + length])
        start += length
    return result


def group_ids(index):
    shapes, lengths = layout()
    labels = jnp.zeros(index.shape, jnp.int32)
    start = 0
    for shape in shapes:
        start += shape[0] * shape[1]
        labels = labels + (index >= start).astype(jnp.int32)
    return labels


def features(scalars, w_one, b_one, w_two, b_two):
    return product(jax.nn.silu(product(scalars, w_one) + b_one), w_two) + b_two


def periodic(shifts, cells):
    columns = []
    for comp in range(3):
        columns.append(
            shifts[..., 0, :] * cells[..., comp]
            + shifts[..., 1, :] * cells[..., 3 + comp]
            + shifts[..., 2, :] * cells[..., 6 + comp]
        )
    return jnp.stack(columns, axis=-2)


def selector(indices, count):
    return (indices[:, None] == jnp.arange(count, dtype=jnp.int32)[None, :]).astype(jnp.float32)


def take_rows(select, table_v):
    return jnp.einsum("ka,cad->ckd", select, table_v, precision=PRECISION_MAX)


def put_rows(select, rows_v):
    return jnp.einsum("ka,ckd->cad", select, rows_v, precision=PRECISION_MAX)


def messages(x_src, v_src, relative, used, w_filter, b_filter):
    distance = jnp.sqrt(jnp.maximum(jnp.sum(relative * relative, axis=0), 0.25))
    heading = relative / distance[None, :]
    orders = jnp.arange(1, R + 1).astype(jnp.float32)
    radial = jnp.sin(orders[None, :] * (jnp.pi / CUTOFF) * distance[:, None]) / distance[:, None]
    envelope = (
        jnp.where(distance < CUTOFF, 0.5 * (jnp.cos(jnp.pi * distance / CUTOFF) + 1.0), 0.0) * used
    )
    filter_rows = (product(radial, w_filter) + b_filter) * envelope[:, None]
    product_rows = x_src * filter_rows
    scalar = product_rows[:, :F]
    vector = (
        product_rows[:, F : 2 * F][None] * heading[:, :, None]
        + product_rows[:, 2 * F :][None] * v_src
    )
    return (scalar, vector)


def edge_sums(table_x, table_v, table_p, w_filter, b_filter, item, atoms_count):
    src_rows, dst_local, offsets, used = item
    table_rows = table_x.shape[0]
    block_len = src_rows.shape[0]
    pick_src = selector(src_rows, table_rows)
    pick_dst = selector(dst_local, atoms_count)
    joined = jnp.concatenate(
        [
            table_x,
            jnp.transpose(table_v, (1, 0, 2)).reshape(table_rows, 3 * F),
            jnp.transpose(table_p),
        ],
        axis=1,
    )
    gathered = product(pick_src, joined)
    x_src = gathered[:, : 3 * F]
    v_src = jnp.transpose(gathered[:, 3 * F : 6 * F].reshape(block_len, 3, F), (1, 0, 2))
    p_src = jnp.transpose(gathered[:, 6 * F :])
    p_dst = jnp.transpose(product(pick_dst, jnp.transpose(table_p[:, :atoms_count])))
    relative = p_src + offsets - p_dst
    scalar, vector = messages(x_src, v_src, relative, used, w_filter, b_filter)
    sums = product(
        jnp.transpose(pick_dst),
        jnp.concatenate(
            [scalar, jnp.transpose(vector, (1, 0, 2)).reshape(block_len, 3 * F)], axis=1
        ),
    )
    sum_scalar = sums[:, :F]
    sum_vector = jnp.transpose(sums[:, F:].reshape(atoms_count, 3, F), (1, 0, 2))
    return (sum_scalar, sum_vector)


def update(s_one, v_one, w_mixing, u_one, c_one, u_two, c_two):
    atoms_count = s_one.shape[0]
    mixing = product(v_one.reshape(3 * atoms_count, F), w_mixing).reshape(3, atoms_count, 2 * F)
    v_linear = mixing[..., :F]
    w_linear = mixing[..., F:]
    magnitude = jnp.sqrt(jnp.sum(v_linear * v_linear, axis=0) + 1.0)
    hidden = jax.nn.silu(product(jnp.concatenate([s_one, magnitude], axis=1), u_one) + c_one)
    gating = product(hidden, u_two) + c_two
    inner_prod = jnp.sum(v_linear * w_linear, axis=0)
    s_two = s_one + gating[:, 2 * F :] + gating[:, F : 2 * F] * inner_prod
    v_two = v_one + gating[:, :F][None] * w_linear
    return (s_two, v_two)


def body(
    scalars_in,
    vectors_in,
    positions,
    cotan_scalar,
    cotan_vector,
    target_energy,
    forces,
    elements,
    crystal,
    lattice,
    edge_src,
    edge_dst,
    edge_shift,
    edge_count,
    send_rows,
    params,
    first_moment,
    second_moment,
):
    atoms_dev = scalars_in.shape[0]
    edges_dev = edge_src.shape[0]
    capacity = send_rows.shape[2]
    all_params = lax.all_gather(params, ("atoms", "rep"), axis=0, tiled=True)
    w_one, w_two, w_filter, w_mixing, u_one, u_two, b_one, b_two, b_filter, c_one, c_two, w_read = (
        unpack(all_params)
    )
    onehot = (elements[:, None] == jnp.arange(ELEMS, dtype=jnp.int32)[None, :]).astype(jnp.float32)
    elem_total = product(target_energy[None, :], onehot)[0]
    elem_count = jnp.sum(onehot, axis=0)
    force_square = jnp.sum(forces * forces)
    elem_total, elem_count, force_square = lax.psum(
        (elem_total, elem_count, force_square), ("atoms", "rep")
    )
    element_mean = elem_total / jnp.maximum(elem_count, 1.0)
    total_atoms = atoms_dev * lax.axis_size(("atoms", "rep"))
    force_scale = jnp.sqrt(force_square / (3.0 * total_atoms) + 1e-06)
    goal = (target_energy - product(onehot, element_mean[:, None])[:, 0]) / force_scale
    hop_offsets = [hop_index + 1 for hop_index in range(HOPS)] + [
        -(hop_index + 1) for hop_index in range(HOPS)
    ]
    row_lists = send_rows[0]
    row_pickers = [selector(row_lists[hop_index], atoms_dev) for hop_index in range(2 * HOPS)]
    x_own, pull_own = jax.vjp(features, scalars_in, w_one, b_one, w_two, b_two)
    received = []
    for hop_index in range(2 * HOPS):
        picker = row_pickers[hop_index]
        received.append(
            passed_along(
                (
                    product(picker, x_own),
                    take_rows(picker, vectors_in),
                    jnp.transpose(product(picker, jnp.transpose(positions))),
                ),
                ("atoms", "rep"),
                hop_offsets[hop_index],
            )
        )
    halo_x = jnp.concatenate([entry[0] for entry in received], axis=0)
    halo_v = jnp.concatenate([entry[1] for entry in received], axis=1)
    halo_p = jnp.concatenate([entry[2] for entry in received], axis=1)
    table_x = jnp.concatenate([x_own, halo_x], axis=0)
    table_v = jnp.concatenate([vectors_in, halo_v], axis=1)
    table_p = jnp.concatenate([positions, halo_p], axis=1)
    valid = (jnp.arange(edges_dev, dtype=jnp.int32) < edge_count[0]).astype(jnp.float32)
    atom_cells = lattice[crystal]
    block_len = math.gcd(edges_dev, 2048)
    blocks = edges_dev // block_len
    shift_blocks = jnp.transpose(
        edge_shift.astype(jnp.float32).reshape(3, blocks, block_len), (1, 0, 2)
    )
    dst_blocks = edge_dst.reshape(blocks, block_len)

    def offset_block(item):
        shifts, dst_rows = item
        cells = product(selector(dst_rows, atoms_dev), atom_cells)
        return periodic(shifts, cells)

    offset_blocks = lax.map(offset_block, (shift_blocks, dst_blocks))
    edge_blocks = (
        edge_src.reshape(blocks, block_len),
        dst_blocks,
        offset_blocks,
        valid.reshape(blocks, block_len),
    )

    def forward_step(carry, item):
        add_s, add_v = edge_sums(table_x, table_v, table_p, w_filter, b_filter, item, atoms_dev)
        return ((carry[0] + add_s, carry[1] + add_v), None)

    start_sums = (jnp.zeros((atoms_dev, F), jnp.float32), jnp.zeros_like(vectors_in))
    (delta_s, delta_v), ignored = lax.scan(forward_step, start_sums, edge_blocks)
    s_one = scalars_in + delta_s
    v_one = vectors_in + delta_v

    def head(s_first, v_first, head_weights):
        s_two, v_two = update(
            s_first,
            v_first,
            head_weights[0],
            head_weights[1],
            head_weights[2],
            head_weights[3],
            head_weights[4],
        )
        energy = product(s_two, head_weights[5][:, None])[:, 0]
        objective = (
            jnp.sum(cotan_scalar * s_two)
            + jnp.sum(cotan_vector * v_two)
            + 0.5 * jnp.sum((energy - goal) ** 2)
        )
        return (objective, (s_two, v_two))

    objective, pull_head, outputs = jax.vjp(
        head, s_one, v_one, (w_mixing, u_one, c_one, u_two, c_two, w_read), has_aux=True
    )
    grad_s_one, grad_v_one, head_grads = pull_head(jnp.ones((), jnp.float32))

    def backward_step(carry, item):

        def block_sums(tab_x, tab_v, tab_p, filter_w, filter_b):
            return edge_sums(tab_x, tab_v, tab_p, filter_w, filter_b, item, atoms_dev)

        block_out, pull_block = jax.vjp(block_sums, table_x, table_v, table_p, w_filter, b_filter)
        grads = pull_block((grad_s_one, grad_v_one))
        return (tuple((total + addend for total, addend in zip(carry, grads))), None)

    start_grads = (
        jnp.zeros_like(table_x),
        jnp.zeros_like(table_v),
        jnp.zeros_like(table_p),
        jnp.zeros_like(w_filter),
        jnp.zeros_like(b_filter),
    )
    totals, ignored = lax.scan(backward_step, start_grads, edge_blocks)
    grad_table_x, grad_table_v, grad_table_p, grad_filter_w, grad_filter_b = totals
    grad_x_own = grad_table_x[:atoms_dev]
    grad_v_own = grad_table_v[:, :atoms_dev]
    grad_p_own = grad_table_p[:, :atoms_dev]
    grad_x_halo = grad_table_x[atoms_dev:]
    grad_v_halo = grad_table_v[:, atoms_dev:]
    grad_p_halo = grad_table_p[:, atoms_dev:]
    grad_s_extra = jnp.zeros_like(scalars_in)
    for hop_index in range(2 * HOPS):
        lower = hop_index * capacity
        upper = lower + capacity
        returned = passed_along(
            (grad_x_halo[lower:upper], grad_v_halo[:, lower:upper], grad_p_halo[:, lower:upper]),
            ("atoms", "rep"),
            -hop_offsets[hop_index],
        )
        picker = row_pickers[hop_index]
        grad_x_own = grad_x_own + product(jnp.transpose(picker), returned[0])
        grad_v_own = grad_v_own + put_rows(picker, returned[1])
        grad_p_own = grad_p_own + jnp.transpose(
            product(jnp.transpose(picker), jnp.transpose(returned[2]))
        )
    grad_s_phi, grad_w_one, grad_b_one, grad_w_two, grad_b_two = pull_own(grad_x_own)
    grad_scalars = grad_s_one + grad_s_phi + grad_s_extra
    grad_vectors = grad_v_one + grad_v_own
    grad_mixing, grad_u_one, grad_c_one, grad_u_two, grad_c_two, grad_read = head_grads
    pieces_flat = [
        grad_w_one,
        grad_w_two,
        grad_filter_w,
        grad_mixing,
        grad_u_one,
        grad_u_two,
        grad_b_one,
        grad_b_two,
        grad_filter_b,
        grad_c_one,
        grad_c_two,
        grad_read,
    ]
    grad_flat = jnp.concatenate([entry.reshape(-1) for entry in pieces_flat])
    grad_shard = lax.psum_scatter(grad_flat, ("atoms", "rep"), scatter_dimension=0, tiled=True)
    shard_len = params.shape[0]
    moment_one = BETA_ONE * first_moment + (1.0 - BETA_ONE) * grad_shard
    moment_two = BETA_TWO * second_moment + (1.0 - BETA_TWO) * grad_shard * grad_shard
    direction = (
        moment_one
        / (1.0 - BETA_ONE**STEP)
        / (jnp.sqrt(moment_two / (1.0 - BETA_TWO**STEP)) + EPSILON)
        + DECAY * params
    )
    first_index = lax.axis_index(("atoms", "rep")) * shard_len
    labels = group_ids(first_index + jnp.arange(shard_len, dtype=jnp.int32))
    member = (labels[None, :] == jnp.arange(GROUPS, dtype=jnp.int32)[:, None]).astype(jnp.float32)
    weight_square = product(member, (params * params)[:, None])[:, 0]
    update_square = product(member, (direction * direction)[:, None])[:, 0]
    weight_square, update_square = lax.psum((weight_square, update_square), ("atoms", "rep"))
    weight_norms = jnp.sqrt(weight_square)
    update_norms = jnp.sqrt(update_square)
    trust_ratio = weight_norms / update_norms
    params_new = params - RATE * product(trust_ratio[None, :], member)[0] * direction
    return (
        outputs[0],
        outputs[1],
        grad_scalars,
        grad_vectors,
        grad_p_own,
        element_mean,
        force_scale,
        grad_shard,
        moment_one,
        moment_two,
        params_new,
        params_new.astype(jnp.bfloat16),
        weight_norms,
        update_norms,
    )


def solution(mesh):
    in_specs = (
        P(("atoms", "rep"), None),
        P(None, ("atoms", "rep"), None),
        P(None, ("atoms", "rep")),
        P(("atoms", "rep"), None),
        P(None, ("atoms", "rep"), None),
        P(("atoms", "rep")),
        P(None, ("atoms", "rep")),
        P(("atoms", "rep")),
        P(("atoms", "rep")),
        P(),
        P(("atoms", "rep")),
        P(("atoms", "rep")),
        P(None, ("atoms", "rep")),
        P(("atoms", "rep")),
        P(("atoms", "rep"), None, None),
        P(("atoms", "rep")),
        P(("atoms", "rep")),
        P(("atoms", "rep")),
    )
    out_specs = (
        P(("atoms", "rep"), None),
        P(None, ("atoms", "rep"), None),
        P(("atoms", "rep"), None),
        P(None, ("atoms", "rep"), None),
        P(None, ("atoms", "rep")),
        P(),
        P(),
        P(("atoms", "rep")),
        P(("atoms", "rep")),
        P(("atoms", "rep")),
        P(("atoms", "rep")),
        P(("atoms", "rep")),
        P(),
        P(),
    )
    return jax.shard_map(body, mesh=mesh, in_specs=in_specs, out_specs=out_specs, check_vma=False)
```

profile of v0, /device:TPU:0, one launch (start us, length us, event | category | flops | bytes accessed | tf_op | source)
XLA Modules:
  0.0 878.1 jit_solution(15454379130290035469)
XLA Ops:
  48.3 11.7 %while.47 = (s32[]{:T(128)}, f32[4,3,2048]{2,1,0:T(4,128)}, f32[4,3,2048]{2,1,0:T(4,128)S(1)}, s32[4,2048]{1,0:T(4,128)S(1)}, f32[512,9]{0,1:T(8,128)S(1)}, /*index=5*/s32[]{:T(128)}, s32[]{:T(128)}, s32[]{}, s32[]{}) while((s32[]{:T(128)}, f32[4,3,2048]{2,1,0:T(4,128)}, f32[4,3,2048]{2,1,0:T(4,128)S(1)}, s32[4,2048]{1,0:T(4,128)S(1)}, ...), condition=%wide.region_1.0_spmd, body=%wide.region_0.0_spmd.sunk | while | flops 114337792 | bytes 297605 | solution.py:234
  62.3 40.1 %all-reduce.16 = (f32[100]{0:T(128)S(1)}, f32[100]{0:T(128)S(1)}, f32[]{:T(128)}) all-reduce(f32[100]{0:T(128)S(1)} %convolution_bitcast_fusion.27, f32[100]{0:T(128)S(1)} %convert_reduce_fusion, f32[]{:T(128)} %multiply_reduce_fusion.11), channel_id=1, replica_groups=mesh['atoms'=16,'rep'=2] {'atoms','rep'}, use_global_device_ids=true, to_apply=%region_7.8 | all-reduce | flops 201 | bytes 1608 | tf_op jit(solution)/shard_map/psum | solution.py:187
  172.1 6.3 collective-permute-start.1
  214.7 115.2 %while.48 = (s32[]{:T(128)}, f32[512,128]{0,1:T(8,128)}, f32[3,512,128]{1,2,0:T(8,128)S(1)}, s32[4,2048]{1,0:T(4,128)S(1)}, s32[4,2048]{1,0:T(4,128)}, /*index=5...) while((s32[]{:T(128)}, f32[512,128]{0,1:T(8,128)}, ...), condition=%wide.region_4.0_spmd.clone, body=%wide.region_2.4_spmd.clone.sunk | while | flops 26082404352 | bytes 47023920 | solution.py:247
  215.9 13.4 %fusion.403 = f32[2048,771]{0,1:T(8,128)S(1)} fusion(f32[1024,771]{1,0:T(8,128)} %get-tuple-element.1227, s32[2048]{0:T(1024)S(1)} %bitcast.475), kind=kOutput, calls=%fused_computation.35.clone.1 | convolution fusion | flops 19404947456 | bytes 9482240 | tf_op jit(solution)/shard_map/while/body/eval_jaxpr/dot_general | solution.py:32
  243.9 13.4 %fusion.403 = f32[2048,771]{0,1:T(8,128)S(1)} fusion(f32[1024,771]{1,0:T(8,128)} %get-tuple-element.1227, s32[2048]{0:T(1024)S(1)} %bitcast.475), kind=kOutput, calls=%fused_computation.35.clone.1 | convolution fusion | flops 19404947456 | bytes 9482240 | tf_op jit(solution)/shard_map/while/body/eval_jaxpr/dot_general | solution.py:32
  272.8 13.4 %fusion.403 = f32[2048,771]{0,1:T(8,128)S(1)} fusion(f32[1024,771]{1,0:T(8,128)} %get-tuple-element.1227, s32[2048]{0:T(1024)S(1)} %bitcast.475), kind=kOutput, calls=%fused_computation.35.clone.1 | convolution fusion | flops 19404947456 | bytes 9482240 | tf_op jit(solution)/shard_map/while/body/eval_jaxpr/dot_general | solution.py:32
  301.7 13.4 %fusion.403 = f32[2048,771]{0,1:T(8,128)S(1)} fusion(f32[1024,771]{1,0:T(8,128)} %get-tuple-element.1227, s32[2048]{0:T(1024)S(1)} %bitcast.475), kind=kOutput, calls=%fused_computation.35.clone.1 | convolution fusion | flops 19404947456 | bytes 9482240 | tf_op jit(solution)/shard_map/while/body/eval_jaxpr/dot_general | solution.py:32
  362.4 223.6 %while.49 = (s32[]{:T(128)}, f32[1024,384]{0,1:T(8,128)}, f32[3,1024,128]{1,2,0:T(8,128)}, f32[3,1024]{1,0:T(4,128)S(1)}, f32[20,384]{1,0:T(8,128)S(1)}, /*index...) while((s32[]{:T(128)}, f32[1024,384]{0,1:T(8,128)}, ...), condition=%wide.region_23.24_spmd.clone, body=%wide.region_13.23_spmd.clone.sunk | while | flops 45919633408 | bytes 158194224 | solution.py:290
  363.4 12.5 %fusion.417 = f32[2048,771]{0,1:T(8,128)S(1)} fusion(f32[1024,771]{1,0:T(8,128)} %get-tuple-element.1280, s32[2048]{0:T(1024)S(1)} %bitcast.471), kind=kOutput, calls=%fused_computation.71.clone.1 | convolution fusion | flops 19404947456 | bytes 9482240 | tf_op jit(solution)/shard_map/while/body/eval_jaxpr/jvp()/dot_general | solution.py:32
  400.7 10.9 %fusion.422 = f32[1024,771]{0,1:T(8,128)S(1)} fusion(f32[2048,384]{0,1:T(8,128)S(1)} %copy-done, f32[2048,384]{0,1:T(8,128)S(1)} %copy-done.1, f32[2048,3]{0,1:T(4,128)S(1)} %bitcast.463, s32[2048]{0:T(1024)S(1)} %bitcast.472), kind=kOutput, calls=%fused_computation.70.clone.1 | convolution fusion | flops 19408105472 | bytes 9482240 | tf_op jit(solution)/shard_map/while/body/eval_jaxpr/transpose(jvp())/dot_general | solution.py:32
  417.4 12.5 %fusion.417 = f32[2048,771]{0,1:T(8,128)S(1)} fusion(f32[1024,771]{1,0:T(8,128)} %get-tuple-element.1280, s32[2048]{0:T(1024)S(1)} %bitcast.471), kind=kOutput, calls=%fused_computation.71.clone.1 | convolution fusion | flops 19404947456 | bytes 9482240 | tf_op jit(solution)/shard_map/while/body/eval_jaxpr/jvp()/dot_general | solution.py:32
  454.5 11.1 %fusion.422 = f32[1024,771]{0,1:T(8,128)S(1)} fusion(f32[2048,384]{0,1:T(8,128)S(1)} %copy-done, f32[2048,384]{0,1:T(8,128)S(1)} %copy-done.1, f32[2048,3]{0,1:T(4,128)S(1)} %bitcast.463, s32[2048]{0:T(1024)S(1)} %bitcast.472), kind=kOutput, calls=%fused_computation.70.clone.1 | convolution fusion | flops 19408105472 | bytes 9482240 | tf_op jit(solution)/shard_map/while/body/eval_jaxpr/transpose(jvp())/dot_general | solution.py:32
  471.1 12.5 %fusion.417 = f32[2048,771]{0,1:T(8,128)S(1)} fusion(f32[1024,771]{1,0:T(8,128)} %get-tuple-element.1280, s32[2048]{0:T(1024)S(1)} %bitcast.471), kind=kOutput, calls=%fused_computation.71.clone.1 | convolution fusion | flops 19404947456 | bytes 9482240 | tf_op jit(solution)/shard_map/while/body/eval_jaxpr/jvp()/dot_general | solution.py:32
  508.5 10.9 %fusion.422 = f32[1024,771]{0,1:T(8,128)S(1)} fusion(f32[2048,384]{0,1:T(8,128)S(1)} %copy-done, f32[2048,384]{0,1:T(8,128)S(1)} %copy-done.1, f32[2048,3]{0,1:T(4,128)S(1)} %bitcast.463, s32[2048]{0:T(1024)S(1)} %bitcast.472), kind=kOutput, calls=%fused_computation.70.clone.1 | convolution fusion | flops 19408105472 | bytes 9482240 | tf_op jit(solution)/shard_map/while/body/eval_jaxpr/transpose(jvp())/dot_general | solution.py:32
  524.9 12.5 %fusion.417 = f32[2048,771]{0,1:T(8,128)S(1)} fusion(f32[1024,771]{1,0:T(8,128)} %get-tuple-element.1280, s32[2048]{0:T(1024)S(1)} %bitcast.471), kind=kOutput, calls=%fused_computation.71.clone.1 | convolution fusion | flops 19404947456 | bytes 9482240 | tf_op jit(solution)/shard_map/while/body/eval_jaxpr/jvp()/dot_general | solution.py:32
  562.2 10.9 %fusion.422 = f32[1024,771]{0,1:T(8,128)S(1)} fusion(f32[2048,384]{0,1:T(8,128)S(1)} %copy-done, f32[2048,384]{0,1:T(8,128)S(1)} %copy-done.1, f32[2048,3]{0,1:T(4,128)S(1)} %bitcast.463, s32[2048]{0:T(1024)S(1)} %bitcast.472), kind=kOutput, calls=%fused_computation.70.clone.1 | convolution fusion | flops 19408105472 | bytes 9482240 | tf_op jit(solution)/shard_map/while/body/eval_jaxpr/transpose(jvp())/dot_general | solution.py:32
  599.3 7.6 collective-permute-start.47
  612.6 5.2 collective-permute-start.46
  628.0 8.8 %collective-permute-done.43 = f32[3,64]{1,0:T(4,128)S(1)} collective-permute-done((f32[3,64]{1,0:T(4,128)S(1)}, f32[3,64]{1,0:T(4,128)S(1)}, u32[]{:S(2)}, u32[]{:S(2)}) %collective-permute-start.43) | collective-permute-done | bytes 800 | tf_op jit(solution)/shard_map/ppermute | solution.py:28
  657.3 5.4 collective-permute-start.30
  672.0 5.8 collective-permute-start.39
  714.0 112.1 %all-reduce.22.cloned.1.call-done = f32[189440]{0:T(1024)} async-done(((f32[189440]{0:T(1024)}), f32[189440]{0:T(1024)}) %all-reduce.22.cloned.1.call-update) | async-done | bytes 757776
  829.2 39.8 %all-reduce.15 = (f32[7]{0:T(128)S(1)}, f32[7]{0:T(128)S(1)}) all-reduce(f32[7]{0:T(128)S(1)} %convolution_bitcast_fusion.29, f32[7]{0:T(128)S(1)} %convolution_bitcast_fusion.28), channel_id=1, replica_groups=mesh['atoms'=16,'rep'=2] {'atoms','rep'}, use_global_device_ids=true, to_apply=%region_29.30 | all-reduce | flops 14 | bytes 112 | tf_op jit(solution)/shard_map/psum | solution.py:347
  (664 shorter events, 469.7 us)
Async XLA Ops:
  7.2 142.0 %all-reduce.20.cloned.1.call-start = ((), (), s32[]{:S(2)}) async-start(), calls=%async_computation | async-start | bytes 1515520
  9.3 816.9 %all-reduce.22.cloned.1.call-start = ((), (), s32[]{:S(2)}) async-start(), calls=%async_computation.1 | async-start | bytes 1515520
  12.0 116.3 %collective-permute-start.8 = (f32[3,64,128]{2,1,0:T(8,128)S(1)}, f32[3,64,128]{2,1,0:T(8,128)S(1)}, u32[]{:S(2)}, u32[]{:S(2)}) collective-permute-start(f32[3,64,128]{2,1,0:T(8,128)S(1)} %convolution_bitcast_fusion.16), channel_id=1, source_target_pairs={{0,1},{1,2},{2,3},{3,4},{4,5},{5,6},{6,7},{7,8},{8,9},{9,10},{10,1... | collective-permute-start | bytes 294920 | tf_op jit(solution)/shard_map/ppermute | solution.py:28
  15.9 113.6 %collective-permute-start.9 = (f32[3,64,128]{2,1,0:T(8,128)S(1)}, f32[3,64,128]{2,1,0:T(8,128)}, u32[]{:S(2)}, u32[]{:S(2)}) collective-permute-start(f32[3,64,128]{2,1,0:T(8,128)S(1)} %convolution_bitcast_fusion.15), channel_id=1, source_target_pairs={{0,2},{1,3},{2,4},{3,5},{4,6},{5,7},{6,8},{7,9},{8,10},{9,11},{10,... | collective-permute-start | bytes 294920 | tf_op jit(solution)/shard_map/ppermute | solution.py:28
  21.4 109.4 %collective-permute-start.10 = (f32[3,64,128]{2,1,0:T(8,128)S(1)}, f32[3,64,128]{2,1,0:T(8,128)}, u32[]{:S(2)}, u32[]{:S(2)}) collective-permute-start(f32[3,64,128]{2,1,0:T(8,128)S(1)} %convolution_bitcast_fusion.14), channel_id=1, source_target_pairs={{0,3},{1,4},{2,5},{3,6},{4,7},{5,8},{6,9},{7,10},{8,11},{9,12},{10... | collective-permute-start | bytes 294920 | tf_op jit(solution)/shard_map/ppermute | solution.py:28
  26.6 76.7 %collective-permute-start.16 = (f32[3,64]{1,0:T(4,128)S(1)}, f32[3,64]{1,0:T(4,128)S(1)}, u32[]{:S(2)}, u32[]{:S(2)}) collective-permute-start(f32[3,64]{1,0:T(4,128)S(1)} %convolution_bitcast_fusion.25), channel_id=1, source_target_pairs={{0,1},{1,2},{2,3},{3,4},{4,5},{5,6},{6,7},{7,8},{8,9},{9,10},{10,1... | collective-permute-start | bytes 2312 | tf_op jit(solution)/shard_map/ppermute | solution.py:28
  28.9 77.2 %collective-permute-start.17 = (f32[3,64]{1,0:T(4,128)S(1)}, f32[3,64]{1,0:T(4,128)S(1)}, u32[]{:S(2)}, u32[]{:S(2)}) collective-permute-start(f32[3,64]{1,0:T(4,128)S(1)} %convolution_bitcast_fusion.24), channel_id=1, source_target_pairs={{0,2},{1,3},{2,4},{3,5},{4,6},{5,7},{6,8},{7,9},{8,10},{9,11},{10,... | collective-permute-start | bytes 2312 | tf_op jit(solution)/shard_map/ppermute | solution.py:28
  166.8 26.6 %collective-permute-start = (f32[64,384]{1,0:T(8,128)}, f32[64,384]{1,0:T(8,128)}, u32[]{:S(2)}, u32[]{:S(2)}) collective-permute-start(f32[64,384]{1,0:T(8,128)} %fusion.166), channel_id=1, source_target_pairs={{0,1},{1,2},{2,3},{3,4},{4,5},{5,6},{6,7},{7,8},{8,9},{9,10},{10,1... | collective-permute-start | bytes 294920 | tf_op jit(solution)/shard_map/ppermute | solution.py:28
  172.1 24.2 %collective-permute-start.1 = (f32[64,384]{1,0:T(8,128)}, f32[64,384]{1,0:T(8,128)}, u32[]{:S(2)}, u32[]{:S(2)}) collective-permute-start(f32[64,384]{1,0:T(8,128)} %fusion.161), channel_id=1, source_target_pairs={{0,2},{1,3},{2,4},{3,5},{4,6},{5,7},{6,8},{7,9},{8,10},{9,11},{10,... | collective-permute-start | bytes 294920 | tf_op jit(solution)/shard_map/ppermute | solution.py:28
  178.3 20.8 %collective-permute-start.2 = (f32[64,384]{1,0:T(8,128)}, f32[64,384]{1,0:T(8,128)}, u32[]{:S(2)}, u32[]{:S(2)}) collective-permute-start(f32[64,384]{1,0:T(8,128)} %fusion.155), channel_id=1, source_target_pairs={{0,3},{1,4},{2,5},{3,6},{4,7},{5,8},{6,9},{7,10},{8,11},{9,12},{10... | collective-permute-start | bytes 294920 | tf_op jit(solution)/shard_map/ppermute | solution.py:28
  183.4 18.6 %collective-permute-start.3 = (f32[64,384]{1,0:T(8,128)}, f32[64,384]{1,0:T(8,128)}, u32[]{:S(2)}, u32[]{:S(2)}) collective-permute-start(f32[64,384]{1,0:T(8,128)} %fusion.149), channel_id=1, source_target_pairs={{0,4},{1,5},{2,6},{3,7},{4,8},{5,9},{6,10},{7,11},{8,12},{9,13},{1... | collective-permute-start | bytes 294920 | tf_op jit(solution)/shard_map/ppermute | solution.py:28
  591.6 65.7 %collective-permute-start.25 = (f32[64,384]{0,1:T(8,128)}, f32[64,384]{0,1:T(8,128)}, u32[]{:S(2)}, u32[]{:S(2)}) collective-permute-start(f32[64,384]{0,1:T(8,128)} %get-tuple-element.867), channel_id=1, source_target_pairs={{2,0},{3,1},{4,2},{5,3},{6,4},{7,5},{8,6},{9,7},{10,8},{11,9},{12,... | collective-permute-start | bytes 294920 | tf_op jit(solution)/shard_map/ppermute | solution.py:28
  592.8 71.4 %collective-permute-start.26 = (f32[64,384]{0,1:T(8,128)}, f32[64,384]{0,1:T(8,128)}, u32[]{:S(2)}, u32[]{:S(2)}) collective-permute-start(f32[64,384]{0,1:T(8,128)} %get-tuple-element.866), channel_id=1, source_target_pairs={{3,0},{4,1},{5,2},{6,3},{7,4},{8,5},{9,6},{10,7},{11,8},{12,9},{13... | collective-permute-start | bytes 294920 | tf_op jit(solution)/shard_map/ppermute | solution.py:28
  594.1 75.0 %collective-permute-start.27 = (f32[64,384]{0,1:T(8,128)}, f32[64,384]{0,1:T(8,128)}, u32[]{:S(2)}, u32[]{:S(2)}) collective-permute-start(f32[64,384]{0,1:T(8,128)} %get-tuple-element.865), channel_id=1, source_target_pairs={{4,0},{5,1},{6,2},{7,3},{8,4},{9,5},{10,6},{11,7},{12,8},{13,9},{1... | collective-permute-start | bytes 294920 | tf_op jit(solution)/shard_map/ppermute | solution.py:28
  595.4 76.5 %collective-permute-start.28 = (f32[64,384]{0,1:T(8,128)}, f32[64,384]{0,1:T(8,128)}, u32[]{:S(2)}, u32[]{:S(2)}) collective-permute-start(f32[64,384]{0,1:T(8,128)} %get-tuple-element.864), channel_id=1, source_target_pairs={{0,1},{1,2},{2,3},{3,4},{4,5},{5,6},{6,7},{7,8},{8,9},{9,10},{10,1... | collective-permute-start | bytes 294920 | tf_op jit(solution)/shard_map/ppermute | solution.py:28
  651.6 27.7 %collective-permute-start.29 = (f32[64,384]{0,1:T(8,128)S(1)}, f32[64,384]{0,1:T(8,128)S(1)}, u32[]{:S(2)}, u32[]{:S(2)}) collective-permute-start(f32[64,384]{0,1:T(8,128)S(1)} %copy-done.48), channel_id=1, source_target_pairs={{0,2},{1,3},{2,4},{3,5},{4,6},{5,7},{6,8},{7,9},{8,10},{9,11},{10,... | collective-permute-start | bytes 294920 | tf_op jit(solution)/shard_map/ppermute | solution.py:28
  657.3 27.4 %collective-permute-start.30 = (f32[64,384]{0,1:T(8,128)S(1)}, f32[64,384]{0,1:T(8,128)S(1)}, u32[]{:S(2)}, u32[]{:S(2)}) collective-permute-start(f32[64,384]{0,1:T(8,128)S(1)} %copy-done.47), channel_id=1, source_target_pairs={{0,3},{1,4},{2,5},{3,6},{4,7},{5,8},{6,9},{7,10},{8,11},{9,12},{10... | collective-permute-start | bytes 294920 | tf_op jit(solution)/shard_map/ppermute | solution.py:28
  664.3 23.2 %collective-permute-start.31 = (f32[64,384]{0,1:T(8,128)S(1)}, f32[64,384]{0,1:T(8,128)S(1)}, u32[]{:S(2)}, u32[]{:S(2)}) collective-permute-start(f32[64,384]{0,1:T(8,128)S(1)} %copy-done.46), channel_id=1, source_target_pairs={{0,4},{1,5},{2,6},{3,7},{4,8},{5,9},{6,10},{7,11},{8,12},{9,13},{1... | collective-permute-start | bytes 294920 | tf_op jit(solution)/shard_map/ppermute | solution.py:28
  669.1 21.8 %collective-permute-start.24 = (f32[64,384]{0,1:T(8,128)S(1)}, f32[64,384]{0,1:T(8,128)S(1)}, u32[]{:S(2)}, u32[]{:S(2)}) collective-permute-start(f32[64,384]{0,1:T(8,128)S(1)} %copy-done.45), channel_id=1, source_target_pairs={{1,0},{2,1},{3,2},{4,3},{5,4},{6,5},{7,6},{8,7},{9,8},{10,9},{11,1... | collective-permute-start | bytes 294920 | tf_op jit(solution)/shard_map/ppermute | solution.py:28
  672.0 25.7 %collective-permute-start.39 = (f32[3,64,128]{2,1,0:T(8,128)}, f32[3,64,128]{2,1,0:T(8,128)}, u32[]{:S(2)}, u32[]{:S(2)}) collective-permute-start(f32[3,64,128]{2,1,0:T(8,128)} %get-tuple-element.855), channel_id=1, source_target_pairs={{0,4},{1,5},{2,6},{3,7},{4,8},{5,9},{6,10},{7,11},{8,12},{9,13},{1... | collective-permute-start | bytes 294920 | tf_op jit(solution)/shard_map/ppermute | solution.py:28
  679.3 21.3 %collective-permute-start.38 = (f32[3,64,128]{2,1,0:T(8,128)}, f32[3,64,128]{2,1,0:T(8,128)}, u32[]{:S(2)}, u32[]{:S(2)}) collective-permute-start(f32[3,64,128]{2,1,0:T(8,128)} %get-tuple-element.856), channel_id=1, source_target_pairs={{0,3},{1,4},{2,5},{3,6},{4,7},{5,8},{6,9},{7,10},{8,11},{9,12},{10... | collective-permute-start | bytes 294920 | tf_op jit(solution)/shard_map/ppermute | solution.py:28
  684.7 18.9 %collective-permute-start.37 = (f32[3,64,128]{2,1,0:T(8,128)}, f32[3,64,128]{2,1,0:T(8,128)}, u32[]{:S(2)}, u32[]{:S(2)}) collective-permute-start(f32[3,64,128]{2,1,0:T(8,128)} %get-tuple-element.857), channel_id=1, source_target_pairs={{0,2},{1,3},{2,4},{3,5},{4,6},{5,7},{6,8},{7,9},{8,10},{9,11},{10,... | collective-permute-start | bytes 294920 | tf_op jit(solution)/shard_map/ppermute | solution.py:28
  687.5 19.1 %collective-permute-start.36 = (f32[3,64,128]{2,1,0:T(8,128)}, f32[3,64,128]{2,1,0:T(8,128)}, u32[]{:S(2)}, u32[]{:S(2)}) collective-permute-start(f32[3,64,128]{2,1,0:T(8,128)} %get-tuple-element.858), channel_id=1, source_target_pairs={{0,1},{1,2},{2,3},{3,4},{4,5},{5,6},{6,7},{7,8},{8,9},{9,10},{10,1... | collective-permute-start | bytes 294920 | tf_op jit(solution)/shard_map/ppermute | solution.py:28
  691.0 17.1 %collective-permute-start.35 = (f32[3,64,128]{2,1,0:T(8,128)}, f32[3,64,128]{2,1,0:T(8,128)}, u32[]{:S(2)}, u32[]{:S(2)}) collective-permute-start(f32[3,64,128]{2,1,0:T(8,128)} %get-tuple-element.859), channel_id=1, source_target_pairs={{4,0},{5,1},{6,2},{7,3},{8,4},{9,5},{10,6},{11,7},{12,8},{13,9},{1... | collective-permute-start | bytes 294920 | tf_op jit(solution)/shard_map/ppermute | solution.py:28
  (141 other events, 3259.7 us)
Sparse Core Ops, SparseCore 0:
  13.8 131.7 all-reduce.19
  697.8 128.3 all-reduce.21
where the time goes:
time: 890 us; the launch traced here: 878 us
  matrix products  346 us (39%)
  waiting for transfers between devices  142 us (16%)
  starting transfers between devices  130 us (15%)
  local copies, waits for them, and re-layouts  88.3 us (10%)
  blocking collectives  79.8 us (9%)
  other arithmetic  62.5 us (7%)
  between operations  18.8 us (2%)
  loops' own time  11.3 us (1%)
    dot_general x106, matrix products, product(): jnp.dot(left, right, precision=PRECISION_MAX, preferred_element_type=jnp....  327 us
    ppermute x48, starting transfers between devices, passed_along(): return lax.ppermute(shard, axis, pairs)  130 us
    unnamed x4, waiting for transfers between devices  112 us
    psum x1, blocking collectives, body(): lax.psum((elem_total, elem_count, force_square), ('atoms', 'rep'))  40.1 us
    psum x1, blocking collectives, body(): lax.psum((weight_square, update_square), ('atoms', 'rep'))  39.8 us
    ppermute x48, waiting for transfers between devices, passed_along(): return lax.ppermute(shard, axis, pairs)  29.4 us
    unnamed x208, local copies, waits for them, and re-layouts  23.1 us
  transfers between devices with their start and end apart: 50, of which 12 were waited for; matrix products, arithmetic and copies ran while one was open for 12% of the time, Pallas kernels for 0%

commit v1 on v0

v1 whole, which is shorter than its diff:
```python
import functools

import jax
import jax.numpy as jnp
from jax import lax
from jax.experimental import pallas as pl
from jax.experimental.pallas import tpu as pltpu
from jax.sharding import PartitionSpec as P

F = 128
R = 20
HOPS = 4
ELEMS = 100
STEP = 10
GROUPS = 7

CUTOFF = 5.0
BETA_ONE = 0.9
BETA_TWO = 0.99
RATE = 0.3
DECAY = 0.01
EPSILON = 1e-06
PRECISION_MAX = lax.Precision.HIGHEST

BLOCK = 256
WINDOW = 128
SUB = 32
ROWS = 256
F32 = jnp.float32
BF16 = jnp.bfloat16

AT_W1, AT_W2, AT_WF, AT_WM, AT_U1, AT_U2 = 0, 128, 512, 572, 828, 1084
AT_B1, AT_B2, AT_BF, AT_C1, AT_C2, AT_READ, PARAM_ROWS = 1468, 1469, 1472, 1475, 1476, 1479, 1480


def product(left, right):
    return jnp.dot(left, right, precision=PRECISION_MAX, preferred_element_type=F32)


def mm(left, right, contract=(1, 0)):
    return lax.dot_general(
        left, right, (((contract[0],), (contract[1],)), ((), ())), preferred_element_type=F32
    )


def split(value):
    high = value.astype(BF16)
    return high, (value - high.astype(F32)).astype(BF16)


def dot3(left, right, contract=(1, 0)):
    return (
        mm(left[0], right[0], contract)
        + mm(left[1], right[0], contract)
        + mm(left[0], right[1], contract)
    )


def sigmoid(value):
    return 1.0 / (1.0 + jnp.exp(-value))


def column(ref, start, parts, j, count=F):
    if parts == 1:
        return ref[start : start + count, :]
    return ref[pl.ds(start + j, count, stride=parts), :]


def add_column(ref, start, parts, j, value, count=F):
    if parts == 1:
        ref[start : start + count, :] += value
    else:
        ref[pl.ds(start + j, count, stride=parts), :] += value


def rows_of(start, count, unit):
    return pl.ds(pl.multiple_of(start, unit), count)


def layer_kernel(
    src_s,
    dst_s,
    count_s,
    crystal_s,
    dst_v,
    shift_v,
    lat,
    par,
    s_own,
    v_own,
    p_own,
    s_halo,
    v_halo,
    p_halo,
    cot_s,
    cot_v,
    goal,
    s_two,
    v_two,
    gs_own,
    gv_own,
    gs_halo,
    gv_halo,
    gp,
    gpar,
    tab,
    rows,
    acc,
    cells,
    dtab,
    lrow,
    drow,
    misc,
    sums,
    gd,
    gbuf,
    fbuf,
    mbuf,
    ltbuf,
    tbuf,
    wcat,
    wq,
    gwf,
    gpd,
):
    atoms = s_own.shape[0]
    halo = s_halo.shape[0]
    edges = shift_v.shape[1]
    blocks = edges // BLOCK

    wcat[...] = jnp.zeros_like(wcat)
    wq[...] = jnp.zeros_like(wq)
    gwf[...] = jnp.zeros_like(gwf)
    gpd[...] = jnp.zeros_like(gpd)
    gpar[...] = jnp.zeros_like(gpar)
    sums[...] = jnp.zeros_like(sums)
    for j in range(3):
        wide = jnp.concatenate(
            [
                column(par, AT_WF, 3, j, R),
                par[AT_BF + j : AT_BF + j + 1, :],
                jnp.zeros((3, F), F32),
            ],
            axis=0,
        )
        high = wide.astype(BF16).astype(F32)
        low = wide - high
        pieces = jnp.concatenate([high, high, low, jnp.zeros((56, F), F32)], axis=0)
        wcat[:, j * F : (j + 1) * F] = pieces.astype(BF16)
        pieces = jnp.concatenate([high, low, jnp.zeros((80, F), F32)], axis=0)
        wq[j * F : (j + 1) * F, :] = jnp.transpose(pieces).astype(BF16)

    @pl.loop(0, atoms // 8)
    def _(step):
        for j in range(8):
            a = step * 8 + j
            cells[pl.ds(a, 1), 0:9] = lat[pl.ds(crystal_s[a], 1), :]

    across = jnp.transpose(cells[...])
    blank = jnp.zeros((5, atoms), F32)
    part = jnp.concatenate(
        [p_own[...], blank, across[0:3], blank, across[3:6], blank, across[6:9], blank], axis=0
    )
    high = part.astype(BF16).astype(F32)
    middle = (part - high).astype(BF16).astype(F32)
    low = part - high - middle
    dtab[...] = jnp.concatenate([high, middle, low], axis=0).astype(BF16)

    for s_ref, v_ref, p_ref, base, count in (
        (s_own, v_own, p_own, 0, atoms),
        (s_halo, v_halo, p_halo, atoms, halo),
    ):
        place = jnp.concatenate([p_ref[...], jnp.zeros((F - 3, count), F32)], axis=0)
        tab[pl.ds(base * 8 + 6, count, stride=8), :] = jnp.transpose(place)
        tab[pl.ds(base * 8 + 7, count, stride=8), :] = jnp.zeros((count, F), F32)
        for c in range(3):
            tab[pl.ds(base * 8 + 3 + c, count, stride=8), :] = v_ref[c]

        @pl.loop(0, count // ROWS)
        def _(step):
            first = step * ROWS
            s_pair = split(s_ref[rows_of(first, ROWS, ROWS), :])
            act = dot3(s_pair, split(column(par, AT_W1, 1, 0))) + par[AT_B1 : AT_B1 + 1, :]
            hidden = split(act * sigmoid(act))
            for j in range(3):
                x = dot3(hidden, split(column(par, AT_W2, 3, j))) + par[AT_B2 + j : AT_B2 + j + 1, :]
                tab[pl.ds((base + first) * 8 + j, ROWS, stride=8), :] = x

    @pl.loop(0, edges // 32)
    def _(step):
        for j in range(32):
            e = step * 32 + j
            rows[rows_of(e * 8, 8, 8), :] = tab[rows_of(src_s[e] * 8, 8, 8), :]

    lanes = lax.broadcasted_iota(jnp.int32, (1, BLOCK), 1)
    slots = lax.broadcasted_iota(jnp.int32, (WINDOW, BLOCK), 0)
    eight = lax.broadcasted_iota(jnp.int32, (8, 1), 0)
    order = lax.broadcasted_iota(jnp.int32, (24, 1), 0)
    wide_lane = lax.broadcasted_iota(jnp.int32, (1, F), 1)

    def destinations(i):
        return jnp.concatenate(
            [dst_v[pl.ds(i * (BLOCK // F) + k, 1), :] for k in range(BLOCK // F)], axis=1
        )

    def window_range(i):
        return dst_s[i * BLOCK] // WINDOW, dst_s[i * BLOCK + BLOCK - 1] // WINDOW

    def hot(dst, w):
        return jnp.where(dst - w * WINDOW == slots, 1.0, 0.0).astype(BF16)

    def over_windows(first, last, body, start):
        return lax.fori_loop(first + 1, last + 1, body, body(first, start))

    def lane_pieces(pieces, extra):
        full = jnp.concatenate(
            [pieces, pieces[0:24], extra, jnp.zeros((F - 80, BLOCK), F32)], axis=0
        )
        return jnp.transpose(full)

    def comp(i, k, sub):
        return pl.ds(i * (BLOCK * 8) + sub * (SUB * 8) + k, SUB, stride=8)

    @pl.loop(0, blocks)
    def _(i):
        here = rows_of(i * BLOCK, BLOCK, BLOCK)
        first, last = window_range(i)
        dst = destinations(i)
        place = jnp.transpose(rows[pl.ds(i * (BLOCK * 8) + 6, BLOCK, stride=8), :])[0:8]
        ends = over_windows(
            first,
            last,
            lambda w, got: got + mm(dtab[:, rows_of(w * WINDOW, WINDOW, WINDOW)], hot(dst, w)),
            jnp.zeros((96, BLOCK), F32),
        )
        ends = ends[0:32] + ends[32:64] + ends[64:96]
        shift = shift_v[:, here].astype(F32)
        rel = (
            place
            + (shift[0:1] * ends[8:16] + shift[1:2] * ends[16:24] + shift[2:3] * ends[24:32])
            - ends[0:8]
        )
        square = jnp.sum(rel * rel, axis=0, keepdims=True)
        dist = jnp.sqrt(jnp.maximum(square, 0.25))
        inv = 1.0 / dist
        unit = rel * inv
        free = jnp.where(square > 0.25, 1.0, 0.0)
        angle = dist * (jnp.pi / CUTOFF)
        phase = (eight + 1).astype(F32) * angle
        sin_a, cos_a = jnp.sin(phase), jnp.cos(phase)
        sin_8, cos_8 = sin_a[7:8], cos_a[7:8]
        sin_b = sin_a * cos_8 + cos_a * sin_8
        cos_b = cos_a * cos_8 - sin_a * sin_8
        sin_c = sin_b * cos_8 + cos_b * sin_8
        cos_c = cos_b * cos_8 - sin_b * sin_8
        sines = jnp.concatenate([sin_a, sin_b, sin_c], axis=0)
        cosines = jnp.concatenate([cos_a, cos_b, cos_c], axis=0)
        radial = sines * inv
        slope = ((order + 1).astype(F32) * (jnp.pi / CUTOFF) * cosines - radial) * inv
        radial = jnp.where(order < R, radial, jnp.where(order == R, 1.0, 0.0))
        slope = jnp.where(order < R, slope, 0.0)
        inside = (dist < CUTOFF) & (i * BLOCK + lanes < count_s[0])
        envelope = jnp.where(inside, 0.5 * (cos_a[0:1] + 1.0), 0.0)
        fall = jnp.where(inside, (-0.5 * jnp.pi / CUTOFF) * sin_a[0:1], 0.0)
        scaled = envelope * radial
        high = scaled.astype(BF16).astype(F32)
        pieces = jnp.concatenate([high, scaled - high], axis=0)
        extra = jnp.where(
            eight < 3,
            unit,
            jnp.where(
                eight == 3,
                dst.astype(F32),
                jnp.where(eight == 4, inv, jnp.where(eight == 5, free, 0.0)),
            ),
        )
        lrow[:, here] = pieces.astype(BF16)
        drow[:, here] = fall * radial + envelope * slope
        misc[:, here] = extra
        ltbuf[...] = lane_pieces(pieces, extra)
        fbuf[...] = mm(ltbuf[...].astype(BF16), wcat[...])
        for sub in range(BLOCK // SUB):
            at = slice(sub * SUB, (sub + 1) * SUB)
            m1, m2, m3 = [
                rows[comp(i, j, sub), :] * fbuf[at, j * F : (j + 1) * F] for j in range(3)
            ]
            out = [m1]
            for c in range(3):
                out.append(m2 * ltbuf[at, 72 + c : 73 + c] + m3 * rows[comp(i, 3 + c, sub), :])
            for k in range(4):
                high, low = split(out[k])
                mbuf[at, k * F : (k + 1) * F] = high
                mbuf[at, (4 + k) * F : (5 + k) * F] = low

        def collect(w, ignored):
            pick = hot(dst, w)
            sums[rows_of(w * WINDOW, WINDOW, WINDOW), :] += mm(pick, mbuf[:, : 4 * F]) + mm(
                pick, mbuf[:, 4 * F :]
            )
            return ignored

        over_windows(first, last, collect, 0)

    @pl.loop(0, atoms // ROWS)
    def _(step):
        at = rows_of(step * ROWS, ROWS, ROWS)
        s_one = s_own[at, :] + sums[at, 0:F]
        v_one = [v_own[c, at, :] + sums[at, (c + 1) * F : (c + 2) * F] for c in range(3)]
        wm = [split(column(par, AT_WM, 2, j)) for j in range(2)]
        u1 = [split(par[AT_U1 + j * F : AT_U1 + (j + 1) * F, :]) for j in range(2)]
        u2 = [split(column(par, AT_U2, 3, j)) for j in range(3)]
        v_pair = [split(v) for v in v_one]
        v_lin = [dot3(v, wm[0]) for v in v_pair]
        w_lin = [dot3(v, wm[1]) for v in v_pair]
        size = jnp.sqrt(v_lin[0] * v_lin[0] + v_lin[1] * v_lin[1] + v_lin[2] * v_lin[2] + 1.0)
        s_pair, size_pair = split(s_one), split(size)
        act = dot3(s_pair, u1[0]) + dot3(size_pair, u1[1]) + par[AT_C1 : AT_C1 + 1, :]
        gate = sigmoid(act)
        hidden = split(act * gate)
        a1, a2, a3 = [dot3(hidden, u2[j]) + par[AT_C2 + j : AT_C2 + j + 1, :] for j in range(3)]
        inner = v_lin[0] * w_lin[0] + v_lin[1] * w_lin[1] + v_lin[2] * w_lin[2]
        s_out = s_one + a3 + a2 * inner
        s_two[at, :] = s_out
        read = par[AT_READ : AT_READ + 1, :]
        out_pair = split(s_out)
        energy = dot3(split(jnp.broadcast_to(read, (8, F))), out_pair, (1, 1))
        error = energy - goal[:, at]
        error_col = jnp.transpose(error)[:, 0:1]
        gpar[AT_READ : AT_READ + 1, :] += dot3(split(error), out_pair)[0:1]
        gs = cot_s[at, :] + error_col * read
        gv = []
        for c in range(3):
            v_two[c, at, :] = v_one[c] + a1 * w_lin[c]
            gv.append(cot_v[c, at, :])
        ga = [gv[0] * w_lin[0] + gv[1] * w_lin[1] + gv[2] * w_lin[2], gs * inner, gs]
        g_inner = gs * a2
        ga_pair = [split(g) for g in ga]
        for j in range(3):
            add_column(gpar, AT_U2, 3, j, dot3(hidden, ga_pair[j], (0, 0)))
            gpar[AT_C2 + j : AT_C2 + j + 1, :] += jnp.sum(ga[j], axis=0, keepdims=True)
        g_hidden = (
            dot3(ga_pair[0], u2[0], (1, 1))
            + dot3(ga_pair[1], u2[1], (1, 1))
            + dot3(ga_pair[2], u2[2], (1, 1))
        )
        g_act = g_hidden * (gate * (1.0 + act * (1.0 - gate)))
        g_act_pair = split(g_act)
        add_column(gpar, AT_U1, 1, 0, dot3(s_pair, g_act_pair, (0, 0)))
        add_column(gpar, AT_U1 + F, 1, 0, dot3(size_pair, g_act_pair, (0, 0)))
        gpar[AT_C1 : AT_C1 + 1, :] += jnp.sum(g_act, axis=0, keepdims=True)
        g_s_one = gs + dot3(g_act_pair, u1[0], (1, 1))
        g_size = dot3(g_act_pair, u1[1], (1, 1)) / size
        gs_own[at, :] = g_s_one
        down = [g_s_one]
        for c in range(3):
            g_w = split(a1 * gv[c] + g_inner * v_lin[c])
            g_v = split(g_inner * w_lin[c] + g_size * v_lin[c])
            add_column(gpar, AT_WM, 2, 0, dot3(v_pair[c], g_v, (0, 0)))
            add_column(gpar, AT_WM, 2, 1, dot3(v_pair[c], g_w, (0, 0)))
            g_v_one = gv[c] + dot3(g_v, wm[0], (1, 1)) + dot3(g_w, wm[1], (1, 1))
            gv_own[c, at, :] = g_v_one
            down.append(g_v_one)
        for k in range(4):
            high, low = split(down[k])
            for part in range(ROWS // WINDOW):
                to = (step * (ROWS // WINDOW) + part) * (2 * WINDOW)
                of = slice(part * WINDOW, (part + 1) * WINDOW)
                gd[rows_of(to, WINDOW, WINDOW), k * F : (k + 1) * F] = high[of]
                gd[rows_of(to + WINDOW, WINDOW, WINDOW), k * F : (k + 1) * F] = low[of]

    twice = (lax.broadcasted_iota(jnp.int32, (1, 2 * WINDOW), 1) % WINDOW).astype(F32)

    @pl.loop(0, blocks)
    def _(i):
        here = rows_of(i * BLOCK, BLOCK, BLOCK)
        first, last = window_range(i)
        dst = destinations(i)
        extra = misc[:, here]
        ltbuf[...] = lane_pieces(lrow[:, here].astype(F32), extra)
        fbuf[...] = mm(ltbuf[...].astype(BF16), wcat[...])
        dst_col = ltbuf[:, 75:76]

        def fetch(w):
            near = dst_col - (w * WINDOW).astype(F32)
            return mm(
                jnp.where(near == twice, 1.0, 0.0).astype(BF16),
                gd[rows_of(w * 2 * WINDOW, 2 * WINDOW, 2 * WINDOW), :],
            )

        gbuf[...] = fetch(first)

        @pl.loop(first + 1, last + 1)
        def _(w):
            gbuf[...] += fetch(w)

        for sub in range(BLOCK // SUB):
            at = slice(sub * SUB, (sub + 1) * SUB)
            g_s = gbuf[at, 0:F]
            g_v = [gbuf[at, (c + 1) * F : (c + 2) * F] for c in range(3)]
            x = [rows[comp(i, j, sub), :] for j in range(3)]
            v = [rows[comp(i, 3 + c, sub), :] for c in range(3)]
            f = [fbuf[at, j * F : (j + 1) * F] for j in range(3)]
            u = [ltbuf[at, 72 + c : 73 + c] for c in range(3)]
            g_m = [
                g_s,
                g_v[0] * u[0] + g_v[1] * u[1] + g_v[2] * u[2],
                g_v[0] * v[0] + g_v[1] * v[1] + g_v[2] * v[2],
            ]
            m2 = x[1] * f[1]
            m3 = x[2] * f[2]
            turn = jnp.zeros((SUB, F), F32)
            for c in range(3):
                total = jnp.sum(g_v[c] * m2, axis=1, keepdims=True)
                turn = jnp.where(wide_lane == 48 + c, total, turn)
                rows[comp(i, 3 + c, sub), :] = g_v[c] * m3
            tbuf[at, :] = turn
            for j in range(3):
                high, low = split(g_m[j] * x[j])
                mbuf[at, j * F : (j + 1) * F] = high
                mbuf[at, (3 + j) * F : (4 + j) * F] = low
                rows[comp(i, j, sub), :] = g_m[j] * f[j]
        h_high, h_low = mbuf[:, : 3 * F], mbuf[:, 3 * F : 6 * F]
        back = jnp.transpose(mm(h_high, wq[...]) + mm(h_low, wq[...]) + tbuf[...])
        pieces = lrow[:, here]
        gwf[...] += mm(pieces, h_high) + mm(pieces, h_low)
        g_row = back[0:24] + back[24:48]
        g_unit = back[48:56]
        unit = jnp.where(eight < 3, extra, 0.0)
        inv, free = extra[4:5], extra[5:6]
        g_dist = jnp.sum(g_row * drow[:, here], axis=0, keepdims=True)
        along = jnp.sum(g_unit * unit, axis=0, keepdims=True)
        g_rel = g_unit * inv + (g_dist - along * inv) * free * unit
        rows[pl.ds(i * (BLOCK * 8) + 6, BLOCK, stride=8), :] = jnp.transpose(
            jnp.concatenate([g_rel, jnp.zeros((F - 8, BLOCK), F32)], axis=0)
        )
        high = g_rel.astype(BF16).astype(F32)
        middle = (g_rel - high).astype(BF16).astype(F32)
        g_pieces = jnp.concatenate([high, middle, g_rel - high - middle, jnp.zeros_like(g_rel)], axis=0)
        g_pieces = g_pieces.astype(BF16)

        def collect(w, ignored):
            got = mm(g_pieces, hot(dst, w), (1, 1))
            gpd[:, rows_of(w * WINDOW, WINDOW, WINDOW)] += got[0:8] + got[8:16] + got[16:24]
            return ignored

        over_windows(first, last, collect, 0)

    for j in range(3):
        total = gwf[0:24, j * F : (j + 1) * F] + gwf[24:48, j * F : (j + 1) * F]
        add_column(gpar, AT_WF, 3, j, total[0:R], R)
        gpar[AT_BF + j : AT_BF + j + 1, :] = total[R : R + 1]

    tab[...] = jnp.zeros_like(tab)
    acc[...] = jnp.zeros_like(acc)
    half = edges // 2

    @pl.loop(0, half // 8)
    def _(step):
        for j in range(8):
            for start, total in ((0, tab), (half, acc)):
                e = start + step * 8 + j
                to = rows_of(src_s[e] * 8, 8, 8)
                total[to, :] += rows[rows_of(e * 8, 8, 8), :]

    for s_ref, gs_ref, gv_ref, base, count in (
        (s_own, gs_own, gv_own, 0, atoms),
        (s_halo, gs_halo, gv_halo, atoms, halo),
    ):
        own = base == 0
        for k in range(0, count, ROWS):
            at = pl.ds((base + k) * 8 + 6, ROWS, stride=8)
            place = jnp.transpose(tab[at, :] + acc[at, :])[0:8]
            if own:
                place = place - gpd[:, k : k + ROWS]
            gp[:, base + k : base + k + ROWS] = place

        @pl.loop(0, count // ROWS)
        def _(step):
            first = step * ROWS
            to = rows_of(first, ROWS, ROWS)

            def gathered(k):
                at = pl.ds((base + first) * 8 + k, ROWS, stride=8)
                return tab[at, :] + acc[at, :]

            for c in range(3):
                if own:
                    gv_ref[c, to, :] += gathered(3 + c)
                else:
                    gv_ref[c, to, :] = gathered(3 + c)
            w1 = split(column(par, AT_W1, 1, 0))
            s_pair = split(s_ref[to, :])
            act = dot3(s_pair, w1) + par[AT_B1 : AT_B1 + 1, :]
            gate = sigmoid(act)
            hidden = split(act * gate)
            g_hidden = jnp.zeros((ROWS, F), F32)
            for j in range(3):
                g_x = gathered(j)
                g_pair = split(g_x)
                add_column(gpar, AT_W2, 3, j, dot3(hidden, g_pair, (0, 0)))
                gpar[AT_B2 + j : AT_B2 + j + 1, :] += jnp.sum(g_x, axis=0, keepdims=True)
                g_hidden = g_hidden + dot3(g_pair, split(column(par, AT_W2, 3, j)), (1, 1))
            g_act = g_hidden * (gate * (1.0 + act * (1.0 - gate)))
            g_act_pair = split(g_act)
            add_column(gpar, AT_W1, 1, 0, dot3(s_pair, g_act_pair, (0, 0)))
            gpar[AT_B1 : AT_B1 + 1, :] += jnp.sum(g_act, axis=0, keepdims=True)
            g_s = dot3(g_act_pair, w1, (1, 1))
            if own:
                gs_ref[to, :] += g_s
            else:
                gs_ref[to, :] = g_s


def layer(atoms, halo, edges, smem, vmem):
    shape = jax.ShapeDtypeStruct
    total = atoms + halo
    in_vmem = pl.BlockSpec(memory_space=pltpu.VMEM)
    in_smem = pl.BlockSpec(memory_space=pltpu.SMEM)
    outs = (
        shape((atoms, F), F32),
        shape((3, atoms, F), F32),
        shape((atoms, F), F32),
        shape((3, atoms, F), F32),
        shape((halo, F), F32),
        shape((3, halo, F), F32),
        shape((8, total), F32),
        shape((PARAM_ROWS, F), F32),
    )
    scratch = [
        pltpu.VMEM((total * 8, F), F32),
        pltpu.VMEM((edges * 8, F), F32),
        pltpu.VMEM((total * 8, F), F32),
        pltpu.VMEM((atoms, F), F32),
        pltpu.VMEM((96, atoms), BF16),
        pltpu.VMEM((48, edges), BF16),
        pltpu.VMEM((24, edges), F32),
        pltpu.VMEM((8, edges), F32),
        pltpu.VMEM((atoms, 4 * F), F32),
        pltpu.VMEM((2 * atoms, 4 * F), BF16),
        pltpu.VMEM((BLOCK, 4 * F), F32),
        pltpu.VMEM((BLOCK, 3 * F), F32),
        pltpu.VMEM((BLOCK, 8 * F), BF16),
        pltpu.VMEM((BLOCK, F), F32),
        pltpu.VMEM((BLOCK, F), F32),
        pltpu.VMEM((F, 3 * F), BF16),
        pltpu.VMEM((3 * F, F), BF16),
        pltpu.VMEM((48, 3 * F), F32),
        pltpu.VMEM((8, atoms), F32),
    ]
    return pl.pallas_call(
        layer_kernel,
        out_shape=outs,
        in_specs=[in_smem] * smem + [in_vmem] * vmem,
        out_specs=(in_vmem,) * len(outs),
        scratch_shapes=scratch,
        compiler_params=pltpu.CompilerParams(vmem_limit_bytes=62 * 1024 * 1024),
        name="layer",
    )


def layout():
    shapes = [(F, F), (F, 3 * F), (R, 3 * F), (F, 2 * F), (2 * F, F), (F, 3 * F)]
    lengths = [F, 3 * F, 3 * F, F, 3 * F, F]
    return (shapes, lengths)


def group_ids(index):
    shapes, lengths = layout()
    labels = jnp.zeros(index.shape, jnp.int32)
    start = 0
    for shape in shapes:
        start += shape[0] * shape[1]
        labels = labels + (index >= start).astype(jnp.int32)
    return labels


def passed_along(shard, axis, by):
    devices = lax.axis_size(axis)
    pairs = [(i, i + by) for i in range(devices) if 0 <= i + by < devices]
    return lax.ppermute(shard, axis, pairs)


def body(
    scalars_in,
    vectors_in,
    positions,
    cotan_scalar,
    cotan_vector,
    target_energy,
    forces,
    elements,
    crystal,
    lattice,
    edge_src,
    edge_dst,
    edge_shift,
    edge_count,
    send_rows,
    params,
    first_moment,
    second_moment,
):
    both = ("atoms", "rep")
    atoms_dev = scalars_in.shape[0]
    edges_dev = edge_src.shape[0]
    capacity = send_rows.shape[2]
    hop_offsets = [k + 1 for k in range(HOPS)] + [-(k + 1) for k in range(HOPS)]
    all_params = lax.all_gather(params, both, axis=0, tiled=True)
    onehot = (elements[:, None] == jnp.arange(ELEMS, dtype=jnp.int32)[None, :]).astype(F32)
    elem_total = product(target_energy[None, :], onehot)[0]
    elem_count = jnp.sum(onehot, axis=0)
    force_square = jnp.sum(forces * forces)
    elem_total, elem_count, force_square = lax.psum((elem_total, elem_count, force_square), both)
    element_mean = elem_total / jnp.maximum(elem_count, 1.0)
    total_atoms = atoms_dev * lax.axis_size(both)
    force_scale = jnp.sqrt(force_square / (3.0 * total_atoms) + 1e-06)
    goal = (target_energy - product(onehot, element_mean[:, None])[:, 0]) / force_scale

    picker = (
        send_rows[0].reshape(-1)[:, None] == jnp.arange(atoms_dev, dtype=jnp.int32)[None, :]
    ).astype(F32)
    joined = jnp.concatenate(
        [scalars_in, vectors_in[0], vectors_in[1], vectors_in[2], jnp.transpose(positions)], axis=1
    )
    picked = product(picker, joined).reshape(2 * HOPS, capacity, 4 * F + 3)
    received = jnp.concatenate(
        [passed_along(picked[k], both, hop_offsets[k]) for k in range(2 * HOPS)], axis=0
    )
    halo_rows = 2 * HOPS * capacity
    s_halo = received[:, :F]
    v_halo = jnp.stack([received[:, (c + 1) * F : (c + 2) * F] for c in range(3)])
    p_halo = jnp.transpose(received[:, 4 * F :])

    run = layer(atoms_dev, halo_rows, edges_dev, 4, 13)
    s_two, v_two, gs_own, gv_own, gs_halo, gv_halo, gp, gpar = run(
        edge_src,
        edge_dst,
        edge_count,
        crystal,
        edge_dst.reshape(-1, F),
        edge_shift,
        lattice,
        all_params.reshape(PARAM_ROWS, F),
        scalars_in,
        vectors_in,
        positions,
        s_halo,
        v_halo,
        p_halo,
        cotan_scalar,
        cotan_vector,
        goal[None, :],
    )
    back = jnp.concatenate(
        [gs_halo, gv_halo[0], gv_halo[1], gv_halo[2], jnp.transpose(gp[:3, atoms_dev:])], axis=1
    ).reshape(2 * HOPS, capacity, 4 * F + 3)
    returned = jnp.concatenate(
        [passed_along(back[k], both, -hop_offsets[k]) for k in range(2 * HOPS)], axis=0
    )
    added = product(jnp.transpose(picker), returned)
    grad_scalars = gs_own + added[:, :F]
    grad_vectors = gv_own + jnp.stack([added[:, (c + 1) * F : (c + 2) * F] for c in range(3)])
    grad_positions = gp[:3, :atoms_dev] + jnp.transpose(added[:, 4 * F :])

    grad_shard = lax.psum_scatter(gpar.reshape(-1), both, scatter_dimension=0, tiled=True)
    shard_len = params.shape[0]
    moment_one = BETA_ONE * first_moment + (1.0 - BETA_ONE) * grad_shard
    moment_two = BETA_TWO * second_moment + (1.0 - BETA_TWO) * grad_shard * grad_shard
    direction = (
        moment_one
        / (1.0 - BETA_ONE**STEP)
        / (jnp.sqrt(moment_two / (1.0 - BETA_TWO**STEP)) + EPSILON)
        + DECAY * params
    )
    first_index = lax.axis_index(both) * shard_len
    labels = group_ids(first_index + jnp.arange(shard_len, dtype=jnp.int32))
    member = (labels[None, :] == jnp.arange(GROUPS, dtype=jnp.int32)[:, None]).astype(F32)
    weight_square = product(member, (params * params)[:, None])[:, 0]
    update_square = product(member, (direction * direction)[:, None])[:, 0]
    weight_square, update_square = lax.psum((weight_square, update_square), both)
    weight_norms = jnp.sqrt(weight_square)
    update_norms = jnp.sqrt(update_square)
    trust_ratio = weight_norms / update_norms
    params_new = params - RATE * product(trust_ratio[None, :], member)[0] * direction
    return (
        s_two,
        v_two,
        grad_scalars,
        grad_vectors,
        grad_positions,
        element_mean,
        force_scale,
        grad_shard,
        moment_one,
        moment_two,
        params_new,
        params_new.astype(BF16),
        weight_norms,
        update_norms,
    )


def solution(mesh):
    joint = ("atoms", "rep")
    in_specs = (
        P(joint, None),
        P(None, joint, None),
        P(None, joint),
        P(joint, None),
        P(None, joint, None),
        P(joint),
        P(None, joint),
        P(joint),
        P(joint),
        P(),
        P(joint),
        P(joint),
        P(None, joint),
        P(joint),
        P(joint, None, None),
        P(joint),
        P(joint),
        P(joint),
    )
    out_specs = (
        P(joint, None),
        P(None, joint, None),
        P(joint, None),
        P(None, joint, None),
        P(None, joint),
        P(),
        P(),
        P(joint),
        P(joint),
        P(joint),
        P(joint),
        P(joint),
        P(),
        P(),
    )
    return jax.shard_map(body, mesh=mesh, in_specs=in_specs, out_specs=out_specs, check_vma=False)
```

time: 890 us -> 487 us (0.55); the launches traced: 878 us -> 486 us
  matrix products: 346 us -> 3.98 us
  Pallas kernels: 0 us -> 113 us
  starting transfers between devices: 130 us -> 43.6 us
  local copies, waits for them, and re-layouts: 88.3 us -> 18 us
  waiting for transfers between devices: 142 us -> 200 us
  other arithmetic: 62.5 us -> 5.83 us
  loops' own time: 11.3 us -> 0 us
    dot_general x122 -> x7, matrix products: 346 us -> 3.98 us  [product(): jnp.dot(left, right, precision=PRECISION_MAX, preferred_element_type=F32)]
    pallas_call x0 -> x1, Pallas kernels: none -> 113 us  [body(): run(edge_src, edge_dst, edge_count, crystal, edge_dst.reshape(-1, F), edg...]
    ppermute x48 -> x16, starting transfers between devices: 130 us -> 43.5 us  [passed_along(): return lax.ppermute(shard, axis, pairs)]
    unnamed x4, waiting for transfers between devices: 112 us -> 181 us
    reduce_sum x14 -> x0, other arithmetic: 22 us -> none  [the longest x4 15 us: messages(): filter_rows = (product(radial, w_filter) + b_filter) * envelope[:, None]]
    slice x23 -> x4, local copies, waits for them, and re-layouts: 15.7 us -> 2.19 us  [the longest x1 1.19 us: body(): picked[k]]
    dynamic_slice x20 -> x0, local copies, waits for them, and re-layouts: 12.4 us -> none  [the longest x12 6.26 us: body(): offset_blocks = lax.map(offset_block, (shift_blocks, dst_blocks))]
    unnamed x208 -> x56, local copies, waits for them, and re-layouts: 23.1 us -> 10.7 us
  transfers between devices with their start and end apart: 50 -> 18, of which waited for: 12 -> 6; matrix products, arithmetic and copies ran while one was open for 12% -> 2% of each run, Pallas kernels for 0% -> 0%
where the time goes in v1:
time: 487 us; the launch traced here: 486 us
  waiting for transfers between devices  200 us (41%)
  Pallas kernels  113 us (23%)
  blocking collectives  84.7 us (17%)
  starting transfers between devices  43.6 us (9%)
  local copies, waits for them, and re-layouts  18 us (4%)
  between operations  17.2 us (4%)
  other arithmetic  5.83 us (1%)
    unnamed x4, waiting for transfers between devices  181 us
    pallas_call x1, Pallas kernels, body(): run(edge_src, edge_dst, edge_count, crystal, edge_dst.reshape(-1, F), edg...  113 us
    psum x1, blocking collectives, body(): lax.psum((elem_total, elem_count, force_square), both)  45 us
    ppermute x16, starting transfers between devices, passed_along(): return lax.ppermute(shard, axis, pairs)  43.5 us
    psum x1, blocking collectives, body(): lax.psum((weight_square, update_square), both)  39.8 us
    ppermute x16, waiting for transfers between devices, passed_along(): return lax.ppermute(shard, axis, pairs)  18.9 us
    unnamed x56, local copies, waits for them, and re-layouts  10.7 us
  transfers between devices with their start and end apart: 18, of which 6 were waited for; matrix products, arithmetic and copies ran while one was open for 2% of the time, Pallas kernels for 0%

profile of v1, /device:TPU:0, one launch (start us, length us, event | category | flops | bytes accessed | tf_op | source)
XLA Modules:
  0.0 486.4 jit_solution(15512895368267926480)
XLA Ops:
  12.1 1.4 fusion.1
  14.7 2.5 collective-permute-start
  17.2 4.4 collective-permute-start.1
  21.6 4.3 collective-permute-start.2
  25.9 3.4 collective-permute-start.3
  29.4 1.3 collective-permute-start.4
  33.1 45.0 %all-reduce.3 = (f32[100]{0:T(128)S(1)}, f32[100]{0:T(128)S(1)}, f32[]{:T(128)}) all-reduce(f32[100]{0:T(128)S(1)} %convolution_bitcast_fusion, f32[100]{0:T(128)S(1)} %convert_reduce_fusion, f32[]{:T(128)} %multiply_reduce_fusion), channel_id=1, replica_groups=mesh['atoms'=16,'rep'=2] {'atoms','rep'}, use_global_device_ids=true, to_apply=%region_0.0 | all-reduce | flops 201 | bytes 1608 | tf_op jit(solution)/shard_map/psum | solution.py:613
  81.8 1.3 collective-permute-start.6
  83.1 1.5 collective-permute-start.7
  85.2 7.0 %collective-permute-done.5 = f32[64,515]{0,1:T(8,128)S(1)} collective-permute-done((f32[64,515]{0,1:T(8,128)S(1)}, f32[64,515]{0,1:T(8,128)S(1)}, u32[]{:S(2)}, u32[]{:S(2)}) %collective-permute-start.5) | collective-permute-done | bytes 131872 | tf_op jit(solution)/shard_map/ppermute | solution.py:580
  93.3 4.8 collective-permute-done.7
  98.2 2.1 concatenate.13
  103.0 75.0 %all-reduce.7.cloned.1.call-done = f32[189440]{0:T(1024)} async-done(((f32[189440]{0:T(1024)}), f32[189440]{0:T(1024)}) %all-reduce.7.cloned.1.call-update) | async-done | bytes 757776
  178.0 113.2 %layer.1 = (f32[512,128]{1,0:T(8,128)}, f32[3,512,128]{2,1,0:T(8,128)}, f32[512,128]{1,0:T(8,128)}, f32[3,512,128]{2,1,0:T(8,128)}, f32[512,128]{1,0:T(8,128)}, ...) custom-call(s32[8192]{0:T(1024)} %src_s.1, s32[8192]{0:T(1024)} %dst_s.1, s32[1]{0:T(128)S(6)} %copy.81.count_s, ...), custom_call_target="tpu_custom_call" | custom-call | tf_op jit(solution)/shard_map/layer/pallas_call | solution.py:635
  295.4 1.3 collective-permute-start.8
  300.7 3.0 collective-permute-start.12
  303.7 4.9 %collective-permute-start.13 = (f32[64,515]{1,0:T(8,128)S(1)}, f32[64,515]{1,0:T(8,128)S(1)}, u32[]{:S(2)}, u32[]{:S(2)}) collective-permute-start(f32[64,515]{1,0:T(8,128)S(1)} %get-tuple-element.43), channel_id=1, source_target_pairs={{0,2},{1,3},{2,4},{3,5},{4,6},{5,7},{6,8},{7,9},{8,10},{9,11},{10,... | collective-permute-start | bytes 395528 | tf_op jit(solution)/shard_map/ppermute | solution.py:580
  308.7 5.3 %collective-permute-start.14 = (f32[64,515]{1,0:T(8,128)S(1)}, f32[64,515]{1,0:T(8,128)S(1)}, u32[]{:S(2)}, u32[]{:S(2)}) collective-permute-start(f32[64,515]{1,0:T(8,128)S(1)} %get-tuple-element.42), channel_id=1, source_target_pairs={{0,3},{1,4},{2,5},{3,6},{4,7},{5,8},{6,9},{7,10},{8,11},{9,12},{10... | collective-permute-start | bytes 395528 | tf_op jit(solution)/shard_map/ppermute | solution.py:580
  314.1 5.0 %collective-permute-start.15 = (f32[64,515]{1,0:T(8,128)S(1)}, f32[64,515]{1,0:T(8,128)S(1)}, u32[]{:S(2)}, u32[]{:S(2)}) collective-permute-start(f32[64,515]{1,0:T(8,128)S(1)} %get-tuple-element.41), channel_id=1, source_target_pairs={{0,4},{1,5},{2,6},{3,7},{4,8},{5,9},{6,10},{7,11},{8,12},{9,13},{1... | collective-permute-start | bytes 395528 | tf_op jit(solution)/shard_map/ppermute | solution.py:580
  319.3 5.9 %collective-permute-done.15 = f32[64,515]{1,0:T(8,128)S(1)} collective-permute-done((f32[64,515]{1,0:T(8,128)S(1)}, f32[64,515]{1,0:T(8,128)S(1)}, u32[]{:S(2)}, u32[]{:S(2)}) %collective-permute-start.15) | collective-permute-done | bytes 131872 | tf_op jit(solution)/shard_map/ppermute | solution.py:580
  325.1 1.4 fusion
  328.7 106.0 %all-reduce.9.cloned.1.call-done = f32[189440]{0:T(1024)} async-done(((f32[189440]{0:T(1024)}), f32[189440]{0:T(1024)}) %all-reduce.9.cloned.1.call-update) | async-done | bytes 757776
  434.8 1.4 fusion.19
  437.7 39.8 %all-reduce.2 = (f32[7]{0:T(128)S(1)}, f32[7]{0:T(128)S(1)}) all-reduce(f32[7]{0:T(128)S(1)} %convolution_bitcast_fusion.2, f32[7]{0:T(128)S(1)} %convolution_bitcast_fusion.1), channel_id=1, replica_groups=mesh['atoms'=16,'rep'=2] {'atoms','rep'}, use_global_device_ids=true, to_apply=%region_6.0 | all-reduce | flops 14 | bytes 112 | tf_op jit(solution)/shard_map/psum | solution.py:680
  (110 shorter events, 28.0 us)
Async XLA Ops:
  7.2 170.8 %all-reduce.7.cloned.1.call-start = ((), (), s32[]{:S(2)}) async-start(), calls=%async_computation | async-start | bytes 1515520
  14.7 64.1 %copy-start.7 = (f32[512,9]{0,1:T(8,128)S(1)}, f32[512,9]{0,1:T(8,128)}, u32[]{:S(2)}) copy-start(f32[512,9]{0,1:T(8,128)} %param.27) | copy-start | bytes 55300
  14.7 65.8 %collective-permute-start = (f32[64,515]{0,1:T(8,128)}, f32[64,515]{0,1:T(8,128)S(1)}, u32[]{:S(2)}, u32[]{:S(2)}) collective-permute-start(f32[64,515]{0,1:T(8,128)} %get-tuple-element.64), channel_id=1, source_target_pairs={{0,1},{1,2},{2,3},{3,4},{4,5},{5,6},{6,7},{7,8},{8,9},{9,10},{10,1... | collective-permute-start | bytes 395528 | tf_op jit(solution)/shard_map/ppermute | solution.py:580
  17.2 64.6 %collective-permute-start.1 = (f32[64,515]{0,1:T(8,128)}, f32[64,515]{0,1:T(8,128)S(1)}, u32[]{:S(2)}, u32[]{:S(2)}) collective-permute-start(f32[64,515]{0,1:T(8,128)} %get-tuple-element.63), channel_id=1, source_target_pairs={{0,2},{1,3},{2,4},{3,5},{4,6},{5,7},{6,8},{7,9},{8,10},{9,11},{10,... | collective-permute-start | bytes 395528 | tf_op jit(solution)/shard_map/ppermute | solution.py:580
  21.6 61.5 %collective-permute-start.2 = (f32[64,515]{0,1:T(8,128)}, f32[64,515]{0,1:T(8,128)S(1)}, u32[]{:S(2)}, u32[]{:S(2)}) collective-permute-start(f32[64,515]{0,1:T(8,128)} %get-tuple-element.62), channel_id=1, source_target_pairs={{0,3},{1,4},{2,5},{3,6},{4,7},{5,8},{6,9},{7,10},{8,11},{9,12},{10... | collective-permute-start | bytes 395528 | tf_op jit(solution)/shard_map/ppermute | solution.py:580
  25.9 59.3 %collective-permute-start.3 = (f32[64,515]{0,1:T(8,128)S(1)}, f32[64,515]{0,1:T(8,128)S(1)}, u32[]{:S(2)}, u32[]{:S(2)}) collective-permute-start(f32[64,515]{0,1:T(8,128)S(1)} %get-tuple-element.61), channel_id=1, source_target_pairs={{0,4},{1,5},{2,6},{3,7},{4,8},{5,9},{6,10},{7,11},{8,12},{9,13},{1... | collective-permute-start | bytes 395528 | tf_op jit(solution)/shard_map/ppermute | solution.py:580
  29.4 55.8 %collective-permute-start.4 = (f32[64,515]{0,1:T(8,128)S(1)}, f32[64,515]{0,1:T(8,128)}, u32[]{:S(2)}, u32[]{:S(2)}) collective-permute-start(f32[64,515]{0,1:T(8,128)S(1)} %get-tuple-element.60), channel_id=1, source_target_pairs={{1,0},{2,1},{3,2},{4,3},{5,4},{6,5},{7,6},{8,7},{9,8},{10,9},{11,1... | collective-permute-start | bytes 395528 | tf_op jit(solution)/shard_map/ppermute | solution.py:580
  32.1 402.6 %all-reduce.9.cloned.1.call-start = ((), (), s32[]{:S(2)}) async-start(), calls=%async_computation.1 | async-start | bytes 1515520
  80.5 11.7 %collective-permute-start.5 = (f32[64,515]{0,1:T(8,128)S(1)}, f32[64,515]{0,1:T(8,128)S(1)}, u32[]{:S(2)}, u32[]{:S(2)}) collective-permute-start(f32[64,515]{0,1:T(8,128)S(1)} %get-tuple-element.59), channel_id=1, source_target_pairs={{2,0},{3,1},{4,2},{5,3},{6,4},{7,5},{8,6},{9,7},{10,8},{11,9},{12,... | collective-permute-start | bytes 395528 | tf_op jit(solution)/shard_map/ppermute | solution.py:580
  81.8 11.5 %collective-permute-start.6 = (f32[64,515]{0,1:T(8,128)S(1)}, f32[64,515]{0,1:T(8,128)S(1)}, u32[]{:S(2)}, u32[]{:S(2)}) collective-permute-start(f32[64,515]{0,1:T(8,128)S(1)} %get-tuple-element.58), channel_id=1, source_target_pairs={{3,0},{4,1},{5,2},{6,3},{7,4},{8,5},{9,6},{10,7},{11,8},{12,9},{13... | collective-permute-start | bytes 395528 | tf_op jit(solution)/shard_map/ppermute | solution.py:580
  83.1 15.0 %collective-permute-start.7 = (f32[64,515]{0,1:T(8,128)S(1)}, f32[64,515]{0,1:T(8,128)S(1)}, u32[]{:S(2)}, u32[]{:S(2)}) collective-permute-start(f32[64,515]{0,1:T(8,128)S(1)} %get-tuple-element.57), channel_id=1, source_target_pairs={{4,0},{5,1},{6,2},{7,3},{8,4},{9,5},{10,6},{11,7},{12,8},{13,9},{1... | collective-permute-start | bytes 395528 | tf_op jit(solution)/shard_map/ppermute | solution.py:580
  295.4 8.3 %collective-permute-start.8 = (f32[64,515]{1,0:T(8,128)S(1)}, f32[64,515]{1,0:T(8,128)S(1)}, u32[]{:S(2)}, u32[]{:S(2)}) collective-permute-start(f32[64,515]{1,0:T(8,128)S(1)} %get-tuple-element.48), channel_id=1, source_target_pairs={{1,0},{2,1},{3,2},{4,3},{5,4},{6,5},{7,6},{8,7},{9,8},{10,9},{11,1... | collective-permute-start | bytes 395528 | tf_op jit(solution)/shard_map/ppermute | solution.py:580
  296.7 11.9 %collective-permute-start.9 = (f32[64,515]{1,0:T(8,128)S(1)}, f32[64,515]{1,0:T(8,128)S(1)}, u32[]{:S(2)}, u32[]{:S(2)}) collective-permute-start(f32[64,515]{1,0:T(8,128)S(1)} %get-tuple-element.47), channel_id=1, source_target_pairs={{2,0},{3,1},{4,2},{5,3},{6,4},{7,5},{8,6},{9,7},{10,8},{11,9},{12,... | collective-permute-start | bytes 395528 | tf_op jit(solution)/shard_map/ppermute | solution.py:580
  298.1 16.0 %collective-permute-start.10 = (f32[64,515]{1,0:T(8,128)S(1)}, f32[64,515]{1,0:T(8,128)S(1)}, u32[]{:S(2)}, u32[]{:S(2)}) collective-permute-start(f32[64,515]{1,0:T(8,128)S(1)} %get-tuple-element.46), channel_id=1, source_target_pairs={{3,0},{4,1},{5,2},{6,3},{7,4},{8,5},{9,6},{10,7},{11,8},{12,9},{13... | collective-permute-start | bytes 395528 | tf_op jit(solution)/shard_map/ppermute | solution.py:580
  299.4 19.8 %collective-permute-start.11 = (f32[64,515]{1,0:T(8,128)S(1)}, f32[64,515]{1,0:T(8,128)S(1)}, u32[]{:S(2)}, u32[]{:S(2)}) collective-permute-start(f32[64,515]{1,0:T(8,128)S(1)} %get-tuple-element.45), channel_id=1, source_target_pairs={{4,0},{5,1},{6,2},{7,3},{8,4},{9,5},{10,6},{11,7},{12,8},{13,9},{1... | collective-permute-start | bytes 395528 | tf_op jit(solution)/shard_map/ppermute | solution.py:580
  300.7 18.5 %collective-permute-start.12 = (f32[64,515]{1,0:T(8,128)S(1)}, f32[64,515]{1,0:T(8,128)S(1)}, u32[]{:S(2)}, u32[]{:S(2)}) collective-permute-start(f32[64,515]{1,0:T(8,128)S(1)} %get-tuple-element.44), channel_id=1, source_target_pairs={{0,1},{1,2},{2,3},{3,4},{4,5},{5,6},{6,7},{7,8},{8,9},{9,10},{10,1... | collective-permute-start | bytes 395528 | tf_op jit(solution)/shard_map/ppermute | solution.py:580
  303.7 15.5 %collective-permute-start.13 = (f32[64,515]{1,0:T(8,128)S(1)}, f32[64,515]{1,0:T(8,128)S(1)}, u32[]{:S(2)}, u32[]{:S(2)}) collective-permute-start(f32[64,515]{1,0:T(8,128)S(1)} %get-tuple-element.43), channel_id=1, source_target_pairs={{0,2},{1,3},{2,4},{3,5},{4,6},{5,7},{6,8},{7,9},{8,10},{9,11},{10,... | collective-permute-start | bytes 395528 | tf_op jit(solution)/shard_map/ppermute | solution.py:580
  308.7 10.6 %collective-permute-start.14 = (f32[64,515]{1,0:T(8,128)S(1)}, f32[64,515]{1,0:T(8,128)S(1)}, u32[]{:S(2)}, u32[]{:S(2)}) collective-permute-start(f32[64,515]{1,0:T(8,128)S(1)} %get-tuple-element.42), channel_id=1, source_target_pairs={{0,3},{1,4},{2,5},{3,6},{4,7},{5,8},{6,9},{7,10},{8,11},{9,12},{10... | collective-permute-start | bytes 395528 | tf_op jit(solution)/shard_map/ppermute | solution.py:580
  314.1 11.1 %collective-permute-start.15 = (f32[64,515]{1,0:T(8,128)S(1)}, f32[64,515]{1,0:T(8,128)S(1)}, u32[]{:S(2)}, u32[]{:S(2)}) collective-permute-start(f32[64,515]{1,0:T(8,128)S(1)} %get-tuple-element.41), channel_id=1, source_target_pairs={{0,4},{1,5},{2,6},{3,7},{4,8},{5,9},{6,10},{7,11},{8,12},{9,13},{1... | collective-permute-start | bytes 395528 | tf_op jit(solution)/shard_map/ppermute | solution.py:580
  327.1 107.6 %copy-start.8 = (f32[5920]{0:T(1024)S(1)}, f32[5920]{0:T(1024)}, u32[]{:S(2)}) copy-start(f32[5920]{0:T(1024)} %param.35) | copy-start | bytes 71044
  327.1 107.6 %copy-start.9 = (f32[5920]{0:T(1024)S(1)}, f32[5920]{0:T(1024)}, u32[]{:S(2)}) copy-start(f32[5920]{0:T(1024)} %param.34) | copy-start | bytes 71044
  327.8 109.1 %copy-start.2 = (f32[512,128]{1,0:T(8,128)S(1)}, f32[512,128]{1,0:T(8,128)}, u32[]{:S(2)}) copy-start(f32[512,128]{1,0:T(8,128)} %get-tuple-element.24) | copy-start | bytes 786436
  436.2 42.2 %copy-start.4 = (f32[5920]{0:T(1024)}, f32[5920]{0:T(1024)S(1)}, u32[]{:S(2)}) copy-start(f32[5920]{0:T(1024)S(1)} %get-tuple-element.38) | copy-start | bytes 71044
  436.2 42.2 %copy-start.5 = (f32[5920]{0:T(1024)}, f32[5920]{0:T(1024)S(1)}, u32[]{:S(2)}) copy-start(f32[5920]{0:T(1024)S(1)} %get-tuple-element.39) | copy-start | bytes 71044
  (11 other events, 102.8 us)
Sparse Core Ops, SparseCore 0:
  32.2 145.7 all-reduce.6
  298.2 136.5 all-reduce.8

commit v2 on v1

--- a/solution.py
+++ b/solution.py
@@ -20,7 +20,6 @@
 RATE = 0.3
 DECAY = 0.01
 EPSILON = 1e-06
-PRECISION_MAX = lax.Precision.HIGHEST
 
 BLOCK = 256
 WINDOW = 128
@@ -31,10 +30,9 @@
 
 AT_W1, AT_W2, AT_WF, AT_WM, AT_U1, AT_U2 = 0, 128, 512, 572, 828, 1084
 AT_B1, AT_B2, AT_BF, AT_C1, AT_C2, AT_READ, PARAM_ROWS = 1468, 1469, 1472, 1475, 1476, 1479, 1480
-
-
-def product(left, right):
-    return jnp.dot(left, right, precision=PRECISION_MAX, preferred_element_type=F32)
+PARAM_PAD = PARAM_ROWS + 8
+GROUP_ENDS = (128, 512, 572, 828, 1084, 1468)
+MESH = pl.DeviceIdType.MESH
 
 
 def mm(left, right, contract=(1, 0)):
@@ -89,8 +87,7 @@
     s_own,
     v_own,
     p_own,
-    s_halo,
-    v_halo,
+    halo_rows,
     p_halo,
     cot_s,
     cot_v,
@@ -99,9 +96,9 @@
     v_two,
     gs_own,
     gv_own,
-    gs_halo,
-    gv_halo,
-    gp,
+    g_halo,
+    gp_own,
+    gp_halo,
     gpar,
     tab,
     rows,
@@ -124,7 +121,9 @@
     gpd,
 ):
     atoms = s_own.shape[0]
-    halo = s_halo.shape[0]
+    halo = halo_rows.shape[1]
+    s_halo, v_halo = halo_rows.at[0], halo_rows.at[1:4]
+    gs_halo, gv_halo = g_halo.at[0], g_halo.at[1:4]
     edges = shift_v.shape[1]
     blocks = edges // BLOCK
 
@@ -170,7 +169,7 @@
         (s_own, v_own, p_own, 0, atoms),
         (s_halo, v_halo, p_halo, atoms, halo),
     ):
-        place = jnp.concatenate([p_ref[...], jnp.zeros((F - 3, count), F32)], axis=0)
+        place = jnp.concatenate([p_ref[0:3, :], jnp.zeros((F - 3, count), F32)], axis=0)
         tab[pl.ds(base * 8 + 6, count, stride=8), :] = jnp.transpose(place)
         tab[pl.ds(base * 8 + 7, count, stride=8), :] = jnp.zeros((count, F), F32)
         for c in range(3):
@@ -462,9 +461,9 @@
                 to = rows_of(src_s[e] * 8, 8, 8)
                 total[to, :] += rows[rows_of(e * 8, 8, 8), :]
 
-    for s_ref, gs_ref, gv_ref, base, count in (
-        (s_own, gs_own, gv_own, 0, atoms),
-        (s_halo, gs_halo, gv_halo, atoms, halo),
+    for s_ref, gs_ref, gv_ref, gp_ref, base, count in (
+        (s_own, gs_own, gv_own, gp_own, 0, atoms),
+        (s_halo, gs_halo, gv_halo, gp_halo, atoms, halo),
     ):
         own = base == 0
         for k in range(0, count, ROWS):
@@ -472,7 +471,7 @@
             place = jnp.transpose(tab[at, :] + acc[at, :])[0:8]
             if own:
                 place = place - gpd[:, k : k + ROWS]
-            gp[:, base + k : base + k + ROWS] = place
+            gp_ref[:, k : k + ROWS] = place
 
         @pl.loop(0, count // ROWS)
         def _(step):
@@ -521,10 +520,10 @@
         shape((3, atoms, F), F32),
         shape((atoms, F), F32),
         shape((3, atoms, F), F32),
-        shape((halo, F), F32),
-        shape((3, halo, F), F32),
-        shape((8, total), F32),
-        shape((PARAM_ROWS, F), F32),
+        shape((4, halo, F), F32),
+        shape((8, atoms), F32),
+        shape((8, halo), F32),
+        shape((PARAM_PAD, F), F32),
     )
     scratch = [
         pltpu.VMEM((total * 8, F), F32),
@@ -558,26 +557,651 @@
     )
 
 
-def layout():
-    shapes = [(F, F), (F, 3 * F), (R, 3 * F), (F, 2 * F), (2 * F, F), (F, 3 * F)]
-    lengths = [F, 3 * F, 3 * F, F, 3 * F, F]
-    return (shapes, lengths)
-
-
-def group_ids(index):
-    shapes, lengths = layout()
-    labels = jnp.zeros(index.shape, jnp.int32)
-    start = 0
-    for shape in shapes:
-        start += shape[0] * shape[1]
-        labels = labels + (index >= start).astype(jnp.int32)
-    return labels
-
-
-def passed_along(shard, axis, by):
-    devices = lax.axis_size(axis)
-    pairs = [(i, i + by) for i in range(devices) if 0 <= i + by < devices]
-    return lax.ppermute(shard, axis, pairs)
+def hop_offset(j):
+    return j + 1 if j < HOPS else HOPS - 1 - j
+
+
+class Place:
+    def __init__(self):
+        self.chips = lax.axis_size("atoms")
+        self.cores = lax.axis_size("rep")
+        self.count = self.chips * self.cores
+        self.groups = self.chips // 4
+        chip = lax.axis_index("atoms")
+        self.core = lax.axis_index("rep")
+        self.joint = chip * self.cores + self.core
+        self.group = chip // 4
+        self.quarter = chip % 4
+        self.mate = 1 - self.core
+
+    def other_groups(self):
+        return [lax.rem(self.group + k, self.groups) for k in range(1, self.groups)]
+
+    def other_quarters(self):
+        return [lax.rem(self.quarter + k, 4) for k in range(1, 4)]
+
+    def in_group(self, group):
+        return (group * 4 + self.quarter, self.core)
+
+    def in_quarter(self, quarter):
+        return (self.group * 4 + quarter, self.core)
+
+    def beside(self):
+        return (self.group * 4 + self.quarter, self.mate)
+
+    def hop(self, by):
+        other = self.joint + by
+        exists = (other >= 0) & (other < self.count)
+        other = jnp.clip(other, 0, self.count - 1)
+        return exists, (other // self.cores, other % self.cores)
+
+    def greet(self):
+        barrier = pltpu.get_barrier_semaphore()
+        fixed = [self.in_group(g) for g in self.other_groups()]
+        fixed += [self.in_quarter(q) for q in self.other_quarters()]
+        fixed.append(self.beside())
+        for device in fixed:
+            pl.semaphore_signal(barrier, inc=1, device_id=device, device_id_type=MESH)
+        hops = [self.hop(hop_offset(j)) for j in range(2 * HOPS)]
+        expected = jnp.int32(len(fixed))
+        for exists, device in hops:
+            expected = expected + jnp.where(exists, 1, 0)
+
+            @pl.when(exists)
+            def _():
+                pl.semaphore_signal(barrier, inc=1, device_id=device, device_id_type=MESH)
+
+        pl.semaphore_wait(barrier, expected)
+
+
+def send(src, dst, send_sem, recv_sem, device):
+    return pltpu.make_async_remote_copy(
+        src_ref=src,
+        dst_ref=dst,
+        send_sem=send_sem,
+        recv_sem=recv_sem,
+        device_id=device,
+        device_id_type=MESH,
+    )
+
+
+def start_all(copies):
+    for copy in copies:
+        copy.start()
+    return copies
+
+
+def wait_sent(copies):
+    for copy in copies:
+        copy.wait_send()
+
+
+def window_rows(length):
+    return -(-((length + F - 1) // F + 1) // 8) * 8
+
+
+class SmallSum:
+    def __init__(self, place, slots_a, slots_b, slots_c, sends, recvs):
+        self.place = place
+        self.slots = (slots_a, slots_b, slots_c)
+        self.sends, self.recvs = sends, recvs
+        self.sent = []
+
+    def start(self, phase, value):
+        p = self.place
+        slots = self.slots[phase]
+        mine = (p.group, p.quarter, p.core)[phase]
+        slots[mine] = value
+        base = (0, p.groups, p.groups + 4)[phase]
+        devices = (
+            [p.in_group(g) for g in p.other_groups()],
+            [p.in_quarter(q) for q in p.other_quarters()],
+            [p.beside()],
+        )[phase]
+        for k, device in enumerate(devices):
+            self.sent.append(
+                send(
+                    slots.at[mine],
+                    slots.at[mine],
+                    self.sends.at[base + k],
+                    self.recvs.at[base + mine],
+                    device,
+                )
+            )
+            self.sent[-1].start()
+
+    def finish(self, phase):
+        p = self.place
+        slots = self.slots[phase]
+        base = (0, p.groups, p.groups + 4)[phase]
+        others = (p.other_groups(), p.other_quarters(), [p.mate])[phase]
+        for o in others:
+            send(
+                slots.at[o], slots.at[o], self.sends.at[base], self.recvs.at[base + o], p.beside()
+            ).wait_recv()
+        total = slots[0]
+        for k in range(1, slots.shape[0]):
+            total = total + slots[k]
+        return total
+
+    def done(self):
+        wait_sent(self.sent)
+
+
+def small_scratch(groups, rows):
+    count = groups + 4 + 2
+    return [
+        pltpu.VMEM((groups, rows, F), F32),
+        pltpu.VMEM((4, rows, F), F32),
+        pltpu.VMEM((2, rows, F), F32),
+        pltpu.SemaphoreType.DMA((count,)),
+        pltpu.SemaphoreType.DMA((count,)),
+    ]
+
+
+def lay_flat(ref, count):
+    return jnp.concatenate([ref[k : k + 1, :] for k in range(count)], axis=1)
+
+
+def gather_kernel(
+    send_s,
+    par_in,
+    s_own,
+    v_own,
+    p_own,
+    energy,
+    elements,
+    forces,
+    par,
+    halo_rows,
+    p_halo,
+    goal,
+    stats,
+    slots,
+    pack,
+    places,
+    p_out,
+    p_in,
+    zeros,
+    ag_send,
+    ag_recv,
+    row_send,
+    row_recv,
+    place_send,
+    place_recv,
+    zero_sem,
+    *small,
+    length,
+):
+    here = Place()
+    atoms = s_own.shape[0]
+    cap = halo_rows.shape[1] // (2 * HOPS)
+    wide = slots.shape[3]
+    here.greet()
+    sums = SmallSum(here, *small)
+
+    offset = lax.rem(here.joint * length, F)
+    lane = lax.broadcasted_iota(jnp.int32, (1, F), 1)
+    turned = pltpu.roll(par_in[...], offset, 1)
+    above = jnp.concatenate([jnp.zeros((1, F), F32), turned[: wide - 1]], axis=0)
+    mine = slots.at[here.group, here.quarter, here.core]
+    mine[...] = jnp.where(lane < offset, above, turned)
+    first = start_all(
+        [
+            send(mine, mine, ag_send.at[k], ag_recv.at[here.group], here.in_group(g))
+            for k, g in enumerate(here.other_groups())
+        ]
+    )
+
+    count = atoms // F
+    energy_row, element_row = lay_flat(energy, count), lay_flat(elements, count)
+    hot = jnp.where(
+        element_row == lax.broadcasted_iota(jnp.int32, (F, atoms), 0), 1.0, 0.0
+    ).astype(BF16)
+    high = energy_row.astype(BF16).astype(F32)
+    middle = (energy_row - high).astype(BF16).astype(F32)
+    eight = lax.broadcasted_iota(jnp.int32, (8, 1), 0)
+    left = jnp.where(
+        eight == 0,
+        high,
+        jnp.where(
+            eight == 1, middle, jnp.where(eight == 2, energy_row - high - middle, jnp.where(eight == 3, 1.0, 0.0))
+        ),
+    )
+    found = mm(left.astype(BF16), hot, (1, 1))
+    squares = jnp.sum(forces[...] * forces[...], axis=0, keepdims=True)
+    square = squares[:, 0:F]
+    for k in range(1, count):
+        square = square + squares[:, k * F : (k + 1) * F]
+    tile = jnp.where(
+        eight == 0,
+        found[0:1] + found[1:2] + found[2:3],
+        jnp.where(eight == 1, found[3:4], jnp.where(eight == 2, square, 0.0)),
+    )
+    sums.start(0, tile)
+
+    places[...] = jnp.transpose(
+        jnp.concatenate([p_own[...], jnp.zeros((F - 3, atoms), F32)], axis=0)
+    )
+    zeros[...] = jnp.zeros_like(zeros)
+    hops = range(2 * HOPS)
+    row_copies, place_copies = [], []
+    for j in hops:
+        exists, device = here.hop(hop_offset(j))
+        block = pl.ds(j * cap, cap)
+
+        @pl.loop(0, cap // 8)
+        def _(step):
+            for k in range(8):
+                r = j * cap + step * 8 + k
+                t = send_s[r]
+                pack[0, pl.ds(r, 1), :] = s_own[pl.ds(t, 1), :]
+                for c in range(3):
+                    pack[1 + c, pl.ds(r, 1), :] = v_own[c, pl.ds(t, 1), :]
+                p_out[pl.ds(r, 1), :] = places[pl.ds(t, 1), :]
+
+        copy = send(
+            pack.at[:, block], halo_rows.at[:, block], row_send.at[j], row_recv.at[j], device
+        )
+        row_copies.append((exists, copy))
+
+        @pl.when(exists)
+        def _():
+            copy.start()
+
+    for j in range(0, 2 * HOPS, 2):
+        pair = slice(j * cap, (j + 2) * cap)
+        p_in[2 * HOPS + j // 2] = jnp.transpose(p_out[pair, :])[0:8]
+        for k in (j, j + 1):
+            exists, device = here.hop(hop_offset(k))
+            copy = send(
+                p_in.at[2 * HOPS + j // 2], p_in.at[k], place_send.at[k], place_recv.at[k], device
+            )
+            place_copies.append((exists, copy))
+
+            @pl.when(exists)
+            def _():
+                copy.start()
+
+    for j in hops:
+        known, device = here.hop(-hop_offset(j))
+
+        @pl.when(jnp.logical_not(known))
+        def _():
+            p_in[j] = jnp.zeros((8, F), F32)
+            fill = pltpu.make_async_copy(
+                zeros, halo_rows.at[:, pl.ds(j * cap, cap)], zero_sem.at[j]
+            )
+            fill.start()
+            fill.wait()
+
+    for g in here.other_groups():
+        spot = slots.at[g, here.quarter, here.core]
+        send(spot, spot, ag_send.at[0], ag_recv.at[g], here.beside()).wait_recv()
+    base = here.groups
+    line = slots.at[:, here.quarter, here.core]
+    second = start_all(
+        [
+            send(line, line, ag_send.at[base + k], ag_recv.at[base + here.quarter], here.in_quarter(q))
+            for k, q in enumerate(here.other_quarters())
+        ]
+    )
+    third = [
+        send(
+            line, line, ag_send.at[base + 4], ag_recv.at[base + 4 + here.quarter], here.beside()
+        )
+    ]
+    third[0].start()
+    sums.start(1, sums.finish(0))
+    for k, q in enumerate(here.other_quarters()):
+        line = slots.at[:, q, here.core]
+        send(line, line, ag_send.at[0], ag_recv.at[base + q], here.beside()).wait_recv()
+        copy = send(
+            line, line, ag_send.at[base + 5 + k], ag_recv.at[base + 4 + q], here.beside()
+        )
+        copy.start()
+        third.append(copy)
+    sums.start(2, sums.finish(1))
+    for q in range(4):
+        line = slots.at[:, q, here.mate]
+        send(line, line, ag_send.at[0], ag_recv.at[base + 4 + q], here.beside()).wait_recv()
+
+    par[...] = jnp.zeros_like(par)
+    for p in range(here.count):
+        row = p * length // F
+        chip, core = p // here.cores, p % here.cores
+        take = min(wide, PARAM_PAD - row)
+        par[row : row + take, :] += slots[chip // 4, chip % 4, core, 0:take, :]
+
+    total = sums.finish(2)
+    mean = total[0:1] / jnp.maximum(total[1:2], 1.0)
+    whole = jnp.sum(total[2:3], axis=1, keepdims=True)
+    scale = jnp.sqrt(whole / (3.0 * atoms * here.count) + 1e-06)
+    high = mean.astype(BF16).astype(F32)
+    middle = (mean - high).astype(BF16).astype(F32)
+    left = jnp.where(
+        eight == 0,
+        high,
+        jnp.where(eight == 1, middle, jnp.where(eight == 2, mean - high - middle, 0.0)),
+    )
+    found = mm(left.astype(BF16), hot)
+    goal[...] = (energy_row - (found[0:1] + found[1:2] + found[2:3])) / scale
+    stats[...] = jnp.where(eight == 0, mean, jnp.where(eight == 1, scale, 0.0))
+
+    for j in hops:
+        known, device = here.hop(-hop_offset(j))
+
+        @pl.when(known)
+        def _():
+            block = pl.ds(j * cap, cap)
+            send(
+                pack.at[:, block], halo_rows.at[:, block], row_send.at[j], row_recv.at[j], device
+            ).wait_recv()
+            send(p_in.at[j], p_in.at[j], place_send.at[j], place_recv.at[j], device).wait_recv()
+
+    low_half = lane < cap
+    for j in range(0, 2 * HOPS, 2):
+        p_halo[:, j * cap : (j + 2) * cap] = jnp.where(low_half, p_in[j], p_in[j + 1])
+    for exists, copy in row_copies + place_copies:
+
+        @pl.when(exists)
+        def _():
+            copy.wait_send()
+
+    wait_sent(first + second + third)
+    sums.done()
+
+
+def gather_all(atoms, cap, groups, length):
+    shape = jax.ShapeDtypeStruct
+    halo = 2 * HOPS * cap
+    wide = window_rows(length)
+    in_vmem = pl.BlockSpec(memory_space=pltpu.VMEM)
+    in_smem = pl.BlockSpec(memory_space=pltpu.SMEM)
+    return pl.pallas_call(
+        functools.partial(gather_kernel, length=length),
+        out_shape=(
+            shape((PARAM_PAD, F), F32),
+            shape((4, halo, F), F32),
+            shape((8, halo), F32),
+            shape((1, atoms), F32),
+            shape((8, F), F32),
+        ),
+        in_specs=[in_smem] + [in_vmem] * 7,
+        out_specs=(in_vmem, pl.BlockSpec(memory_space=pl.ANY), in_vmem, in_vmem, in_vmem),
+        scratch_shapes=[
+            pltpu.VMEM((groups, 4, 2, wide, F), F32),
+            pltpu.VMEM((4, halo, F), F32),
+            pltpu.VMEM((atoms, F), F32),
+            pltpu.VMEM((halo, F), F32),
+            pltpu.VMEM((3 * HOPS, 8, F), F32),
+            pltpu.VMEM((4, cap, F), F32),
+            pltpu.SemaphoreType.DMA((groups + 8,)),
+            pltpu.SemaphoreType.DMA((groups + 8,)),
+            pltpu.SemaphoreType.DMA((2 * HOPS,)),
+            pltpu.SemaphoreType.DMA((2 * HOPS,)),
+            pltpu.SemaphoreType.DMA((2 * HOPS,)),
+            pltpu.SemaphoreType.DMA((2 * HOPS,)),
+            pltpu.SemaphoreType.DMA((2 * HOPS,)),
+        ]
+        + small_scratch(groups, 8),
+        compiler_params=pltpu.CompilerParams(
+            collective_id=0, has_side_effects=True, vmem_limit_bytes=40 * 1024 * 1024
+        ),
+        name="gather_inputs",
+    )
+
+
+def reduce_kernel(
+    gpar,
+    g_halo,
+    gp_halo,
+    gs_own,
+    gv_own,
+    gp_own,
+    pick,
+    par,
+    one,
+    two,
+    grad_s,
+    grad_v,
+    grad_p,
+    grad,
+    one_new,
+    two_new,
+    par_new,
+    norms,
+    slots,
+    pair_in,
+    line_in,
+    spot_in,
+    back,
+    p_back,
+    turn,
+    rs_send,
+    rs_recv,
+    row_send,
+    row_recv,
+    place_send,
+    place_recv,
+    *small,
+    length,
+):
+    here = Place()
+    atoms = gs_own.shape[0]
+    cap = back.shape[1] // (2 * HOPS)
+    wide = slots.shape[3]
+    here.greet()
+    sums = SmallSum(here, *small)
+
+    for p in range(here.count):
+        row = p * length // F
+        chip, core = p // here.cores, p % here.cores
+        take = min(wide, PARAM_PAD - row)
+        slots[chip // 4, chip % 4, core, 0:take, :] = gpar[row : row + take, :]
+    order = here.other_quarters() + [here.quarter]
+    base = here.groups
+    third = start_all(
+        [
+            send(
+                slots.at[:, q, here.mate],
+                pair_in.at[:, q],
+                rs_send.at[base + 4 + k],
+                rs_recv.at[base + 4 + q],
+                here.beside(),
+            )
+            for k, q in enumerate(order)
+        ]
+    )
+
+    hops = range(2 * HOPS)
+    copies = []
+    for j in hops:
+        exists, device = here.hop(-hop_offset(j))
+        block = pl.ds(j * cap, cap)
+        tile = pl.ds((j // 2) * F, F)
+        rows_copy = send(
+            g_halo.at[:, block], back.at[:, block], row_send.at[j], row_recv.at[j], device
+        )
+        place_copy = send(
+            gp_halo.at[:, tile], p_back.at[j], place_send.at[j], place_recv.at[j], device
+        )
+        copies += [(exists, rows_copy), (exists, place_copy)]
+
+        @pl.when(exists)
+        def _():
+            rows_copy.start()
+            place_copy.start()
+
+        known, device = here.hop(hop_offset(j))
+
+        @pl.when(jnp.logical_not(known))
+        def _():
+            back[:, block, :] = jnp.zeros((4, cap, F), F32)
+            p_back[j] = jnp.zeros((8, F), F32)
+
+    second = []
+    for k, q in enumerate(order):
+        line = pair_in.at[:, q]
+        send(line, line, rs_send.at[0], rs_recv.at[base + 4 + q], here.beside()).wait_recv()
+        slots[:, q, here.core] += pair_in[:, q]
+        if k < 3:
+            copy = send(
+                slots.at[:, q, here.core],
+                line_in.at[here.quarter],
+                rs_send.at[base + k],
+                rs_recv.at[base + here.quarter],
+                here.in_quarter(q),
+            )
+            copy.start()
+            second.append(copy)
+    for q in here.other_quarters():
+        line = line_in.at[q]
+        send(line, line, rs_send.at[0], rs_recv.at[base + q], here.beside()).wait_recv()
+        slots[:, here.quarter, here.core] += line_in[q]
+    first = start_all(
+        [
+            send(
+                slots.at[g, here.quarter, here.core],
+                spot_in.at[here.group],
+                rs_send.at[k],
+                rs_recv.at[here.group],
+                here.in_group(g),
+            )
+            for k, g in enumerate(here.other_groups())
+        ]
+    )
+    total = slots[here.group, here.quarter, here.core]
+    for g in here.other_groups():
+        spot = spot_in.at[g]
+        send(spot, spot, rs_send.at[0], rs_recv.at[g], here.beside()).wait_recv()
+        total = total + spot_in[g]
+
+    offset = lax.rem(here.joint * length, F)
+    lane = lax.broadcasted_iota(jnp.int32, (1, F), 1)
+    turn[0:wide, :] = pltpu.roll(total, lax.rem(F - offset, F), 1)
+    turn[wide : wide + 8, :] = jnp.zeros((8, F), F32)
+    place = lax.broadcasted_iota(jnp.int32, (wide, F), 0) * F + lane
+    inside = place < length
+    g = jnp.where(lane + offset < F, turn[0:wide, :], turn[1 : wide + 1, :])
+    g = jnp.where(inside, g, 0.0)
+    grad[...] = g
+    m_one = BETA_ONE * one[...] + (1.0 - BETA_ONE) * g
+    m_two = BETA_TWO * two[...] + (1.0 - BETA_TWO) * g * g
+    one_new[...] = m_one
+    two_new[...] = m_two
+    direction = (
+        m_one
+        / (1.0 - BETA_ONE**STEP)
+        / (jnp.sqrt(m_two / (1.0 - BETA_TWO**STEP)) + EPSILON)
+        + DECAY * par[...]
+    )
+    spot = place + here.joint * length
+    label = jnp.zeros((wide, F), jnp.int32)
+    for end in GROUP_ENDS:
+        label = label + jnp.where(spot >= end * F, 1, 0)
+    label = jnp.where(inside, label, GROUPS)
+    lines = []
+    for value in (par[...], direction):
+        square = value * value
+        lines += [
+            jnp.sum(jnp.where(label == k, square, 0.0), axis=0, keepdims=True)
+            for k in range(GROUPS)
+        ]
+        lines.append(jnp.zeros((1, F), F32))
+    sums.start(0, jnp.concatenate(lines, axis=0))
+
+    hot = jnp.where(
+        pick[...] == lax.broadcasted_iota(jnp.int32, (atoms, 2 * HOPS * cap), 0), 1.0, 0.0
+    ).astype(BF16)
+    for j in hops:
+        known, device = here.hop(hop_offset(j))
+
+        @pl.when(known)
+        def _():
+            block = pl.ds(j * cap, cap)
+            tile = p_back.at[j]
+            send(
+                back.at[:, block], back.at[:, block], row_send.at[j], row_recv.at[j], device
+            ).wait_recv()
+            send(tile, tile, place_send.at[j], place_recv.at[j], device).wait_recv()
+
+    sums.start(1, sums.finish(0))
+    for k in range(2):
+        high, low = split(back[k])
+        extra = mm(hot, high) + mm(hot, low)
+        if k == 0:
+            grad_s[...] = gs_own[...] + extra
+        else:
+            grad_v[k - 1] = gv_own[k - 1] + extra
+    sums.start(2, sums.finish(1))
+    for k in range(2, 4):
+        high, low = split(back[k])
+        grad_v[k - 1] = gv_own[k - 1] + (mm(hot, high) + mm(hot, low))
+    low_half = lane < cap
+    place = jnp.concatenate(
+        [jnp.where(low_half, p_back[j], p_back[j + 1]) for j in range(0, 2 * HOPS, 2)], axis=1
+    )
+    high = place.astype(BF16).astype(F32)
+    middle = (place - high).astype(BF16).astype(F32)
+    pieces = jnp.concatenate([high, middle, place - high - middle, jnp.zeros_like(place)], axis=0)
+    got = mm(pieces.astype(BF16), hot, (1, 1))
+    grad_p[...] = gp_own[...] + (got[0:8] + got[8:16] + got[16:24])
+
+    whole = jnp.sqrt(jnp.sum(sums.finish(2), axis=1, keepdims=True))
+    ratio = whole[0:8] / whole[8:16]
+    norms[...] = jnp.broadcast_to(whole, (16, F))
+    trust = jnp.zeros((wide, F), F32)
+    for k in range(GROUPS):
+        trust = jnp.where(label == k, ratio[k : k + 1], trust)
+    par_new[...] = par[...] - RATE * trust * direction
+
+    for exists, copy in copies:
+
+        @pl.when(exists)
+        def _():
+            copy.wait_send()
+
+    wait_sent(first + second + third)
+    sums.done()
+
+
+def reduce_all(atoms, cap, groups, length):
+    shape = jax.ShapeDtypeStruct
+    halo = 2 * HOPS * cap
+    wide = window_rows(length)
+    in_vmem = pl.BlockSpec(memory_space=pltpu.VMEM)
+    outs = (
+        [shape((atoms, F), F32), shape((3, atoms, F), F32), shape((8, atoms), F32)]
+        + [shape((wide, F), F32)] * 4
+        + [shape((16, F), F32)]
+    )
+    return pl.pallas_call(
+        functools.partial(reduce_kernel, length=length),
+        out_shape=tuple(outs),
+        in_specs=[in_vmem] * 10,
+        out_specs=(in_vmem,) * len(outs),
+        scratch_shapes=[
+            pltpu.VMEM((groups, 4, 2, wide, F), F32),
+            pltpu.VMEM((groups, 4, wide, F), F32),
+            pltpu.VMEM((4, groups, wide, F), F32),
+            pltpu.VMEM((groups, wide, F), F32),
+            pltpu.VMEM((4, halo, F), F32),
+            pltpu.VMEM((2 * HOPS, 8, F), F32),
+            pltpu.VMEM((wide + 8, F), F32),
+            pltpu.SemaphoreType.DMA((groups + 8,)),
+            pltpu.SemaphoreType.DMA((groups + 8,)),
+            pltpu.SemaphoreType.DMA((2 * HOPS,)),
+            pltpu.SemaphoreType.DMA((2 * HOPS,)),
+            pltpu.SemaphoreType.DMA((2 * HOPS,)),
+            pltpu.SemaphoreType.DMA((2 * HOPS,)),
+        ]
+        + small_scratch(groups, 16),
+        compiler_params=pltpu.CompilerParams(
+            collective_id=1, has_side_effects=True, vmem_limit_bytes=40 * 1024 * 1024
+        ),
+        name="reduce_outputs",
+    )
 
 
 def body(
@@ -600,39 +1224,30 @@
     first_moment,
     second_moment,
 ):
-    both = ("atoms", "rep")
-    atoms_dev = scalars_in.shape[0]
-    edges_dev = edge_src.shape[0]
-    capacity = send_rows.shape[2]
-    hop_offsets = [k + 1 for k in range(HOPS)] + [-(k + 1) for k in range(HOPS)]
-    all_params = lax.all_gather(params, both, axis=0, tiled=True)
-    onehot = (elements[:, None] == jnp.arange(ELEMS, dtype=jnp.int32)[None, :]).astype(F32)
-    elem_total = product(target_energy[None, :], onehot)[0]
-    elem_count = jnp.sum(onehot, axis=0)
-    force_square = jnp.sum(forces * forces)
-    elem_total, elem_count, force_square = lax.psum((elem_total, elem_count, force_square), both)
-    element_mean = elem_total / jnp.maximum(elem_count, 1.0)
-    total_atoms = atoms_dev * lax.axis_size(both)
-    force_scale = jnp.sqrt(force_square / (3.0 * total_atoms) + 1e-06)
-    goal = (target_energy - product(onehot, element_mean[:, None])[:, 0]) / force_scale
-
-    picker = (
-        send_rows[0].reshape(-1)[:, None] == jnp.arange(atoms_dev, dtype=jnp.int32)[None, :]
-    ).astype(F32)
-    joined = jnp.concatenate(
-        [scalars_in, vectors_in[0], vectors_in[1], vectors_in[2], jnp.transpose(positions)], axis=1
-    )
-    picked = product(picker, joined).reshape(2 * HOPS, capacity, 4 * F + 3)
-    received = jnp.concatenate(
-        [passed_along(picked[k], both, hop_offsets[k]) for k in range(2 * HOPS)], axis=0
-    )
-    halo_rows = 2 * HOPS * capacity
-    s_halo = received[:, :F]
-    v_halo = jnp.stack([received[:, (c + 1) * F : (c + 2) * F] for c in range(3)])
-    p_halo = jnp.transpose(received[:, 4 * F :])
-
-    run = layer(atoms_dev, halo_rows, edges_dev, 4, 13)
-    s_two, v_two, gs_own, gv_own, gs_halo, gv_halo, gp, gpar = run(
+    atoms = scalars_in.shape[0]
+    edges = edge_src.shape[0]
+    cap = send_rows.shape[2]
+    halo = 2 * HOPS * cap
+    groups = lax.axis_size("atoms") // 4
+    length = params.shape[0]
+    wide = window_rows(length)
+
+    def padded(value):
+        return jnp.pad(value, (0, wide * F - length)).reshape(wide, F)
+
+    par_share = padded(params)
+    pick = send_rows.reshape(1, halo)
+    par, halo_rows, p_halo, goal, stats = gather_all(atoms, cap, groups, length)(
+        pick.reshape(-1),
+        par_share,
+        scalars_in,
+        vectors_in,
+        positions,
+        target_energy.reshape(-1, F),
+        elements.reshape(-1, F),
+        forces,
+    )
+    s_two, v_two, gs_own, gv_own, g_halo, gp_own, gp_halo, gpar = layer(atoms, halo, edges, 4, 12)(
         edge_src,
         edge_dst,
         edge_count,
@@ -640,63 +1255,50 @@
         edge_dst.reshape(-1, F),
         edge_shift,
         lattice,
-        all_params.reshape(PARAM_ROWS, F),
+        par,
         scalars_in,
         vectors_in,
         positions,
-        s_halo,
-        v_halo,
+        halo_rows,
         p_halo,
         cotan_scalar,
         cotan_vector,
-        goal[None, :],
-    )
-    back = jnp.concatenate(
-        [gs_halo, gv_halo[0], gv_halo[1], gv_halo[2], jnp.transpose(gp[:3, atoms_dev:])], axis=1
-    ).reshape(2 * HOPS, capacity, 4 * F + 3)
-    returned = jnp.concatenate(
-        [passed_along(back[k], both, -hop_offsets[k]) for k in range(2 * HOPS)], axis=0
-    )
-    added = product(jnp.transpose(picker), returned)
-    grad_scalars = gs_own + added[:, :F]
-    grad_vectors = gv_own + jnp.stack([added[:, (c + 1) * F : (c + 2) * F] for c in range(3)])
-    grad_positions = gp[:3, :atoms_dev] + jnp.transpose(added[:, 4 * F :])
-
-    grad_shard = lax.psum_scatter(gpar.reshape(-1), both, scatter_dimension=0, tiled=True)
-    shard_len = params.shape[0]
-    moment_one = BETA_ONE * first_moment + (1.0 - BETA_ONE) * grad_shard
-    moment_two = BETA_TWO * second_moment + (1.0 - BETA_TWO) * grad_shard * grad_shard
-    direction = (
-        moment_one
-        / (1.0 - BETA_ONE**STEP)
-        / (jnp.sqrt(moment_two / (1.0 - BETA_TWO**STEP)) + EPSILON)
-        + DECAY * params
-    )
-    first_index = lax.axis_index(both) * shard_len
-    labels = group_ids(first_index + jnp.arange(shard_len, dtype=jnp.int32))
-    member = (labels[None, :] == jnp.arange(GROUPS, dtype=jnp.int32)[:, None]).astype(F32)
-    weight_square = product(member, (params * params)[:, None])[:, 0]
-    update_square = product(member, (direction * direction)[:, None])[:, 0]
-    weight_square, update_square = lax.psum((weight_square, update_square), both)
-    weight_norms = jnp.sqrt(weight_square)
-    update_norms = jnp.sqrt(update_square)
-    trust_ratio = weight_norms / update_norms
-    params_new = params - RATE * product(trust_ratio[None, :], member)[0] * direction
+        goal,
+    )
+    grad_s, grad_v, grad_p, grad, one_new, two_new, par_new, norms = reduce_all(
+        atoms, cap, groups, length
+    )(
+        gpar,
+        g_halo,
+        gp_halo,
+        gs_own,
+        gv_own,
+        gp_own,
+        pick,
+        par_share,
+        padded(first_moment),
+        padded(second_moment),
+    )
+
+    def share(value):
+        return value.reshape(-1)[:length]
+
+    params_new = share(par_new)
     return (
         s_two,
         v_two,
-        grad_scalars,
-        grad_vectors,
-        grad_positions,
-        element_mean,
-        force_scale,
-        grad_shard,
-        moment_one,
-        moment_two,
+        grad_s,
+        grad_v,
+        grad_p[:3],
+        stats[0, :ELEMS],
+        stats[1, 0],
+        share(grad),
+        share(one_new),
+        share(two_new),
         params_new,
         params_new.astype(BF16),
-        weight_norms,
-        update_norms,
+        norms[:GROUPS, 0],
+        norms[8 : 8 + GROUPS, 0],
     )
 
 

time: 487 us -> 201 us (0.41)
  waiting for transfers between devices: 200 us -> 0 us
  blocking collectives: 84.7 us -> 0 us
  Pallas kernels: 113 us -> 180 us
  starting transfers between devices: 43.6 us -> 0 us
  between operations: 17.2 us -> 1.43 us
  other arithmetic: 5.83 us -> 0.61 us
    unnamed x4 -> x0, waiting for transfers between devices: 181 us -> none
    psum x2 -> x0, blocking collectives: 84.7 us -> none  [the longest x1 45 us: body(): lax.psum((elem_total, elem_count, force_square), both)]
    pallas_call x1 -> x3, Pallas kernels: 113 us -> 180 us  [the longest x1 115 us: body(): layer(atoms, halo, edges, 4, 12)]
    ppermute x16 -> x0, starting transfers between devices: 43.5 us -> none  [passed_along(): return lax.ppermute(shard, axis, pairs)]
    ppermute x16 -> x0, waiting for transfers between devices: 18.9 us -> none  [passed_along(): return lax.ppermute(shard, axis, pairs)]
    unnamed x56 -> x46, local copies, waits for them, and re-layouts: 10.7 us -> 15.1 us
  transfers between devices with their start and end apart: 18 -> 0, of which waited for: 6 -> 0; matrix products, arithmetic and copies ran while one was open for 2% -> 0% of each run, Pallas kernels for 0% -> 0%
where the time goes in v2:
time: 201 us; the launch traced here: 200 us
  Pallas kernels  180 us (90%)
  local copies, waits for them, and re-layouts  18.3 us (9%)
    pallas_call x1, Pallas kernels, body(): layer(atoms, halo, edges, 4, 12)  115 us
    pallas_call x1, Pallas kernels, body(): reduce_all(atoms, cap, groups, length)  39.3 us
    pallas_call x1, Pallas kernels, body(): gather_all(atoms, cap, groups, length)  26.1 us
    unnamed x46, local copies, waits for them, and re-layouts  15.1 us

profile of v2, /device:TPU:0, one launch (start us, length us, event | category | flops | bytes accessed | tf_op | source)
XLA Modules:
  0.0 200.4 jit_solution(9149368490369545826)
XLA Ops:
  0.7 0.8 pad_bitcast_fusion.2.par_in.par
  1.5 0.6 copy-done.8
  2.2 1.1 copy-done
  3.3 0.9 copy-done.3
  4.2 26.1 %gather_inputs.1 = (f32[1488,128]{1,0:T(8,128)S(1)}, f32[4,512,128]{2,1,0:T(8,128)S(1)}, f32[8,512]{1,0:T(8,128)S(1)}, f32[1,512]{1,0:T(1,128)S(1)}, f32[8,128]{1,0:T(8,128)S(1)}) custom-call(s32[512]{0:T(512)S(1)} %reshape_reshape.3.send_s, f32[48,128]{1,0:T(8,128)S(1)} %pad_bitcast_fusion.2.par_in.par, f32[512,128]{1,0:T(8,128)S(1)} %copy-done.3, ...), custom_call_target="tpu_custom_call" | custom-call | tf_op jit(solution)/shard_map/gather_inputs/pallas_call | solution.py:1240
  30.3 1.0 copy-done.2
  31.3 0.9 copy-done.6
  32.2 0.6 copy-done.11
  33.4 0.9 copy.33.lat
  34.9 114.7 %layer.1 = (f32[512,128]{1,0:T(8,128)}, f32[3,512,128]{2,1,0:T(8,128)}, f32[512,128]{1,0:T(8,128)}, f32[3,512,128]{2,1,0:T(8,128)}, f32[4,512,128]{2,1,0:T(8,128...) custom-call(s32[8192]{0:T(1024)} %src_s.1, s32[8192]{0:T(1024)} %dst_s.1, s32[1]{0:T(128)S(6)} %copy.39.count_s, ...), custom_call_target="tpu_custom_call" | custom-call | tf_op jit(solution)/shard_map/layer/pallas_call | solution.py:1250
  149.8 0.6 copy-done.9
  150.4 1.2 copy-done.1
  151.6 1.1 copy-done.4
  152.8 1.1 copy-done.5
  153.9 0.9 copy-done.7
  154.8 39.3 %reduce_outputs.1 = (f32[512,128]{1,0:T(8,128)S(1)}, f32[3,512,128]{2,1,0:T(8,128)S(1)}, f32[8,512]{1,0:T(8,128)S(1)}, f32[48,128]{1,0:T(8,128)S(1)}, f32[48,128...) custom-call(f32[1488,128]{1,0:T(8,128)S(1)} %copy-done.5, ...), custom_call_target="tpu_custom_call" | custom-call | tf_op jit(solution)/shard_map/reduce_outputs/pallas_call | solution.py:1268
  194.1 0.6 fusion
  194.7 0.6 slice.27
  195.3 0.7 slice_reduce_fusion
  197.0 0.7 copy.40
  197.7 0.9 copy.41
  198.6 0.6 copy.42
  199.2 0.6 copy.43
  199.8 0.6 copy.44
  (34 shorter events, 1.8 us)
Async XLA Ops:
  0.6 0.8 copy-start.19
  0.7 0.9 copy-start.12
  0.7 0.9 copy-start.13
  0.7 0.9 copy-start.14
  1.5 0.7 copy-start.8
  2.2 1.1 copy-start
  3.3 0.9 copy-start.3
  4.2 29.1 %copy-start.16 = (f32[512,9]{0,1:T(8,128)S(1)}, f32[512,9]{0,1:T(8,128)}, u32[]{:S(2)}) copy-start(f32[512,9]{0,1:T(8,128)} %param.27) | copy-start | bytes 55300
  30.3 1.0 copy-start.2
  31.3 0.9 copy-start.6
  32.2 0.6 copy-start.11
  32.8 0.6 copy-start.15
  34.9 114.8 %copy-start.17 = (f32[5920]{0:T(1024)S(1)}, f32[5920]{0:T(1024)}, u32[]{:S(2)}) copy-start(f32[5920]{0:T(1024)} %param.35) | copy-start | bytes 71044
  34.9 114.8 %copy-start.18 = (f32[5920]{0:T(1024)S(1)}, f32[5920]{0:T(1024)}, u32[]{:S(2)}) copy-start(f32[5920]{0:T(1024)} %param.34) | copy-start | bytes 71044
  149.7 0.7 copy-start.9
  149.7 0.7 copy-start.10
  150.4 1.2 copy-start.1
  151.6 1.1 copy-start.4
  152.8 1.1 copy-start.5
  153.9 0.9 copy-start.7

commit v3 on v2

--- a/solution.py
+++ b/solution.py
@@ -23,6 +23,8 @@
 
 BLOCK = 256
 WINDOW = 128
+PAIR = 2
+LANE_ROWS = 80
 SUB = 32
 ROWS = 256
 F32 = jnp.float32
@@ -75,11 +77,25 @@
     return pl.ds(pl.multiple_of(start, unit), count)
 
 
+def lay_flat(ref, count):
+    return jnp.concatenate([ref[k : k + 1, :] for k in range(count)], axis=1)
+
+
+def weave(*parts):
+    parts = list(parts)
+    while parts:
+        for part in list(parts):
+            try:
+                next(part)
+            except StopIteration:
+                parts.remove(part)
+
+
 def layer_kernel(
-    src_s,
     dst_s,
     count_s,
-    crystal_s,
+    src_s,
+    crystal,
     dst_v,
     shift_v,
     lat,
@@ -103,11 +119,13 @@
     tab,
     rows,
     acc,
-    cells,
+    stage,
     dtab,
-    lrow,
-    drow,
-    misc,
+    lane_buf,
+    slope_buf,
+    inv_buf,
+    free_buf,
+    turn_buf,
     sums,
     gd,
     gbuf,
@@ -122,6 +140,10 @@
 ):
     atoms = s_own.shape[0]
     halo = halo_rows.shape[1]
+    blocks_128 = shift_v.shape[1] // F
+    ends_buf = stage.at[0 : blocks_128 * 16]
+    shift_buf = stage.at[blocks_128 * 16 : blocks_128 * 24]
+    place_buf = stage.at[blocks_128 * 24 : blocks_128 * 32]
     s_halo, v_halo = halo_rows.at[0], halo_rows.at[1:4]
     gs_halo, gv_halo = g_halo.at[0], g_halo.at[1:4]
     edges = shift_v.shape[1]
@@ -149,17 +171,25 @@
         pieces = jnp.concatenate([high, low, jnp.zeros((80, F), F32)], axis=0)
         wq[j * F : (j + 1) * F, :] = jnp.transpose(pieces).astype(BF16)
 
-    @pl.loop(0, atoms // 8)
+    names = lay_flat(crystal, atoms // F)
+    spots = lax.broadcasted_iota(jnp.int32, (F, atoms), 0)
+    for k in range(atoms // F):
+        acc[16 * k : 16 * k + 16, :] = jnp.zeros((16, F), F32)
+
+    @pl.loop(0, lat.shape[1] // F)
     def _(step):
-        for j in range(8):
-            a = step * 8 + j
-            cells[pl.ds(a, 1), 0:9] = lat[pl.ds(crystal_s[a], 1), :]
-
-    across = jnp.transpose(cells[...])
-    blank = jnp.zeros((5, atoms), F32)
-    part = jnp.concatenate(
-        [p_own[...], blank, across[0:3], blank, across[3:6], blank, across[6:9], blank], axis=0
-    )
+        table = lat[:, rows_of(step * F, F, F)]
+        high = table.astype(BF16).astype(F32)
+        middle = (table - high).astype(BF16).astype(F32)
+        gap = jnp.zeros((7, F), F32)
+        pieces = jnp.concatenate([high, gap, middle, gap, table - high - middle, gap], axis=0)
+        got = mm(pieces.astype(BF16), jnp.where(names - step * F == spots, 1.0, 0.0).astype(BF16))
+        got = got[0:16] + got[16:32] + got[32:48]
+        for k in range(atoms // F):
+            acc[16 * k : 16 * k + 16, :] += got[:, k * F : (k + 1) * F]
+
+    across = jnp.concatenate([acc[16 * k : 16 * k + 16, :] for k in range(atoms // F)], axis=1)
+    part = jnp.concatenate([p_own[...], across[0:9], jnp.zeros((4, atoms), F32)], axis=0)
     high = part.astype(BF16).astype(F32)
     middle = (part - high).astype(BF16).astype(F32)
     low = part - high - middle
@@ -185,22 +215,14 @@
                 x = dot3(hidden, split(column(par, AT_W2, 3, j))) + par[AT_B2 + j : AT_B2 + j + 1, :]
                 tab[pl.ds((base + first) * 8 + j, ROWS, stride=8), :] = x
 
-    @pl.loop(0, edges // 32)
-    def _(step):
-        for j in range(32):
-            e = step * 32 + j
-            rows[rows_of(e * 8, 8, 8), :] = tab[rows_of(src_s[e] * 8, 8, 8), :]
-
-    lanes = lax.broadcasted_iota(jnp.int32, (1, BLOCK), 1)
     slots = lax.broadcasted_iota(jnp.int32, (WINDOW, BLOCK), 0)
     eight = lax.broadcasted_iota(jnp.int32, (8, 1), 0)
-    order = lax.broadcasted_iota(jnp.int32, (24, 1), 0)
     wide_lane = lax.broadcasted_iota(jnp.int32, (1, F), 1)
+    chunks = edges // F
+    per = BLOCK // F
 
     def destinations(i):
-        return jnp.concatenate(
-            [dst_v[pl.ds(i * (BLOCK // F) + k, 1), :] for k in range(BLOCK // F)], axis=1
-        )
+        return jnp.concatenate([dst_v[pl.ds(i * per + k, 1), :] for k in range(per)], axis=1)
 
     def window_range(i):
         return dst_s[i * BLOCK] // WINDOW, dst_s[i * BLOCK + BLOCK - 1] // WINDOW
@@ -208,97 +230,174 @@
     def hot(dst, w):
         return jnp.where(dst - w * WINDOW == slots, 1.0, 0.0).astype(BF16)
 
-    def over_windows(first, last, body, start):
-        return lax.fori_loop(first + 1, last + 1, body, body(first, start))
-
-    def lane_pieces(pieces, extra):
-        full = jnp.concatenate(
-            [pieces, pieces[0:24], extra, jnp.zeros((F - 80, BLOCK), F32)], axis=0
+    def window(w):
+        return rows_of(w * WINDOW, WINDOW, WINDOW)
+
+    def lane_chunk(i, k):
+        return rows_of((i * per + k) * LANE_ROWS, LANE_ROWS, LANE_ROWS)
+
+    def source(i, j):
+        return pl.ds(pl.multiple_of(src_s[i * BLOCK + j], 8), 8)
+
+    def ends_in(i, w):
+        got = mm(dtab[:, window(w)], hot(destinations(i), w))
+        return got[0:16] + got[16:32] + got[32:48]
+
+    def gather(i):
+        for j in range(BLOCK):
+            spot = pl.multiple_of(i * (BLOCK * 8), BLOCK * 8) + j * 8
+            rows[pl.ds(pl.multiple_of(spot, 8), 8), :] = tab[source(i, j), :]
+            if j % 16 == 15:
+                yield
+
+    def ends(i):
+        got = ends_in(i, window_range(i)[0])
+        yield
+        for k in range(per):
+            chunk = i * per + k
+            shift_buf[pl.ds(pl.multiple_of(chunk * 8, 8), 3), :] = shift_v[
+                :, rows_of(chunk * F, F, F)
+            ].astype(F32)
+            ends_buf[rows_of(chunk * 16, 16, 16), :] = got[:, k * F : (k + 1) * F]
+            yield
+
+    def places_of(i):
+        for k in range(per):
+            chunk = i * per + k
+            place = rows[pl.ds(chunk * (F * 8) + 6, F, stride=8), :]
+            yield
+            place_buf[rows_of(chunk * 8, 8, 8), :] = jnp.transpose(place)[0:8]
+            yield
+
+    @pl.loop(0, blocks // PAIR)
+    def _(step):
+        for t in range(PAIR):
+            i = step * PAIR + t
+            weave(ends(i), places_of(jnp.maximum(i - 1, 0)), gather(i))
+            first, last = window_range(i)
+
+            @pl.loop(first + 1, last + 1)
+            def _(w):
+                more = ends_in(i, w)
+                for k in range(per):
+                    ends_buf[rows_of((i * per + k) * 16, 16, 16), :] += more[:, k * F : (k + 1) * F]
+
+    weave(places_of(blocks - 1))
+
+    def dense(ref, row, step):
+        return ref[pl.ds(row, chunks, stride=step), :]
+
+    def put_row(row, value):
+        lane_buf[pl.ds(row, chunks, stride=LANE_ROWS), :] = value
+
+    shift = [dense(shift_buf, k, 8) for k in range(3)]
+    rel = [
+        dense(place_buf, c, 8)
+        + (
+            shift[0] * dense(ends_buf, 3 + c, 16)
+            + shift[1] * dense(ends_buf, 6 + c, 16)
+            + shift[2] * dense(ends_buf, 9 + c, 16)
         )
-        return jnp.transpose(full)
+        - dense(ends_buf, c, 16)
+        for c in range(3)
+    ]
+    square = rel[0] * rel[0] + rel[1] * rel[1] + rel[2] * rel[2]
+    dist = jnp.sqrt(jnp.maximum(square, 0.25))
+    inv = 1.0 / dist
+    inv_buf[...] = inv
+    free_buf[...] = jnp.where(square > 0.25, 1.0, 0.0)
+    for c in range(3):
+        put_row(72 + c, rel[c] * inv)
+    put_row(75, dst_v[...].astype(F32))
+    nothing = jnp.zeros((chunks, F), F32)
+    for row in (21, 22, 23, 45, 46, 47, 69, 70, 71, 76, 77, 78, 79):
+        put_row(row, nothing)
+    for row in (21, 22, 23):
+        slope_buf[pl.ds(row, chunks, stride=24), :] = nothing
+    angle = dist * (jnp.pi / CUTOFF)
+    sin_one, cos_one = jnp.sin(angle), jnp.cos(angle)
+    place = lax.broadcasted_iota(jnp.int32, (chunks, F), 0) * F + lax.broadcasted_iota(
+        jnp.int32, (chunks, F), 1
+    )
+    inside = (dist < CUTOFF) & (place < count_s[0])
+    envelope = jnp.where(inside, 0.5 * (cos_one + 1.0), 0.0)
+    fall = jnp.where(inside, (-0.5 * jnp.pi / CUTOFF) * sin_one, 0.0)
+    sin_n, cos_n = sin_one, cos_one
+    for n in range(R + 1):
+        if n < R:
+            radial = sin_n * inv
+            slope = (((n + 1) * jnp.pi / CUTOFF) * cos_n - radial) * inv
+            scaled = envelope * radial
+            change = fall * radial + envelope * slope
+            sin_n, cos_n = sin_n * cos_one + cos_n * sin_one, cos_n * cos_one - sin_n * sin_one
+        else:
+            scaled, change = envelope, fall
+        high = scaled.astype(BF16).astype(F32)
+        put_row(n, high)
+        put_row(24 + n, scaled - high)
+        put_row(48 + n, high)
+        slope_buf[pl.ds(n, chunks, stride=24), :] = change
 
     def comp(i, k, sub):
         return pl.ds(i * (BLOCK * 8) + sub * (SUB * 8) + k, SUB, stride=8)
 
-    @pl.loop(0, blocks)
-    def _(i):
-        here = rows_of(i * BLOCK, BLOCK, BLOCK)
-        first, last = window_range(i)
-        dst = destinations(i)
-        place = jnp.transpose(rows[pl.ds(i * (BLOCK * 8) + 6, BLOCK, stride=8), :])[0:8]
-        ends = over_windows(
-            first,
-            last,
-            lambda w, got: got + mm(dtab[:, rows_of(w * WINDOW, WINDOW, WINDOW)], hot(dst, w)),
-            jnp.zeros((96, BLOCK), F32),
-        )
-        ends = ends[0:32] + ends[32:64] + ends[64:96]
-        shift = shift_v[:, here].astype(F32)
-        rel = (
-            place
-            + (shift[0:1] * ends[8:16] + shift[1:2] * ends[16:24] + shift[2:3] * ends[24:32])
-            - ends[0:8]
-        )
-        square = jnp.sum(rel * rel, axis=0, keepdims=True)
-        dist = jnp.sqrt(jnp.maximum(square, 0.25))
-        inv = 1.0 / dist
-        unit = rel * inv
-        free = jnp.where(square > 0.25, 1.0, 0.0)
-        angle = dist * (jnp.pi / CUTOFF)
-        phase = (eight + 1).astype(F32) * angle
-        sin_a, cos_a = jnp.sin(phase), jnp.cos(phase)
-        sin_8, cos_8 = sin_a[7:8], cos_a[7:8]
-        sin_b = sin_a * cos_8 + cos_a * sin_8
-        cos_b = cos_a * cos_8 - sin_a * sin_8
-        sin_c = sin_b * cos_8 + cos_b * sin_8
-        cos_c = cos_b * cos_8 - sin_b * sin_8
-        sines = jnp.concatenate([sin_a, sin_b, sin_c], axis=0)
-        cosines = jnp.concatenate([cos_a, cos_b, cos_c], axis=0)
-        radial = sines * inv
-        slope = ((order + 1).astype(F32) * (jnp.pi / CUTOFF) * cosines - radial) * inv
-        radial = jnp.where(order < R, radial, jnp.where(order == R, 1.0, 0.0))
-        slope = jnp.where(order < R, slope, 0.0)
-        inside = (dist < CUTOFF) & (i * BLOCK + lanes < count_s[0])
-        envelope = jnp.where(inside, 0.5 * (cos_a[0:1] + 1.0), 0.0)
-        fall = jnp.where(inside, (-0.5 * jnp.pi / CUTOFF) * sin_a[0:1], 0.0)
-        scaled = envelope * radial
-        high = scaled.astype(BF16).astype(F32)
-        pieces = jnp.concatenate([high, scaled - high], axis=0)
-        extra = jnp.where(
-            eight < 3,
-            unit,
-            jnp.where(
-                eight == 3,
-                dst.astype(F32),
-                jnp.where(eight == 4, inv, jnp.where(eight == 5, free, 0.0)),
-            ),
-        )
-        lrow[:, here] = pieces.astype(BF16)
-        drow[:, here] = fall * radial + envelope * slope
-        misc[:, here] = extra
-        ltbuf[...] = lane_pieces(pieces, extra)
-        fbuf[...] = mm(ltbuf[...].astype(BF16), wcat[...])
+    def filters(i, t):
+        for k in range(per):
+            full = jnp.concatenate(
+                [lane_buf[lane_chunk(i, k), :], jnp.zeros((F - LANE_ROWS, F), F32)], axis=0
+            )
+            ltbuf[t, k * F : (k + 1) * F, :] = jnp.transpose(full)
+            yield
+        fbuf[t] = mm(ltbuf[t].astype(BF16), wcat[...])
+        yield
+
+    def messages(i, t):
         for sub in range(BLOCK // SUB):
             at = slice(sub * SUB, (sub + 1) * SUB)
             m1, m2, m3 = [
-                rows[comp(i, j, sub), :] * fbuf[at, j * F : (j + 1) * F] for j in range(3)
+                rows[comp(i, j, sub), :] * fbuf[t, at, j * F : (j + 1) * F] for j in range(3)
             ]
             out = [m1]
             for c in range(3):
-                out.append(m2 * ltbuf[at, 72 + c : 73 + c] + m3 * rows[comp(i, 3 + c, sub), :])
+                out.append(m2 * ltbuf[t, at, 72 + c : 73 + c] + m3 * rows[comp(i, 3 + c, sub), :])
             for k in range(4):
                 high, low = split(out[k])
-                mbuf[at, k * F : (k + 1) * F] = high
-                mbuf[at, (4 + k) * F : (5 + k) * F] = low
-
-        def collect(w, ignored):
-            pick = hot(dst, w)
-            sums[rows_of(w * WINDOW, WINDOW, WINDOW), :] += mm(pick, mbuf[:, : 4 * F]) + mm(
-                pick, mbuf[:, 4 * F :]
+                mbuf[t, at, k * F : (k + 1) * F] = high
+                mbuf[t, at, (4 + k) * F : (5 + k) * F] = low
+            yield
+
+    def collect(i, t, w):
+        pick = hot(destinations(i), w)
+        for k in range(2):
+            of = slice(k * 2 * F, (k + 1) * 2 * F)
+            more = slice((k + 2) * 2 * F, (k + 3) * 2 * F)
+            sums[window(w), of] += mm(pick, mbuf[t, :, of]) + mm(pick, mbuf[t, :, more])
+            yield
+
+    def collect_more(i, t):
+        first, last = window_range(i)
+
+        @pl.loop(first + 1, last + 1)
+        def _(w):
+            weave(collect(i, t, w))
+
+    mbuf[...] = jnp.zeros_like(mbuf)
+    weave(filters(0, 0))
+
+    @pl.loop(0, blocks // PAIR)
+    def _(step):
+        for t in range(PAIR):
+            i = step * PAIR + t
+            before = jnp.maximum(i - 1, 0)
+            weave(
+                filters(jnp.minimum(i + 1, blocks - 1), 1 - t),
+                collect(before, 1 - t, window_range(before)[0]),
+                messages(i, t),
             )
-            return ignored
-
-        over_windows(first, last, collect, 0)
+            collect_more(before, 1 - t)
+
+    weave(collect(blocks - 1, PAIR - 1, window_range(blocks - 1)[0]))
+    collect_more(blocks - 1, PAIR - 1)
 
     @pl.loop(0, atoms // ROWS)
     def _(step):
@@ -368,38 +467,48 @@
                 gd[rows_of(to + WINDOW, WINDOW, WINDOW), k * F : (k + 1) * F] = low[of]
 
     twice = (lax.broadcasted_iota(jnp.int32, (1, 2 * WINDOW), 1) % WINDOW).astype(F32)
-
-    @pl.loop(0, blocks)
-    def _(i):
-        here = rows_of(i * BLOCK, BLOCK, BLOCK)
-        first, last = window_range(i)
-        dst = destinations(i)
-        extra = misc[:, here]
-        ltbuf[...] = lane_pieces(lrow[:, here].astype(F32), extra)
-        fbuf[...] = mm(ltbuf[...].astype(BF16), wcat[...])
-        dst_col = ltbuf[:, 75:76]
-
-        def fetch(w):
-            near = dst_col - (w * WINDOW).astype(F32)
-            return mm(
-                jnp.where(near == twice, 1.0, 0.0).astype(BF16),
-                gd[rows_of(w * 2 * WINDOW, 2 * WINDOW, 2 * WINDOW), :],
-            )
-
-        gbuf[...] = fetch(first)
-
-        @pl.loop(first + 1, last + 1)
-        def _(w):
-            gbuf[...] += fetch(w)
-
+    for ref in (tab, acc, stage, mbuf, tbuf, turn_buf):
+        ref[...] = jnp.zeros_like(ref)
+
+    def collect_places(i, t, w):
+        g_rel = turn_buf[t]
+        high = g_rel.astype(BF16).astype(F32)
+        middle = (g_rel - high).astype(BF16).astype(F32)
+        pieces = jnp.concatenate(
+            [high, middle, g_rel - high - middle, jnp.zeros_like(g_rel)], axis=0
+        )
+        got = mm(pieces.astype(BF16), hot(destinations(i), w), (1, 1))
+        gpd[:, window(w)] += got[0:8] + got[8:16] + got[16:24]
+
+    def fetch(t, w):
+        near = ltbuf[t, :, 75:76] - (w * WINDOW).astype(F32)
+        return mm(
+            jnp.where(near == twice, 1.0, 0.0).astype(BF16),
+            gd[rows_of(w * 2 * WINDOW, 2 * WINDOW, 2 * WINDOW), :],
+        )
+
+    def prepare(i, t):
+        yield from filters(i, t)
+        gbuf[t] = fetch(t, window_range(i)[0])
+        yield
+
+    def spread(i, t, earlier):
         for sub in range(BLOCK // SUB):
             at = slice(sub * SUB, (sub + 1) * SUB)
-            g_s = gbuf[at, 0:F]
-            g_v = [gbuf[at, (c + 1) * F : (c + 2) * F] for c in range(3)]
+            for j in range(SUB // 2):
+                for k, total in enumerate((tab, acc)):
+                    spot = sub * SUB + k * (SUB // 2) + j
+                    held = (t * BLOCK + spot) * 8
+                    total[source(earlier, spot), :] += stage[held : held + 8, :]
+                if j % 8 == 7:
+                    yield
+            to = [pl.ds(t * (BLOCK * 8) + sub * (SUB * 8) + k, SUB, stride=8) for k in range(6)]
+            g_s = gbuf[t, at, 0:F]
+            g_v = [gbuf[t, at, (c + 1) * F : (c + 2) * F] for c in range(3)]
             x = [rows[comp(i, j, sub), :] for j in range(3)]
             v = [rows[comp(i, 3 + c, sub), :] for c in range(3)]
-            f = [fbuf[at, j * F : (j + 1) * F] for j in range(3)]
-            u = [ltbuf[at, 72 + c : 73 + c] for c in range(3)]
+            f = [fbuf[t, at, j * F : (j + 1) * F] for j in range(3)]
+            u = [ltbuf[t, at, 72 + c : 73 + c] for c in range(3)]
             g_m = [
                 g_s,
                 g_v[0] * u[0] + g_v[1] * u[1] + g_v[2] * u[2],
@@ -411,55 +520,88 @@
             for c in range(3):
                 total = jnp.sum(g_v[c] * m2, axis=1, keepdims=True)
                 turn = jnp.where(wide_lane == 48 + c, total, turn)
-                rows[comp(i, 3 + c, sub), :] = g_v[c] * m3
-            tbuf[at, :] = turn
+                stage[to[3 + c], :] = g_v[c] * m3
+            tbuf[t, at, :] = turn
             for j in range(3):
                 high, low = split(g_m[j] * x[j])
-                mbuf[at, j * F : (j + 1) * F] = high
-                mbuf[at, (3 + j) * F : (4 + j) * F] = low
-                rows[comp(i, j, sub), :] = g_m[j] * f[j]
-        h_high, h_low = mbuf[:, : 3 * F], mbuf[:, 3 * F : 6 * F]
-        back = jnp.transpose(mm(h_high, wq[...]) + mm(h_low, wq[...]) + tbuf[...])
-        pieces = lrow[:, here]
+                mbuf[t, at, j * F : (j + 1) * F] = high
+                mbuf[t, at, (3 + j) * F : (4 + j) * F] = low
+                stage[to[j], :] = g_m[j] * f[j]
+            yield
+
+    def settle(i, t):
+        h_high, h_low = mbuf[t, :, : 3 * F], mbuf[t, :, 3 * F : 6 * F]
+        back = mm(h_high, wq[...]) + mm(h_low, wq[...]) + tbuf[t]
+        yield
+        back = jnp.transpose(back)
+        yield
+        pieces = jnp.concatenate(
+            [lane_buf[lane_chunk(i, k), :][0:48] for k in range(per)], axis=1
+        ).astype(BF16)
         gwf[...] += mm(pieces, h_high) + mm(pieces, h_low)
-        g_row = back[0:24] + back[24:48]
+        yield
+        slope = jnp.concatenate(
+            [slope_buf[rows_of((i * per + k) * 24, 24, 24), :] for k in range(per)], axis=1
+        )
+        g_dist = jnp.sum((back[0:24] + back[24:48]) * slope, axis=0, keepdims=True)
         g_unit = back[48:56]
-        unit = jnp.where(eight < 3, extra, 0.0)
-        inv, free = extra[4:5], extra[5:6]
-        g_dist = jnp.sum(g_row * drow[:, here], axis=0, keepdims=True)
+        unit = jnp.concatenate([lane_buf[lane_chunk(i, k), :][72:80] for k in range(per)], axis=1)
+        unit = jnp.where(eight < 3, unit, 0.0)
+        inv, free = [
+            jnp.concatenate([ref[pl.ds(i * per + k, 1), :] for k in range(per)], axis=1)
+            for ref in (inv_buf, free_buf)
+        ]
+        yield
         along = jnp.sum(g_unit * unit, axis=0, keepdims=True)
         g_rel = g_unit * inv + (g_dist - along * inv) * free * unit
-        rows[pl.ds(i * (BLOCK * 8) + 6, BLOCK, stride=8), :] = jnp.transpose(
+        turn_buf[t] = g_rel
+        yield
+        stage[pl.ds(t * (BLOCK * 8) + 6, BLOCK, stride=8), :] = jnp.transpose(
             jnp.concatenate([g_rel, jnp.zeros((F - 8, BLOCK), F32)], axis=0)
         )
-        high = g_rel.astype(BF16).astype(F32)
-        middle = (g_rel - high).astype(BF16).astype(F32)
-        g_pieces = jnp.concatenate([high, middle, g_rel - high - middle, jnp.zeros_like(g_rel)], axis=0)
-        g_pieces = g_pieces.astype(BF16)
-
-        def collect(w, ignored):
-            got = mm(g_pieces, hot(dst, w), (1, 1))
-            gpd[:, rows_of(w * WINDOW, WINDOW, WINDOW)] += got[0:8] + got[8:16] + got[16:24]
-            return ignored
-
-        over_windows(first, last, collect, 0)
+        yield
+        collect_places(i, t, window_range(i)[0])
+        yield
+
+    def prepare_more(i, t):
+        first, last = window_range(i)
+
+        @pl.loop(first + 1, last + 1)
+        def _(w):
+            gbuf[t] += fetch(t, w)
+
+    def settle_more(i, t):
+        first, last = window_range(i)
+
+        @pl.loop(first + 1, last + 1)
+        def _(w):
+            collect_places(i, t, w)
+
+    weave(prepare(0, 0))
+    prepare_more(0, 0)
+
+    @pl.loop(0, blocks // PAIR)
+    def _(step):
+        for t in range(PAIR):
+            i = step * PAIR + t
+            before, after = jnp.maximum(i - 1, 0), jnp.minimum(i + 1, blocks - 1)
+            weave(spread(i, t, jnp.maximum(i - 2, 0)), settle(before, 1 - t), prepare(after, 1 - t))
+            prepare_more(after, 1 - t)
+            settle_more(before, 1 - t)
+
+    weave(settle(blocks - 1, PAIR - 1))
+    settle_more(blocks - 1, PAIR - 1)
+    for t in range(PAIR):
+        for j in range(BLOCK // 2):
+            for k, total in enumerate((tab, acc)):
+                spot = k * (BLOCK // 2) + j
+                held = (t * BLOCK + spot) * 8
+                total[source(blocks - PAIR + t, spot), :] += stage[held : held + 8, :]
 
     for j in range(3):
         total = gwf[0:24, j * F : (j + 1) * F] + gwf[24:48, j * F : (j + 1) * F]
         add_column(gpar, AT_WF, 3, j, total[0:R], R)
         gpar[AT_BF + j : AT_BF + j + 1, :] = total[R : R + 1]
-
-    tab[...] = jnp.zeros_like(tab)
-    acc[...] = jnp.zeros_like(acc)
-    half = edges // 2
-
-    @pl.loop(0, half // 8)
-    def _(step):
-        for j in range(8):
-            for start, total in ((0, tab), (half, acc)):
-                e = start + step * 8 + j
-                to = rows_of(src_s[e] * 8, 8, 8)
-                total[to, :] += rows[rows_of(e * 8, 8, 8), :]
 
     for s_ref, gs_ref, gv_ref, gp_ref, base, count in (
         (s_own, gs_own, gv_own, gp_own, 0, atoms),
@@ -510,7 +652,7 @@
                 gs_ref[to, :] = g_s
 
 
-def layer(atoms, halo, edges, smem, vmem):
+def layer(atoms, halo, edges):
     shape = jax.ShapeDtypeStruct
     total = atoms + halo
     in_vmem = pl.BlockSpec(memory_space=pltpu.VMEM)
@@ -529,18 +671,20 @@
         pltpu.VMEM((total * 8, F), F32),
         pltpu.VMEM((edges * 8, F), F32),
         pltpu.VMEM((total * 8, F), F32),
-        pltpu.VMEM((atoms, F), F32),
-        pltpu.VMEM((96, atoms), BF16),
-        pltpu.VMEM((48, edges), BF16),
-        pltpu.VMEM((24, edges), F32),
-        pltpu.VMEM((8, edges), F32),
+        pltpu.VMEM((PAIR * BLOCK * 8, F), F32),
+        pltpu.VMEM((48, atoms), BF16),
+        pltpu.VMEM((edges // F * LANE_ROWS, F), F32),
+        pltpu.VMEM((edges // F * 24, F), F32),
+        pltpu.VMEM((edges // F, F), F32),
+        pltpu.VMEM((edges // F, F), F32),
+        pltpu.VMEM((PAIR, 8, BLOCK), F32),
         pltpu.VMEM((atoms, 4 * F), F32),
         pltpu.VMEM((2 * atoms, 4 * F), BF16),
-        pltpu.VMEM((BLOCK, 4 * F), F32),
-        pltpu.VMEM((BLOCK, 3 * F), F32),
-        pltpu.VMEM((BLOCK, 8 * F), BF16),
-        pltpu.VMEM((BLOCK, F), F32),
-        pltpu.VMEM((BLOCK, F), F32),
+        pltpu.VMEM((PAIR, BLOCK, 4 * F), F32),
+        pltpu.VMEM((PAIR, BLOCK, 3 * F), F32),
+        pltpu.VMEM((PAIR, BLOCK, 8 * F), BF16),
+        pltpu.VMEM((PAIR, BLOCK, F), F32),
+        pltpu.VMEM((PAIR, BLOCK, F), F32),
         pltpu.VMEM((F, 3 * F), BF16),
         pltpu.VMEM((3 * F, F), BF16),
         pltpu.VMEM((48, 3 * F), F32),
@@ -549,7 +693,7 @@
     return pl.pallas_call(
         layer_kernel,
         out_shape=outs,
-        in_specs=[in_smem] * smem + [in_vmem] * vmem,
+        in_specs=[in_smem] * 3 + [in_vmem] * 13,
         out_specs=(in_vmem,) * len(outs),
         scratch_shapes=scratch,
         compiler_params=pltpu.CompilerParams(vmem_limit_bytes=62 * 1024 * 1024),
@@ -595,11 +739,15 @@
         other = jnp.clip(other, 0, self.count - 1)
         return exists, (other // self.cores, other % self.cores)
 
+    def others_of_group(self):
+        own = self.quarter * self.cores + self.core
+        places = [lax.rem(own + k, 4 * self.cores) for k in range(1, 4 * self.cores)]
+        return [(o, (self.group * 4 + o // self.cores, o % self.cores)) for o in places]
+
     def greet(self):
         barrier = pltpu.get_barrier_semaphore()
         fixed = [self.in_group(g) for g in self.other_groups()]
-        fixed += [self.in_quarter(q) for q in self.other_quarters()]
-        fixed.append(self.beside())
+        fixed += [device for _, device in self.others_of_group()]
         for device in fixed:
             pl.semaphore_signal(barrier, inc=1, device_id=device, device_id_type=MESH)
         hops = [self.hop(hop_offset(j)) for j in range(2 * HOPS)]
@@ -611,7 +759,7 @@
             def _():
                 pl.semaphore_signal(barrier, inc=1, device_id=device, device_id_type=MESH)
 
-        pl.semaphore_wait(barrier, expected)
+        return expected
 
 
 def send(src, dst, send_sem, recv_sem, device):
@@ -641,44 +789,34 @@
 
 
 class SmallSum:
-    def __init__(self, place, slots_a, slots_b, slots_c, sends, recvs):
+    def __init__(self, place, slots_a, slots_b, sends, recvs):
         self.place = place
-        self.slots = (slots_a, slots_b, slots_c)
+        self.slots = (slots_a, slots_b)
         self.sends, self.recvs = sends, recvs
         self.sent = []
 
+    def partners(self, phase):
+        p = self.place
+        if phase == 0:
+            return p.quarter * p.cores + p.core, p.others_of_group(), 0
+        return p.group, [(g, p.in_group(g)) for g in p.other_groups()], 4 * p.cores
+
     def start(self, phase, value):
-        p = self.place
         slots = self.slots[phase]
-        mine = (p.group, p.quarter, p.core)[phase]
+        mine, others, base = self.partners(phase)
         slots[mine] = value
-        base = (0, p.groups, p.groups + 4)[phase]
-        devices = (
-            [p.in_group(g) for g in p.other_groups()],
-            [p.in_quarter(q) for q in p.other_quarters()],
-            [p.beside()],
-        )[phase]
-        for k, device in enumerate(devices):
-            self.sent.append(
-                send(
-                    slots.at[mine],
-                    slots.at[mine],
-                    self.sends.at[base + k],
-                    self.recvs.at[base + mine],
-                    device,
-                )
-            )
-            self.sent[-1].start()
+        for k, (_, device) in enumerate(others):
+            spot = slots.at[mine]
+            copy = send(spot, spot, self.sends.at[base + k], self.recvs.at[base + mine], device)
+            copy.start()
+            self.sent.append(copy)
 
     def finish(self, phase):
-        p = self.place
         slots = self.slots[phase]
-        base = (0, p.groups, p.groups + 4)[phase]
-        others = (p.other_groups(), p.other_quarters(), [p.mate])[phase]
-        for o in others:
-            send(
-                slots.at[o], slots.at[o], self.sends.at[base], self.recvs.at[base + o], p.beside()
-            ).wait_recv()
+        _, others, base = self.partners(phase)
+        for o, device in others:
+            spot = slots.at[o]
+            send(spot, spot, self.sends.at[base], self.recvs.at[base + o], device).wait_recv()
         total = slots[0]
         for k in range(1, slots.shape[0]):
             total = total + slots[k]
@@ -689,18 +827,33 @@
 
 
 def small_scratch(groups, rows):
-    count = groups + 4 + 2
+    count = groups + 8
     return [
+        pltpu.VMEM((8, rows, F), F32),
         pltpu.VMEM((groups, rows, F), F32),
-        pltpu.VMEM((4, rows, F), F32),
-        pltpu.VMEM((2, rows, F), F32),
         pltpu.SemaphoreType.DMA((count,)),
         pltpu.SemaphoreType.DMA((count,)),
     ]
 
 
-def lay_flat(ref, count):
-    return jnp.concatenate([ref[k : k + 1, :] for k in range(count)], axis=1)
+def from_flat(ref, rows):
+    length = ref.shape[0]
+    whole, rest = length // F, length % F
+    lines = [ref[pl.ds(r * F, F)].reshape(1, F) for r in range(whole)]
+    if rest:
+        last = ref[pl.ds(whole * F, rest)].reshape(1, rest)
+        lines.append(jnp.concatenate([last, jnp.zeros((1, F - rest), F32)], axis=1))
+    lines.append(jnp.zeros((rows - len(lines), F), F32))
+    return jnp.concatenate(lines, axis=0)
+
+
+def to_flat(ref, value):
+    length = ref.shape[0]
+    whole, rest = length // F, length % F
+    for r in range(whole):
+        ref[pl.ds(r * F, F)] = value[r]
+    if rest:
+        ref[pl.ds(whole * F, rest)] = value[whole, :rest]
 
 
 def gather_kernel(
@@ -712,11 +865,13 @@
     energy,
     elements,
     forces,
+    edge_src,
     par,
     halo_rows,
     p_halo,
     goal,
     stats,
+    src_tiles,
     slots,
     pack,
     places,
@@ -737,21 +892,16 @@
     atoms = s_own.shape[0]
     cap = halo_rows.shape[1] // (2 * HOPS)
     wide = slots.shape[3]
-    here.greet()
+    expected = here.greet()
     sums = SmallSum(here, *small)
 
     offset = lax.rem(here.joint * length, F)
     lane = lax.broadcasted_iota(jnp.int32, (1, F), 1)
-    turned = pltpu.roll(par_in[...], offset, 1)
+    turned = pltpu.roll(from_flat(par_in, wide), offset, 1)
     above = jnp.concatenate([jnp.zeros((1, F), F32), turned[: wide - 1]], axis=0)
     mine = slots.at[here.group, here.quarter, here.core]
     mine[...] = jnp.where(lane < offset, above, turned)
-    first = start_all(
-        [
-            send(mine, mine, ag_send.at[k], ag_recv.at[here.group], here.in_group(g))
-            for k, g in enumerate(here.other_groups())
-        ]
-    )
+    src_tiles[...] = edge_src[...] * 8
 
     count = atoms // F
     energy_row, element_row = lay_flat(energy, count), lay_flat(elements, count)
@@ -778,50 +928,53 @@
         found[0:1] + found[1:2] + found[2:3],
         jnp.where(eight == 1, found[3:4], jnp.where(eight == 2, square, 0.0)),
     )
-    sums.start(0, tile)
-
     places[...] = jnp.transpose(
         jnp.concatenate([p_own[...], jnp.zeros((F - 3, atoms), F32)], axis=0)
     )
     zeros[...] = jnp.zeros_like(zeros)
     hops = range(2 * HOPS)
+    for j in hops:
+
+        @pl.loop(0, cap // 16)
+        def _(step):
+            for k in range(16):
+                r = step * 16 + k
+                t = send_s[0, j, r]
+                r = j * cap + r
+                pack[0, pl.ds(r, 1), :] = s_own[pl.ds(t, 1), :]
+                for c in range(3):
+                    pack[1 + c, pl.ds(r, 1), :] = v_own[c, pl.ds(t, 1), :]
+                p_out[pl.ds(r, 1), :] = places[pl.ds(t, 1), :]
+
+    for j in range(0, 2 * HOPS, 2):
+        pair = slice(j * cap, (j + 2) * cap)
+        p_in[2 * HOPS + j // 2] = jnp.transpose(p_out[pair, :])[0:8]
+
+    pl.semaphore_wait(pltpu.get_barrier_semaphore(), expected)
+    first = start_all(
+        [
+            send(mine, mine, ag_send.at[k], ag_recv.at[here.group], here.in_group(g))
+            for k, g in enumerate(here.other_groups())
+        ]
+    )
+    sums.start(0, tile)
     row_copies, place_copies = [], []
     for j in hops:
         exists, device = here.hop(hop_offset(j))
         block = pl.ds(j * cap, cap)
-
-        @pl.loop(0, cap // 8)
-        def _(step):
-            for k in range(8):
-                r = j * cap + step * 8 + k
-                t = send_s[r]
-                pack[0, pl.ds(r, 1), :] = s_own[pl.ds(t, 1), :]
-                for c in range(3):
-                    pack[1 + c, pl.ds(r, 1), :] = v_own[c, pl.ds(t, 1), :]
-                p_out[pl.ds(r, 1), :] = places[pl.ds(t, 1), :]
-
-        copy = send(
+        rows_copy = send(
             pack.at[:, block], halo_rows.at[:, block], row_send.at[j], row_recv.at[j], device
         )
-        row_copies.append((exists, copy))
+        place_copy = send(
+            p_in.at[2 * HOPS + j // 2], p_in.at[j], place_send.at[j], place_recv.at[j], device
+        )
+        row_copies.append((exists, rows_copy))
+        place_copies.append((exists, place_copy))
 
         @pl.when(exists)
         def _():
-            copy.start()
-
-    for j in range(0, 2 * HOPS, 2):
-        pair = slice(j * cap, (j + 2) * cap)
-        p_in[2 * HOPS + j // 2] = jnp.transpose(p_out[pair, :])[0:8]
-        for k in (j, j + 1):
-            exists, device = here.hop(hop_offset(k))
-            copy = send(
-                p_in.at[2 * HOPS + j // 2], p_in.at[k], place_send.at[k], place_recv.at[k], device
-            )
-            place_copies.append((exists, copy))
-
-            @pl.when(exists)
-            def _():
-                copy.start()
+            rows_copy.start()
+            place_copy.start()
 
     for j in hops:
         known, device = here.hop(-hop_offset(j))
@@ -861,7 +1014,6 @@
         )
         copy.start()
         third.append(copy)
-    sums.start(2, sums.finish(1))
     for q in range(4):
         line = slots.at[:, q, here.mate]
         send(line, line, ag_send.at[0], ag_recv.at[base + 4 + q], here.beside()).wait_recv()
@@ -873,7 +1025,7 @@
         take = min(wide, PARAM_PAD - row)
         par[row : row + take, :] += slots[chip // 4, chip % 4, core, 0:take, :]
 
-    total = sums.finish(2)
+    total = sums.finish(1)
     mean = total[0:1] / jnp.maximum(total[1:2], 1.0)
     whole = jnp.sum(total[2:3], axis=1, keepdims=True)
     scale = jnp.sqrt(whole / (3.0 * atoms * here.count) + 1e-06)
@@ -912,7 +1064,7 @@
     sums.done()
 
 
-def gather_all(atoms, cap, groups, length):
+def gather_all(atoms, cap, groups, length, edges):
     shape = jax.ShapeDtypeStruct
     halo = 2 * HOPS * cap
     wide = window_rows(length)
@@ -926,9 +1078,10 @@
             shape((8, halo), F32),
             shape((1, atoms), F32),
             shape((8, F), F32),
+            shape((edges // F, F), jnp.int32),
         ),
-        in_specs=[in_smem] + [in_vmem] * 7,
-        out_specs=(in_vmem, pl.BlockSpec(memory_space=pl.ANY), in_vmem, in_vmem, in_vmem),
+        in_specs=[in_smem] + [in_vmem] * 8,
+        out_specs=(in_vmem, pl.BlockSpec(memory_space=pl.ANY)) + (in_vmem,) * 4,
         scratch_shapes=[
             pltpu.VMEM((groups, 4, 2, wide, F), F32),
             pltpu.VMEM((4, halo, F), F32),
@@ -946,7 +1099,7 @@
         ]
         + small_scratch(groups, 8),
         compiler_params=pltpu.CompilerParams(
-            collective_id=0, has_side_effects=True, vmem_limit_bytes=40 * 1024 * 1024
+            collective_id=0, has_side_effects=True, vmem_limit_bytes=62 * 1024 * 1024
         ),
         name="gather_inputs",
     )
@@ -956,42 +1109,34 @@
     gpar,
     g_halo,
     gp_halo,
-    gs_own,
-    gv_own,
-    gp_own,
-    pick,
     par,
     one,
     two,
-    grad_s,
-    grad_v,
-    grad_p,
-    grad,
-    one_new,
-    two_new,
-    par_new,
+    back,
+    p_back,
+    shares,
     norms,
     slots,
     pair_in,
     line_in,
     spot_in,
-    back,
-    p_back,
     turn,
+    zeros,
+    p_in,
     rs_send,
     rs_recv,
     row_send,
     row_recv,
     place_send,
     place_recv,
+    zero_sem,
     *small,
     length,
 ):
     here = Place()
-    atoms = gs_own.shape[0]
     cap = back.shape[1] // (2 * HOPS)
     wide = slots.shape[3]
-    here.greet()
+    expected = here.greet()
     sums = SmallSum(here, *small)
 
     for p in range(here.count):
@@ -999,8 +1144,11 @@
         chip, core = p // here.cores, p % here.cores
         take = min(wide, PARAM_PAD - row)
         slots[chip // 4, chip % 4, core, 0:take, :] = gpar[row : row + take, :]
+    old, m_one, m_two = [from_flat(ref, wide) for ref in (par, one, two)]
+    zeros[...] = jnp.zeros_like(zeros)
     order = here.other_quarters() + [here.quarter]
     base = here.groups
+    pl.semaphore_wait(pltpu.get_barrier_semaphore(), expected)
     third = start_all(
         [
             send(
@@ -1013,32 +1161,6 @@
             for k, q in enumerate(order)
         ]
     )
-
-    hops = range(2 * HOPS)
-    copies = []
-    for j in hops:
-        exists, device = here.hop(-hop_offset(j))
-        block = pl.ds(j * cap, cap)
-        tile = pl.ds((j // 2) * F, F)
-        rows_copy = send(
-            g_halo.at[:, block], back.at[:, block], row_send.at[j], row_recv.at[j], device
-        )
-        place_copy = send(
-            gp_halo.at[:, tile], p_back.at[j], place_send.at[j], place_recv.at[j], device
-        )
-        copies += [(exists, rows_copy), (exists, place_copy)]
-
-        @pl.when(exists)
-        def _():
-            rows_copy.start()
-            place_copy.start()
-
-        known, device = here.hop(hop_offset(j))
-
-        @pl.when(jnp.logical_not(known))
-        def _():
-            back[:, block, :] = jnp.zeros((4, cap, F), F32)
-            p_back[j] = jnp.zeros((8, F), F32)
 
     second = []
     for k, q in enumerate(order):
@@ -1055,6 +1177,36 @@
             )
             copy.start()
             second.append(copy)
+
+    hops = range(2 * HOPS)
+    copies = []
+    for j in hops:
+        exists, device = here.hop(-hop_offset(j))
+        block = pl.ds(j * cap, cap)
+        tile = pl.ds((j // 2) * F, F)
+        rows_copy = send(
+            g_halo.at[:, block], back.at[:, block], row_send.at[j], row_recv.at[j], device
+        )
+        place_copy = send(
+            gp_halo.at[:, tile], p_in.at[j], place_send.at[j], place_recv.at[j], device
+        )
+        copies += [(exists, rows_copy), (exists, place_copy)]
+
+        @pl.when(exists)
+        def _():
+            rows_copy.start()
+            place_copy.start()
+
+    for j in hops:
+        known, device = here.hop(hop_offset(j))
+
+        @pl.when(jnp.logical_not(known))
+        def _():
+            p_in[j] = jnp.zeros((8, F), F32)
+            fill = pltpu.make_async_copy(zeros, back.at[:, pl.ds(j * cap, cap)], zero_sem.at[j])
+            fill.start()
+            fill.wait()
+
     for q in here.other_quarters():
         line = line_in.at[q]
         send(line, line, rs_send.at[0], rs_recv.at[base + q], here.beside()).wait_recv()
@@ -1085,16 +1237,16 @@
     inside = place < length
     g = jnp.where(lane + offset < F, turn[0:wide, :], turn[1 : wide + 1, :])
     g = jnp.where(inside, g, 0.0)
-    grad[...] = g
-    m_one = BETA_ONE * one[...] + (1.0 - BETA_ONE) * g
-    m_two = BETA_TWO * two[...] + (1.0 - BETA_TWO) * g * g
-    one_new[...] = m_one
-    two_new[...] = m_two
+    shares[0] = g
+    m_one = BETA_ONE * m_one + (1.0 - BETA_ONE) * g
+    m_two = BETA_TWO * m_two + (1.0 - BETA_TWO) * g * g
+    shares[1] = m_one
+    shares[2] = m_two
     direction = (
         m_one
         / (1.0 - BETA_ONE**STEP)
         / (jnp.sqrt(m_two / (1.0 - BETA_TWO**STEP)) + EPSILON)
-        + DECAY * par[...]
+        + DECAY * old
     )
     spot = place + here.joint * length
     label = jnp.zeros((wide, F), jnp.int32)
@@ -1102,7 +1254,7 @@
         label = label + jnp.where(spot >= end * F, 1, 0)
     label = jnp.where(inside, label, GROUPS)
     lines = []
-    for value in (par[...], direction):
+    for value in (old, direction):
         square = value * value
         lines += [
             jnp.sum(jnp.where(label == k, square, 0.0), axis=0, keepdims=True)
@@ -1110,52 +1262,30 @@
         ]
         lines.append(jnp.zeros((1, F), F32))
     sums.start(0, jnp.concatenate(lines, axis=0))
-
-    hot = jnp.where(
-        pick[...] == lax.broadcasted_iota(jnp.int32, (atoms, 2 * HOPS * cap), 0), 1.0, 0.0
-    ).astype(BF16)
-    for j in hops:
-        known, device = here.hop(hop_offset(j))
-
-        @pl.when(known)
-        def _():
-            block = pl.ds(j * cap, cap)
-            tile = p_back.at[j]
-            send(
-                back.at[:, block], back.at[:, block], row_send.at[j], row_recv.at[j], device
-            ).wait_recv()
-            send(tile, tile, place_send.at[j], place_recv.at[j], device).wait_recv()
-
     sums.start(1, sums.finish(0))
-    for k in range(2):
-        high, low = split(back[k])
-        extra = mm(hot, high) + mm(hot, low)
-        if k == 0:
-            grad_s[...] = gs_own[...] + extra
-        else:
-            grad_v[k - 1] = gv_own[k - 1] + extra
-    sums.start(2, sums.finish(1))
-    for k in range(2, 4):
-        high, low = split(back[k])
-        grad_v[k - 1] = gv_own[k - 1] + (mm(hot, high) + mm(hot, low))
-    low_half = lane < cap
-    place = jnp.concatenate(
-        [jnp.where(low_half, p_back[j], p_back[j + 1]) for j in range(0, 2 * HOPS, 2)], axis=1
-    )
-    high = place.astype(BF16).astype(F32)
-    middle = (place - high).astype(BF16).astype(F32)
-    pieces = jnp.concatenate([high, middle, place - high - middle, jnp.zeros_like(place)], axis=0)
-    got = mm(pieces.astype(BF16), hot, (1, 1))
-    grad_p[...] = gp_own[...] + (got[0:8] + got[8:16] + got[16:24])
-
-    whole = jnp.sqrt(jnp.sum(sums.finish(2), axis=1, keepdims=True))
+    whole = jnp.sqrt(jnp.sum(sums.finish(1), axis=1, keepdims=True))
     ratio = whole[0:8] / whole[8:16]
     norms[...] = jnp.broadcast_to(whole, (16, F))
     trust = jnp.zeros((wide, F), F32)
     for k in range(GROUPS):
         trust = jnp.where(label == k, ratio[k : k + 1], trust)
-    par_new[...] = par[...] - RATE * trust * direction
-
+    shares[3] = old - RATE * trust * direction
+
+    for j in hops:
+        known, device = here.hop(hop_offset(j))
+
+        @pl.when(known)
+        def _():
+            block = pl.ds(j * cap, cap)
+            tile = p_in.at[j]
+            send(
+                back.at[:, block], back.at[:, block], row_send.at[j], row_recv.at[j], device
+            ).wait_recv()
+            send(tile, tile, place_send.at[j], place_recv.at[j], device).wait_recv()
+
+    low_half = lane < cap
+    for j in range(0, 2 * HOPS, 2):
+        p_back[:, j * cap : (j + 2) * cap] = jnp.where(low_half, p_in[j], p_in[j + 1])
     for exists, copy in copies:
 
         @pl.when(exists)
@@ -1166,31 +1296,33 @@
     sums.done()
 
 
-def reduce_all(atoms, cap, groups, length):
+def reduce_all(cap, groups, length):
     shape = jax.ShapeDtypeStruct
     halo = 2 * HOPS * cap
     wide = window_rows(length)
     in_vmem = pl.BlockSpec(memory_space=pltpu.VMEM)
-    outs = (
-        [shape((atoms, F), F32), shape((3, atoms, F), F32), shape((8, atoms), F32)]
-        + [shape((wide, F), F32)] * 4
-        + [shape((16, F), F32)]
-    )
+    in_any = pl.BlockSpec(memory_space=pl.ANY)
     return pl.pallas_call(
         functools.partial(reduce_kernel, length=length),
-        out_shape=tuple(outs),
-        in_specs=[in_vmem] * 10,
-        out_specs=(in_vmem,) * len(outs),
+        out_shape=(
+            shape((4, halo, F), F32),
+            shape((8, halo), F32),
+            shape((4, wide, F), F32),
+            shape((16, F), F32),
+        ),
+        in_specs=[in_vmem, in_any] + [in_vmem] * 4,
+        out_specs=(in_any, in_vmem, in_vmem, in_vmem),
         scratch_shapes=[
             pltpu.VMEM((groups, 4, 2, wide, F), F32),
             pltpu.VMEM((groups, 4, wide, F), F32),
             pltpu.VMEM((4, groups, wide, F), F32),
             pltpu.VMEM((groups, wide, F), F32),
-            pltpu.VMEM((4, halo, F), F32),
+            pltpu.VMEM((wide + 8, F), F32),
+            pltpu.VMEM((4, cap, F), F32),
             pltpu.VMEM((2 * HOPS, 8, F), F32),
-            pltpu.VMEM((wide + 8, F), F32),
             pltpu.SemaphoreType.DMA((groups + 8,)),
             pltpu.SemaphoreType.DMA((groups + 8,)),
+            pltpu.SemaphoreType.DMA((2 * HOPS,)),
             pltpu.SemaphoreType.DMA((2 * HOPS,)),
             pltpu.SemaphoreType.DMA((2 * HOPS,)),
             pltpu.SemaphoreType.DMA((2 * HOPS,)),
@@ -1198,9 +1330,83 @@
         ]
         + small_scratch(groups, 16),
         compiler_params=pltpu.CompilerParams(
-            collective_id=1, has_side_effects=True, vmem_limit_bytes=40 * 1024 * 1024
+            collective_id=1, has_side_effects=True, vmem_limit_bytes=62 * 1024 * 1024
         ),
         name="reduce_outputs",
+    )
+
+
+def finish_kernel(
+    back,
+    p_back,
+    shares,
+    norms,
+    stats,
+    send_rows,
+    gs_own,
+    gv_own,
+    gp_own,
+    grad_s,
+    grad_v,
+    grad_p,
+    elem_mean,
+    scale,
+    grad,
+    one_new,
+    two_new,
+    par_new,
+    par_low,
+    weight_norms,
+    update_norms,
+):
+    atoms = gs_own.shape[0]
+    halo = back.shape[1]
+    pick = jnp.concatenate([send_rows[0, j : j + 1, :] for j in range(2 * HOPS)], axis=1)
+    hot = jnp.where(pick == lax.broadcasted_iota(jnp.int32, (atoms, halo), 0), 1.0, 0.0)
+    hot = hot.astype(BF16)
+    for k in range(4):
+        high, low = split(back[k])
+        extra = mm(hot, high) + mm(hot, low)
+        if k == 0:
+            grad_s[...] = gs_own[...] + extra
+        else:
+            grad_v[k - 1] = gv_own[k - 1] + extra
+    place = p_back[...]
+    high = place.astype(BF16).astype(F32)
+    middle = (place - high).astype(BF16).astype(F32)
+    pieces = jnp.concatenate([high, middle, place - high - middle, jnp.zeros_like(place)], axis=0)
+    got = mm(pieces.astype(BF16), hot, (1, 1))
+    grad_p[...] = (gp_own[...] + (got[0:8] + got[8:16] + got[16:24]))[0:3]
+    for k, ref in enumerate((grad, one_new, two_new, par_new)):
+        to_flat(ref, shares[k])
+    to_flat(par_low, shares[3].astype(BF16))
+    rows = lax.broadcasted_iota(jnp.int32, (8, F), 0)
+    lanes = lax.broadcasted_iota(jnp.int32, (8, F), 1)
+    for k, ref in enumerate((weight_norms, update_norms)):
+        line = jnp.sum(
+            jnp.where(rows == lanes, norms[8 * k : 8 * k + 8, :], 0.0), axis=0, keepdims=True
+        )
+        ref[...] = line[0, :GROUPS]
+    elem_mean[...] = stats[0, :ELEMS]
+    scale[...] = stats[1, :1]
+
+
+def finish(atoms, length):
+    shape = jax.ShapeDtypeStruct
+    in_vmem = pl.BlockSpec(memory_space=pltpu.VMEM)
+    outs = (
+        [shape((atoms, F), F32), shape((3, atoms, F), F32), shape((3, atoms), F32)]
+        + [shape((ELEMS,), F32), shape((1,), F32)]
+        + [shape((length,), F32)] * 4
+        + [shape((length,), BF16), shape((GROUPS,), F32), shape((GROUPS,), F32)]
+    )
+    return pl.pallas_call(
+        finish_kernel,
+        out_shape=tuple(outs),
+        in_specs=[in_vmem] * 9,
+        out_specs=(in_vmem,) * len(outs),
+        compiler_params=pltpu.CompilerParams(vmem_limit_bytes=62 * 1024 * 1024),
+        name="finish",
     )
 
 
@@ -1230,31 +1436,25 @@
     halo = 2 * HOPS * cap
     groups = lax.axis_size("atoms") // 4
     length = params.shape[0]
-    wide = window_rows(length)
-
-    def padded(value):
-        return jnp.pad(value, (0, wide * F - length)).reshape(wide, F)
-
-    par_share = padded(params)
-    pick = send_rows.reshape(1, halo)
-    par, halo_rows, p_halo, goal, stats = gather_all(atoms, cap, groups, length)(
-        pick.reshape(-1),
-        par_share,
+    par, halo_rows, p_halo, goal, stats, src_tiles = gather_all(atoms, cap, groups, length, edges)(
+        send_rows,
+        params,
         scalars_in,
         vectors_in,
         positions,
         target_energy.reshape(-1, F),
         elements.reshape(-1, F),
         forces,
-    )
-    s_two, v_two, gs_own, gv_own, g_halo, gp_own, gp_halo, gpar = layer(atoms, halo, edges, 4, 12)(
-        edge_src,
+        edge_src.reshape(-1, F),
+    )
+    s_two, v_two, gs_own, gv_own, g_halo, gp_own, gp_halo, gpar = layer(atoms, halo, edges)(
         edge_dst,
         edge_count,
-        crystal,
+        src_tiles.reshape(-1),
+        crystal.reshape(-1, F),
         edge_dst.reshape(-1, F),
         edge_shift,
-        lattice,
+        jnp.transpose(lattice),
         par,
         scalars_in,
         vectors_in,
@@ -1265,40 +1465,40 @@
         cotan_vector,
         goal,
     )
-    grad_s, grad_v, grad_p, grad, one_new, two_new, par_new, norms = reduce_all(
-        atoms, cap, groups, length
-    )(
-        gpar,
-        g_halo,
-        gp_halo,
-        gs_own,
-        gv_own,
-        gp_own,
-        pick,
-        par_share,
-        padded(first_moment),
-        padded(second_moment),
-    )
-
-    def share(value):
-        return value.reshape(-1)[:length]
-
-    params_new = share(par_new)
+    back, p_back, shares, norms = reduce_all(cap, groups, length)(
+        gpar, g_halo, gp_halo, params, first_moment, second_moment
+    )
+    (
+        grad_s,
+        grad_v,
+        grad_p,
+        elem_mean,
+        scale,
+        grad,
+        one_new,
+        two_new,
+        par_new,
+        par_low,
+        weight_norms,
+        update_norms,
+    ) = finish(atoms, length)(
+        back, p_back, shares, norms, stats, send_rows, gs_own, gv_own, gp_own
+    )
     return (
         s_two,
         v_two,
         grad_s,
         grad_v,
-        grad_p[:3],
-        stats[0, :ELEMS],
-        stats[1, 0],
-        share(grad),
-        share(one_new),
-        share(two_new),
-        params_new,
-        params_new.astype(BF16),
-        norms[:GROUPS, 0],
-        norms[8 : 8 + GROUPS, 0],
+        grad_p,
+        elem_mean,
+        scale.reshape(()),
+        grad,
+        one_new,
+        two_new,
+        par_new,
+        par_low,
+        weight_norms,
+        update_norms,
     )
 
 

time: 201 us -> 146 us (0.73)
  Pallas kernels: 180 us -> 144 us
  local copies, waits for them, and re-layouts: 18.3 us -> 0 us
    pallas_call x3 -> x4, Pallas kernels: 180 us -> 144 us  [the longest x1 75.5 us: body(): layer(atoms, halo, edges)]
    unnamed x46 -> x0, local copies, waits for them, and re-layouts: 15.1 us -> none
where the time goes in v3:
time: 146 us
  Pallas kernels  144 us (99%)
  between operations  1.46 us (1%)
    pallas_call x1, Pallas kernels, body(): layer(atoms, halo, edges)  75.5 us
    pallas_call x1, Pallas kernels, body(): reduce_all(cap, groups, length)  36.8 us
    pallas_call x1, Pallas kernels, body(): gather_all(atoms, cap, groups, length, edges)  28.2 us
    pallas_call x1, Pallas kernels, body(): finish(atoms, length)  3.92 us

profile of v3, /device:TPU:0, one launch (start us, length us, event | category | flops | bytes accessed | tf_op | source)
XLA Modules:
  0.0 145.9 jit_solution(9015241982945733202)
XLA Ops:
  1.3 28.2 %gather_inputs.1 = (f32[1488,128]{1,0:T(8,128)}, f32[4,512,128]{2,1,0:T(8,128)}, f32[8,512]{1,0:T(8,128)}, f32[1,512]{1,0:T(1,128)}, f32[8,128]{1,0:T(8,128)}, /*index=5*/s32[64,128]{1,0:T(8,128)}) custom-call(s32[1,8,64]{2,1,0:T(8,128)} %send_rows.1, f32[5920]{0:T(1024)} %par.1, f32[512,128]{1,0:T(8,128)} %s_own.3, f32[3,512,128]{2,1,0:T(8,128)} %v_own.3, ...), custom_call_target="tpu_custom_call" | custom-call | tf_op jit(solution)/shard_map/gather_inputs/pallas_call | solution.py:1439
  29.5 75.5 %layer.1 = (f32[512,128]{1,0:T(8,128)}, f32[3,512,128]{2,1,0:T(8,128)}, f32[512,128]{1,0:T(8,128)}, f32[3,512,128]{2,1,0:T(8,128)}, f32[4,512,128]{2,1,0:T(8,128...) custom-call(s32[8192]{0:T(1024)} %dst_s.1, s32[1]{0:T(128)S(6)} %copy.32.count_s, s32[8192]{0:T(1024)} %bitcast.10, ...), custom_call_target="tpu_custom_call" | custom-call | tf_op jit(solution)/shard_map/layer/pallas_call | solution.py:1450
  105.1 36.8 %reduce_outputs.1 = (f32[4,512,128]{2,1,0:T(8,128)}, f32[8,512]{1,0:T(8,128)}, f32[4,48,128]{2,1,0:T(8,128)}, f32[16,128]{1,0:T(8,128)}) custom-call(f32[1488,128]{1,0:T(8,128)} %get-tuple-element.51.gpar, f32[4,512,128]{2,1,0:T(8,128)} %get-tuple-element.52.g_halo, f32[8,512]{1,0:T(8,128)} %get-tuple-element.53.gp_halo, f32[5920]{0:T(1024)} %par.1, ...), custom_call_target="tpu_custom_call" | custom-call | tf_op jit(solution)/shard_map/reduce_outputs/pallas_call | solution.py:1468
  141.9 3.9 %finish.1 = (f32[512,128]{1,0:T(8,128)}, f32[3,512,128]{2,1,0:T(8,128)}, f32[3,512]{1,0:T(4,128)}, f32[100]{0:T(128)}, f32[1]{0:T(128)}, /*index=5*/f32[5920]{0:...) custom-call(f32[4,512,128]{2,1,0:T(8,128)} %get-tuple-element.54.bac, ...), custom_call_target="tpu_custom_call" | custom-call | tf_op jit(solution)/shard_map/finish/pallas_call | solution.py:1484

commit v4 on v3

--- a/solution.py
+++ b/solution.py
@@ -25,7 +25,7 @@
 WINDOW = 128
 PAIR = 2
 LANE_ROWS = 80
-SUB = 32
+SUB = 16
 ROWS = 256
 F32 = jnp.float32
 BF16 = jnp.bfloat16
@@ -35,6 +35,7 @@
 PARAM_PAD = PARAM_ROWS + 8
 GROUP_ENDS = (128, 512, 572, 828, 1084, 1468)
 MESH = pl.DeviceIdType.MESH
+BATCHES = ((3, 7), (2, 6), (1, 5), (0, 4))
 
 
 def mm(left, right, contract=(1, 0)):
@@ -54,6 +55,30 @@
         + mm(left[1], right[0], contract)
         + mm(left[0], right[1], contract)
     )
+
+
+def linear(pair, weights):
+    both = jnp.concatenate(pair, axis=1)
+    return mm(both, weights[0 : 2 * F, :]) + mm(pair[0], weights[2 * F : 3 * F, :])
+
+
+def back_through(pair, weights):
+    return dot3(pair, (weights[0:F, :], weights[2 * F : 3 * F, :]), (1, 1))
+
+
+def wide_row(ref, start, parts):
+    return jnp.concatenate([ref[start + j : start + j + 1, :] for j in range(parts)], axis=1)
+
+
+def add_row(ref, start, parts, value):
+    total = jnp.sum(value, axis=0, keepdims=True)
+    for j in range(parts):
+        ref[start + j : start + j + 1, :] += total[:, j * F : (j + 1) * F]
+
+
+def add_matrix(ref, start, parts, value):
+    for j in range(parts):
+        add_column(ref, start, parts, j, value[:, j * F : (j + 1) * F], value.shape[0])
 
 
 def sigmoid(value):
@@ -137,6 +162,11 @@
     wq,
     gwf,
     gpd,
+    w1,
+    w2,
+    wm,
+    u1,
+    u2,
 ):
     atoms = s_own.shape[0]
     halo = halo_rows.shape[1]
@@ -155,6 +185,12 @@
     gpd[...] = jnp.zeros_like(gpd)
     gpar[...] = jnp.zeros_like(gpar)
     sums[...] = jnp.zeros_like(sums)
+    for ref, start, parts in ((w1, AT_W1, 1), (w2, AT_W2, 3), (wm, AT_WM, 2), (u2, AT_U2, 3)):
+        for j in range(parts):
+            high, low = split(column(par, start, parts, j))
+            for k, value in enumerate((high, high, low)):
+                ref[k * F : (k + 1) * F, j * F : (j + 1) * F] = value
+    u1[0 : 2 * F, :], u1[2 * F : 4 * F, :] = split(par[AT_U1 : AT_U1 + 2 * F, :])
     for j in range(3):
         wide = jnp.concatenate(
             [
@@ -209,11 +245,10 @@
         def _(step):
             first = step * ROWS
             s_pair = split(s_ref[rows_of(first, ROWS, ROWS), :])
-            act = dot3(s_pair, split(column(par, AT_W1, 1, 0))) + par[AT_B1 : AT_B1 + 1, :]
-            hidden = split(act * sigmoid(act))
+            act = linear(s_pair, w1) + par[AT_B1 : AT_B1 + 1, :]
+            x = linear(split(act * sigmoid(act)), w2) + wide_row(par, AT_B2, 3)
             for j in range(3):
-                x = dot3(hidden, split(column(par, AT_W2, 3, j))) + par[AT_B2 + j : AT_B2 + j + 1, :]
-                tab[pl.ds((base + first) * 8 + j, ROWS, stride=8), :] = x
+                tab[pl.ds((base + first) * 8 + j, ROWS, stride=8), :] = x[:, j * F : (j + 1) * F]
 
     slots = lax.broadcasted_iota(jnp.int32, (WINDOW, BLOCK), 0)
     eight = lax.broadcasted_iota(jnp.int32, (8, 1), 0)
@@ -404,18 +439,18 @@
         at = rows_of(step * ROWS, ROWS, ROWS)
         s_one = s_own[at, :] + sums[at, 0:F]
         v_one = [v_own[c, at, :] + sums[at, (c + 1) * F : (c + 2) * F] for c in range(3)]
-        wm = [split(column(par, AT_WM, 2, j)) for j in range(2)]
-        u1 = [split(par[AT_U1 + j * F : AT_U1 + (j + 1) * F, :]) for j in range(2)]
-        u2 = [split(column(par, AT_U2, 3, j)) for j in range(3)]
         v_pair = [split(v) for v in v_one]
-        v_lin = [dot3(v, wm[0]) for v in v_pair]
-        w_lin = [dot3(v, wm[1]) for v in v_pair]
+        mixed = [linear(v, wm) for v in v_pair]
+        v_lin = [m[:, :F] for m in mixed]
+        w_lin = [m[:, F:] for m in mixed]
         size = jnp.sqrt(v_lin[0] * v_lin[0] + v_lin[1] * v_lin[1] + v_lin[2] * v_lin[2] + 1.0)
-        s_pair, size_pair = split(s_one), split(size)
-        act = dot3(s_pair, u1[0]) + dot3(size_pair, u1[1]) + par[AT_C1 : AT_C1 + 1, :]
+        s_pair = split(jnp.concatenate([s_one, size], axis=1))
+        u1_pair = (u1[0 : 2 * F, :], u1[2 * F : 4 * F, :])
+        act = dot3(s_pair, u1_pair) + par[AT_C1 : AT_C1 + 1, :]
         gate = sigmoid(act)
         hidden = split(act * gate)
-        a1, a2, a3 = [dot3(hidden, u2[j]) + par[AT_C2 + j : AT_C2 + j + 1, :] for j in range(3)]
+        gating = linear(hidden, u2) + wide_row(par, AT_C2, 3)
+        a1, a2, a3 = [gating[:, j * F : (j + 1) * F] for j in range(3)]
         inner = v_lin[0] * w_lin[0] + v_lin[1] * w_lin[1] + v_lin[2] * w_lin[2]
         s_out = s_one + a3 + a2 * inner
         s_two[at, :] = s_out
@@ -432,30 +467,31 @@
             gv.append(cot_v[c, at, :])
         ga = [gv[0] * w_lin[0] + gv[1] * w_lin[1] + gv[2] * w_lin[2], gs * inner, gs]
         g_inner = gs * a2
-        ga_pair = [split(g) for g in ga]
-        for j in range(3):
-            add_column(gpar, AT_U2, 3, j, dot3(hidden, ga_pair[j], (0, 0)))
-            gpar[AT_C2 + j : AT_C2 + j + 1, :] += jnp.sum(ga[j], axis=0, keepdims=True)
-        g_hidden = (
-            dot3(ga_pair[0], u2[0], (1, 1))
-            + dot3(ga_pair[1], u2[1], (1, 1))
-            + dot3(ga_pair[2], u2[2], (1, 1))
-        )
-        g_act = g_hidden * (gate * (1.0 + act * (1.0 - gate)))
+        ga = jnp.concatenate(ga, axis=1)
+        ga_pair = split(ga)
+        add_matrix(gpar, AT_U2, 3, dot3(hidden, ga_pair, (0, 0)))
+        add_row(gpar, AT_C2, 3, ga)
+        g_act = back_through(ga_pair, u2) * (gate * (1.0 + act * (1.0 - gate)))
         g_act_pair = split(g_act)
-        add_column(gpar, AT_U1, 1, 0, dot3(s_pair, g_act_pair, (0, 0)))
-        add_column(gpar, AT_U1 + F, 1, 0, dot3(size_pair, g_act_pair, (0, 0)))
-        gpar[AT_C1 : AT_C1 + 1, :] += jnp.sum(g_act, axis=0, keepdims=True)
-        g_s_one = gs + dot3(g_act_pair, u1[0], (1, 1))
-        g_size = dot3(g_act_pair, u1[1], (1, 1)) / size
+        gpar[AT_U1 : AT_U1 + 2 * F, :] += dot3(s_pair, g_act_pair, (0, 0))
+        add_row(gpar, AT_C1, 1, g_act)
+        g_both = dot3(g_act_pair, u1_pair, (1, 1))
+        g_s_one = gs + g_both[:, :F]
+        g_size = g_both[:, F:] / size
         gs_own[at, :] = g_s_one
         down = [g_s_one]
         for c in range(3):
-            g_w = split(a1 * gv[c] + g_inner * v_lin[c])
-            g_v = split(g_inner * w_lin[c] + g_size * v_lin[c])
-            add_column(gpar, AT_WM, 2, 0, dot3(v_pair[c], g_v, (0, 0)))
-            add_column(gpar, AT_WM, 2, 1, dot3(v_pair[c], g_w, (0, 0)))
-            g_v_one = gv[c] + dot3(g_v, wm[0], (1, 1)) + dot3(g_w, wm[1], (1, 1))
+            g_mixed = split(
+                jnp.concatenate(
+                    [
+                        g_inner * w_lin[c] + g_size * v_lin[c],
+                        a1 * gv[c] + g_inner * v_lin[c],
+                    ],
+                    axis=1,
+                )
+            )
+            add_matrix(gpar, AT_WM, 2, dot3(v_pair[c], g_mixed, (0, 0)))
+            g_v_one = gv[c] + back_through(g_mixed, wm)
             gv_own[c, at, :] = g_v_one
             down.append(g_v_one)
         for k in range(4):
@@ -629,23 +665,19 @@
                     gv_ref[c, to, :] += gathered(3 + c)
                 else:
                     gv_ref[c, to, :] = gathered(3 + c)
-            w1 = split(column(par, AT_W1, 1, 0))
             s_pair = split(s_ref[to, :])
-            act = dot3(s_pair, w1) + par[AT_B1 : AT_B1 + 1, :]
+            act = linear(s_pair, w1) + par[AT_B1 : AT_B1 + 1, :]
             gate = sigmoid(act)
             hidden = split(act * gate)
-            g_hidden = jnp.zeros((ROWS, F), F32)
-            for j in range(3):
-                g_x = gathered(j)
-                g_pair = split(g_x)
-                add_column(gpar, AT_W2, 3, j, dot3(hidden, g_pair, (0, 0)))
-                gpar[AT_B2 + j : AT_B2 + j + 1, :] += jnp.sum(g_x, axis=0, keepdims=True)
-                g_hidden = g_hidden + dot3(g_pair, split(column(par, AT_W2, 3, j)), (1, 1))
-            g_act = g_hidden * (gate * (1.0 + act * (1.0 - gate)))
+            g_x = jnp.concatenate([gathered(j) for j in range(3)], axis=1)
+            g_pair = split(g_x)
+            add_matrix(gpar, AT_W2, 3, dot3(hidden, g_pair, (0, 0)))
+            add_row(gpar, AT_B2, 3, g_x)
+            g_act = back_through(g_pair, w2) * (gate * (1.0 + act * (1.0 - gate)))
             g_act_pair = split(g_act)
-            add_column(gpar, AT_W1, 1, 0, dot3(s_pair, g_act_pair, (0, 0)))
-            gpar[AT_B1 : AT_B1 + 1, :] += jnp.sum(g_act, axis=0, keepdims=True)
-            g_s = dot3(g_act_pair, w1, (1, 1))
+            add_matrix(gpar, AT_W1, 1, dot3(s_pair, g_act_pair, (0, 0)))
+            add_row(gpar, AT_B1, 1, g_act)
+            g_s = back_through(g_act_pair, w1)
             if own:
                 gs_ref[to, :] += g_s
             else:
@@ -689,6 +721,11 @@
         pltpu.VMEM((3 * F, F), BF16),
         pltpu.VMEM((48, 3 * F), F32),
         pltpu.VMEM((8, atoms), F32),
+        pltpu.VMEM((3 * F, F), BF16),
+        pltpu.VMEM((3 * F, 3 * F), BF16),
+        pltpu.VMEM((3 * F, 2 * F), BF16),
+        pltpu.VMEM((4 * F, F), BF16),
+        pltpu.VMEM((3 * F, 3 * F), BF16),
     ]
     return pl.pallas_call(
         layer_kernel,
@@ -696,7 +733,7 @@
         in_specs=[in_smem] * 3 + [in_vmem] * 13,
         out_specs=(in_vmem,) * len(outs),
         scratch_shapes=scratch,
-        compiler_params=pltpu.CompilerParams(vmem_limit_bytes=62 * 1024 * 1024),
+        compiler_params=pltpu.CompilerParams(vmem_limit_bytes=63 * 1024 * 1024),
         name="layer",
     )
 
@@ -1180,23 +1217,26 @@
 
     hops = range(2 * HOPS)
     copies = []
-    for j in hops:
-        exists, device = here.hop(-hop_offset(j))
-        block = pl.ds(j * cap, cap)
-        tile = pl.ds((j // 2) * F, F)
-        rows_copy = send(
-            g_halo.at[:, block], back.at[:, block], row_send.at[j], row_recv.at[j], device
-        )
-        place_copy = send(
-            gp_halo.at[:, tile], p_in.at[j], place_send.at[j], place_recv.at[j], device
-        )
-        copies += [(exists, rows_copy), (exists, place_copy)]
-
-        @pl.when(exists)
-        def _():
-            rows_copy.start()
-            place_copy.start()
-
+
+    def give_back(some):
+        for j in some:
+            exists, device = here.hop(-hop_offset(j))
+            block = pl.ds(j * cap, cap)
+            tile = pl.ds((j // 2) * F, F)
+            rows_copy = send(
+                g_halo.at[:, block], back.at[:, block], row_send.at[j], row_recv.at[j], device
+            )
+            place_copy = send(
+                gp_halo.at[:, tile], p_in.at[j], place_send.at[j], place_recv.at[j], device
+            )
+            copies.extend([(exists, rows_copy), (exists, place_copy)])
+
+            @pl.when(exists)
+            def _():
+                rows_copy.start()
+                place_copy.start()
+
+    give_back(BATCHES[0])
     for j in hops:
         known, device = here.hop(hop_offset(j))
 
@@ -1223,6 +1263,7 @@
             for k, g in enumerate(here.other_groups())
         ]
     )
+    give_back(BATCHES[1])
     total = slots[here.group, here.quarter, here.core]
     for g in here.other_groups():
         spot = spot_in.at[g]
@@ -1262,7 +1303,9 @@
         ]
         lines.append(jnp.zeros((1, F), F32))
     sums.start(0, jnp.concatenate(lines, axis=0))
+    give_back(BATCHES[2])
     sums.start(1, sums.finish(0))
+    give_back(BATCHES[3])
     whole = jnp.sqrt(jnp.sum(sums.finish(1), axis=1, keepdims=True))
     ratio = whole[0:8] / whole[8:16]
     norms[...] = jnp.broadcast_to(whole, (16, F))

time: 146 us -> 141 us (0.966)
  Pallas kernels: 144 us -> 139 us
    pallas_call x1, Pallas kernels: 36.8 us -> 32.1 us  [body(): reduce_all(cap, groups, length)]
where the time goes in v4:
time: 141 us; the launch traced here: 140 us
  Pallas kernels  139 us (99%)
  between operations  1.47 us (1%)
    pallas_call x1, Pallas kernels, body(): layer(atoms, halo, edges)  74.7 us
    pallas_call x1, Pallas kernels, body(): reduce_all(cap, groups, length)  32.1 us
    pallas_call x1, Pallas kernels, body(): gather_all(atoms, cap, groups, length, edges)  28.2 us
    pallas_call x1, Pallas kernels, body(): finish(atoms, length)  3.92 us

profile of v4, /device:TPU:0, one launch (start us, length us, event | category | flops | bytes accessed | tf_op | source)
XLA Modules:
  0.0 140.4 jit_solution(4103435743282787837)
XLA Ops:
  1.3 28.2 %gather_inputs.1 = (f32[1488,128]{1,0:T(8,128)}, f32[4,512,128]{2,1,0:T(8,128)}, f32[8,512]{1,0:T(8,128)}, f32[1,512]{1,0:T(1,128)}, f32[8,128]{1,0:T(8,128)}, /*index=5*/s32[64,128]{1,0:T(8,128)}) custom-call(s32[1,8,64]{2,1,0:T(8,128)} %send_rows.1, f32[5920]{0:T(1024)} %par.1, f32[512,128]{1,0:T(8,128)} %s_own.3, f32[3,512,128]{2,1,0:T(8,128)} %v_own.3, ...), custom_call_target="tpu_custom_call" | custom-call | tf_op jit(solution)/shard_map/gather_inputs/pallas_call | solution.py:1482
  29.5 74.7 %layer.1 = (f32[512,128]{1,0:T(8,128)}, f32[3,512,128]{2,1,0:T(8,128)}, f32[512,128]{1,0:T(8,128)}, f32[3,512,128]{2,1,0:T(8,128)}, f32[4,512,128]{2,1,0:T(8,128...) custom-call(s32[8192]{0:T(1024)} %dst_s.1, s32[1]{0:T(128)S(6)} %copy.32.count_s, s32[8192]{0:T(1024)} %bitcast.10, ...), custom_call_target="tpu_custom_call" | custom-call | tf_op jit(solution)/shard_map/layer/pallas_call | solution.py:1493
  104.3 32.1 %reduce_outputs.1 = (f32[4,512,128]{2,1,0:T(8,128)}, f32[8,512]{1,0:T(8,128)}, f32[4,48,128]{2,1,0:T(8,128)}, f32[16,128]{1,0:T(8,128)}) custom-call(f32[1488,128]{1,0:T(8,128)} %get-tuple-element.51.gpar, f32[4,512,128]{2,1,0:T(8,128)} %get-tuple-element.52.g_halo, f32[8,512]{1,0:T(8,128)} %get-tuple-element.53.gp_halo, f32[5920]{0:T(1024)} %par.1, ...), custom_call_target="tpu_custom_call" | custom-call | tf_op jit(solution)/shard_map/reduce_outputs/pallas_call | solution.py:1511
  136.3 3.9 %finish.1 = (f32[512,128]{1,0:T(8,128)}, f32[3,512,128]{2,1,0:T(8,128)}, f32[3,512]{1,0:T(4,128)}, f32[100]{0:T(128)}, f32[1]{0:T(128)}, /*index=5*/f32[5920]{0:...) custom-call(f32[4,512,128]{2,1,0:T(8,128)} %get-tuple-element.54.bac, ...), custom_call_target="tpu_custom_call" | custom-call | tf_op jit(solution)/shard_map/finish/pallas_call | solution.py:1527

commit v5 on v4

--- a/solution.py
+++ b/solution.py
@@ -35,6 +35,7 @@
 PARAM_PAD = PARAM_ROWS + 8
 GROUP_ENDS = (128, 512, 572, 828, 1084, 1468)
 MESH = pl.DeviceIdType.MESH
+SENT = ((3, 7, 2, 6), (1, 5, 0, 4), ())
 BATCHES = ((3, 7), (2, 6), (1, 5), (0, 4))
 
 
@@ -528,15 +529,20 @@
         gbuf[t] = fetch(t, window_range(i)[0])
         yield
 
+    def into_sources(i, t, one, two):
+        to = (source(i, one), source(i, two))
+        held = [(t * BLOCK + spot) * 8 for spot in (one, two)]
+        first = tab[to[0], :] + stage[held[0] : held[0] + 8, :]
+        second = acc[to[1], :] + stage[held[1] : held[1] + 8, :]
+        tab[to[0], :] = first
+        acc[to[1], :] = second
+
     def spread(i, t, earlier):
         for sub in range(BLOCK // SUB):
             at = slice(sub * SUB, (sub + 1) * SUB)
             for j in range(SUB // 2):
-                for k, total in enumerate((tab, acc)):
-                    spot = sub * SUB + k * (SUB // 2) + j
-                    held = (t * BLOCK + spot) * 8
-                    total[source(earlier, spot), :] += stage[held : held + 8, :]
-                if j % 8 == 7:
+                into_sources(earlier, t, sub * SUB + j, sub * SUB + SUB // 2 + j)
+                if j % 4 == 3:
                     yield
             to = [pl.ds(t * (BLOCK * 8) + sub * (SUB * 8) + k, SUB, stride=8) for k in range(6)]
             g_s = gbuf[t, at, 0:F]
@@ -621,7 +627,7 @@
         for t in range(PAIR):
             i = step * PAIR + t
             before, after = jnp.maximum(i - 1, 0), jnp.minimum(i + 1, blocks - 1)
-            weave(spread(i, t, jnp.maximum(i - 2, 0)), settle(before, 1 - t), prepare(after, 1 - t))
+            weave(prepare(after, 1 - t), settle(before, 1 - t), spread(i, t, jnp.maximum(i - 2, 0)))
             prepare_more(after, 1 - t)
             settle_more(before, 1 - t)
 
@@ -629,10 +635,7 @@
     settle_more(blocks - 1, PAIR - 1)
     for t in range(PAIR):
         for j in range(BLOCK // 2):
-            for k, total in enumerate((tab, acc)):
-                spot = k * (BLOCK // 2) + j
-                held = (t * BLOCK + spot) * 8
-                total[source(blocks - PAIR + t, spot), :] += stage[held : held + 8, :]
+            into_sources(blocks - PAIR + t, t, j, BLOCK // 2 + j)
 
     for j in range(3):
         total = gwf[0:24, j * F : (j + 1) * F] + gwf[24:48, j * F : (j + 1) * F]
@@ -996,23 +999,26 @@
     )
     sums.start(0, tile)
     row_copies, place_copies = [], []
-    for j in hops:
-        exists, device = here.hop(hop_offset(j))
-        block = pl.ds(j * cap, cap)
-        rows_copy = send(
-            pack.at[:, block], halo_rows.at[:, block], row_send.at[j], row_recv.at[j], device
-        )
-        place_copy = send(
-            p_in.at[2 * HOPS + j // 2], p_in.at[j], place_send.at[j], place_recv.at[j], device
-        )
-        row_copies.append((exists, rows_copy))
-        place_copies.append((exists, place_copy))
-
-        @pl.when(exists)
-        def _():
-            rows_copy.start()
-            place_copy.start()
-
+
+    def give(some):
+        for j in some:
+            exists, device = here.hop(hop_offset(j))
+            block = pl.ds(j * cap, cap)
+            rows_copy = send(
+                pack.at[:, block], halo_rows.at[:, block], row_send.at[j], row_recv.at[j], device
+            )
+            place_copy = send(
+                p_in.at[2 * HOPS + j // 2], p_in.at[j], place_send.at[j], place_recv.at[j], device
+            )
+            row_copies.append((exists, rows_copy))
+            place_copies.append((exists, place_copy))
+
+            @pl.when(exists)
+            def _():
+                rows_copy.start()
+                place_copy.start()
+
+    give(SENT[0])
     for j in hops:
         known, device = here.hop(-hop_offset(j))
 
@@ -1042,6 +1048,7 @@
         )
     ]
     third[0].start()
+    give(SENT[1])
     sums.start(1, sums.finish(0))
     for k, q in enumerate(here.other_quarters()):
         line = slots.at[:, q, here.core]
@@ -1051,6 +1058,7 @@
         )
         copy.start()
         third.append(copy)
+    give(SENT[2])
     for q in range(4):
         line = slots.at[:, q, here.mate]
         send(line, line, ag_send.at[0], ag_recv.at[base + 4 + q], here.beside()).wait_recv()
@@ -1407,13 +1415,11 @@
     pick = jnp.concatenate([send_rows[0, j : j + 1, :] for j in range(2 * HOPS)], axis=1)
     hot = jnp.where(pick == lax.broadcasted_iota(jnp.int32, (atoms, halo), 0), 1.0, 0.0)
     hot = hot.astype(BF16)
-    for k in range(4):
-        high, low = split(back[k])
-        extra = mm(hot, high) + mm(hot, low)
-        if k == 0:
-            grad_s[...] = gs_own[...] + extra
-        else:
-            grad_v[k - 1] = gv_own[k - 1] + extra
+    high, low = split(jnp.concatenate([back[k] for k in range(4)], axis=1))
+    extra = mm(hot, high) + mm(hot, low)
+    grad_s[...] = gs_own[...] + extra[:, :F]
+    for c in range(3):
+        grad_v[c] = gv_own[c] + extra[:, (c + 1) * F : (c + 2) * F]
     place = p_back[...]
     high = place.astype(BF16).astype(F32)
     middle = (place - high).astype(BF16).astype(F32)

time: 141 us -> 139 us (0.986)
    pallas_call x1, Pallas kernels: 32.1 us -> 33.8 us  [body(): reduce_all(cap, groups, length)]
    pallas_call x1, Pallas kernels: 28.2 us -> 26.5 us  [body(): gather_all(atoms, cap, groups, length, edges)]
where the time goes in v5:
time: 139 us
  Pallas kernels  138 us (99%)
  between operations  1.47 us (1%)
    pallas_call x1, Pallas kernels, body(): layer(atoms, halo, edges)  73.9 us
    pallas_call x1, Pallas kernels, body(): reduce_all(cap, groups, length)  33.8 us
    pallas_call x1, Pallas kernels, body(): gather_all(atoms, cap, groups, length, edges)  26.5 us
    pallas_call x1, Pallas kernels, body(): finish(atoms, length)  3.37 us

profile of v5, /device:TPU:0, one launch (start us, length us, event | category | flops | bytes accessed | tf_op | source)
XLA Modules:
  0.0 139.1 jit_solution(12647994886998029826)
XLA Ops:
  1.3 26.5 %gather_inputs.1 = (f32[1488,128]{1,0:T(8,128)}, f32[4,512,128]{2,1,0:T(8,128)}, f32[8,512]{1,0:T(8,128)}, f32[1,512]{1,0:T(1,128)}, f32[8,128]{1,0:T(8,128)}, /*index=5*/s32[64,128]{1,0:T(8,128)}) custom-call(s32[1,8,64]{2,1,0:T(8,128)} %send_rows.1, f32[5920]{0:T(1024)} %par.1, f32[512,128]{1,0:T(8,128)} %s_own.3, f32[3,512,128]{2,1,0:T(8,128)} %v_own.3, ...), custom_call_target="tpu_custom_call" | custom-call | tf_op jit(solution)/shard_map/gather_inputs/pallas_call | solution.py:1488
  27.8 73.9 %layer.1 = (f32[512,128]{1,0:T(8,128)}, f32[3,512,128]{2,1,0:T(8,128)}, f32[512,128]{1,0:T(8,128)}, f32[3,512,128]{2,1,0:T(8,128)}, f32[4,512,128]{2,1,0:T(8,128...) custom-call(s32[8192]{0:T(1024)} %dst_s.1, s32[1]{0:T(128)S(6)} %copy.32.count_s, s32[8192]{0:T(1024)} %bitcast.10, ...), custom_call_target="tpu_custom_call" | custom-call | tf_op jit(solution)/shard_map/layer/pallas_call | solution.py:1499
  101.8 33.8 %reduce_outputs.1 = (f32[4,512,128]{2,1,0:T(8,128)}, f32[8,512]{1,0:T(8,128)}, f32[4,48,128]{2,1,0:T(8,128)}, f32[16,128]{1,0:T(8,128)}) custom-call(f32[1488,128]{1,0:T(8,128)} %get-tuple-element.51.gpar, f32[4,512,128]{2,1,0:T(8,128)} %get-tuple-element.52.g_halo, f32[8,512]{1,0:T(8,128)} %get-tuple-element.53.gp_halo, f32[5920]{0:T(1024)} %par.1, ...), custom_call_target="tpu_custom_call" | custom-call | tf_op jit(solution)/shard_map/reduce_outputs/pallas_call | solution.py:1517
  135.6 3.4 %finish.1 = (f32[512,128]{1,0:T(8,128)}, f32[3,512,128]{2,1,0:T(8,128)}, f32[3,512]{1,0:T(4,128)}, f32[100]{0:T(128)}, f32[1]{0:T(128)}, /*index=5*/f32[5920]{0:...) custom-call(f32[4,512,128]{2,1,0:T(8,128)} %get-tuple-element.54.bac, ...), custom_call_target="tpu_custom_call" | custom-call | tf_op jit(solution)/shard_map/finish/pallas_call | solution.py:1533

commit v6 on v5

--- a/solution.py
+++ b/solution.py
@@ -286,6 +286,12 @@
             if j % 16 == 15:
                 yield
 
+    def clear(ref, i):
+        each = ref.shape[0] // blocks // 8
+        for k in range(8):
+            ref[rows_of((i * 8 + k) * each, each, each), :] = jnp.zeros((each, F), F32)
+            yield
+
     def ends(i):
         got = ends_in(i, window_range(i)[0])
         yield
@@ -309,7 +315,7 @@
     def _(step):
         for t in range(PAIR):
             i = step * PAIR + t
-            weave(ends(i), places_of(jnp.maximum(i - 1, 0)), gather(i))
+            weave(ends(i), places_of(jnp.maximum(i - 1, 0)), gather(i), clear(acc, i))
             first, last = window_range(i)
 
             @pl.loop(first + 1, last + 1)
@@ -429,6 +435,7 @@
                 filters(jnp.minimum(i + 1, blocks - 1), 1 - t),
                 collect(before, 1 - t, window_range(before)[0]),
                 messages(i, t),
+                clear(tab, i),
             )
             collect_more(before, 1 - t)
 
@@ -504,7 +511,7 @@
                 gd[rows_of(to + WINDOW, WINDOW, WINDOW), k * F : (k + 1) * F] = low[of]
 
     twice = (lax.broadcasted_iota(jnp.int32, (1, 2 * WINDOW), 1) % WINDOW).astype(F32)
-    for ref in (tab, acc, stage, mbuf, tbuf, turn_buf):
+    for ref in (stage, mbuf, tbuf, turn_buf):
         ref[...] = jnp.zeros_like(ref)
 
     def collect_places(i, t, w):
@@ -899,8 +906,8 @@
 def gather_kernel(
     send_s,
     par_in,
-    s_own,
-    v_own,
+    s_h,
+    v_h,
     p_own,
     energy,
     elements,
@@ -912,6 +919,9 @@
     goal,
     stats,
     src_tiles,
+    s_own,
+    v_own,
+    own_sem,
     slots,
     pack,
     places,
@@ -932,6 +942,12 @@
     atoms = s_own.shape[0]
     cap = halo_rows.shape[1] // (2 * HOPS)
     wide = slots.shape[3]
+    loads = [
+        pltpu.make_async_copy(s_h, s_own, own_sem.at[0]),
+        pltpu.make_async_copy(v_h, v_own, own_sem.at[1]),
+    ]
+    for load in loads:
+        load.start()
     expected = here.greet()
     sums = SmallSum(here, *small)
 
@@ -972,6 +988,8 @@
         jnp.concatenate([p_own[...], jnp.zeros((F - 3, atoms), F32)], axis=0)
     )
     zeros[...] = jnp.zeros_like(zeros)
+    for load in loads:
+        load.wait()
     hops = range(2 * HOPS)
     for j in hops:
 
@@ -1125,9 +1143,12 @@
             shape((8, F), F32),
             shape((edges // F, F), jnp.int32),
         ),
-        in_specs=[in_smem] + [in_vmem] * 8,
+        in_specs=[in_smem, in_vmem] + [pl.BlockSpec(memory_space=pl.ANY)] * 2 + [in_vmem] * 5,
         out_specs=(in_vmem, pl.BlockSpec(memory_space=pl.ANY)) + (in_vmem,) * 4,
         scratch_shapes=[
+            pltpu.VMEM((atoms, F), F32),
+            pltpu.VMEM((3, atoms, F), F32),
+            pltpu.SemaphoreType.DMA((2,)),
             pltpu.VMEM((groups, 4, 2, wide, F), F32),
             pltpu.VMEM((4, halo, F), F32),
             pltpu.VMEM((atoms, F), F32),
@@ -1151,7 +1172,7 @@
 
 
 def reduce_kernel(
-    gpar,
+    gpar_h,
     g_halo,
     gp_halo,
     par,
@@ -1161,6 +1182,8 @@
     p_back,
     shares,
     norms,
+    gpar,
+    gpar_sem,
     slots,
     pair_in,
     line_in,
@@ -1181,7 +1204,10 @@
     here = Place()
     cap = back.shape[1] // (2 * HOPS)
     wide = slots.shape[3]
+    load = pltpu.make_async_copy(gpar_h, gpar, gpar_sem)
+    load.start()
     expected = here.greet()
+    load.wait()
     sums = SmallSum(here, *small)
 
     for p in range(here.count):
@@ -1361,9 +1387,11 @@
             shape((4, wide, F), F32),
             shape((16, F), F32),
         ),
-        in_specs=[in_vmem, in_any] + [in_vmem] * 4,
+        in_specs=[in_any] * 2 + [in_vmem] * 4,
         out_specs=(in_any, in_vmem, in_vmem, in_vmem),
         scratch_shapes=[
+            pltpu.VMEM((PARAM_PAD, F), F32),
+            pltpu.SemaphoreType.DMA(()),
             pltpu.VMEM((groups, 4, 2, wide, F), F32),
             pltpu.VMEM((groups, 4, wide, F), F32),
             pltpu.VMEM((4, groups, wide, F), F32),

time: 139 us -> 139 us (level)
  no operation moved by 1% of the time
where the time goes in v6:
time: 139 us
  Pallas kernels  137 us (99%)
  between operations  1.47 us (1%)
    pallas_call x1, Pallas kernels, body(): layer(atoms, halo, edges)  73.7 us
    pallas_call x1, Pallas kernels, body(): reduce_all(cap, groups, length)  33.6 us
    pallas_call x1, Pallas kernels, body(): gather_all(atoms, cap, groups, length, edges)  26.7 us
    pallas_call x1, Pallas kernels, body(): finish(atoms, length)  3.37 us

profile of v6, /device:TPU:0, one launch (start us, length us, event | category | flops | bytes accessed | tf_op | source)
XLA Modules:
  0.0 138.8 jit_solution(7247988768257865449)
XLA Ops:
  1.3 26.7 %gather_inputs.1 = (f32[1488,128]{1,0:T(8,128)}, f32[4,512,128]{2,1,0:T(8,128)}, f32[8,512]{1,0:T(8,128)}, f32[1,512]{1,0:T(1,128)}, f32[8,128]{1,0:T(8,128)}, /*index=5*/s32[64,128]{1,0:T(8,128)}) custom-call(s32[1,8,64]{2,1,0:T(8,128)} %send_rows.1, f32[5920]{0:T(1024)} %par.1, f32[512,128]{1,0:T(8,128)} %s_own.1, f32[3,512,128]{2,1,0:T(8,128)} %v_own.1, ...), custom_call_target="tpu_custom_call" | custom-call | tf_op jit(solution)/shard_map/gather_inputs/pallas_call | solution.py:1516
  28.0 73.7 %layer.1 = (f32[512,128]{1,0:T(8,128)}, f32[3,512,128]{2,1,0:T(8,128)}, f32[512,128]{1,0:T(8,128)}, f32[3,512,128]{2,1,0:T(8,128)}, f32[4,512,128]{2,1,0:T(8,128...) custom-call(s32[8192]{0:T(1024)} %dst_s.1, s32[1]{0:T(128)S(6)} %copy.32.count_s, s32[8192]{0:T(1024)} %bitcast.10, ...), custom_call_target="tpu_custom_call" | custom-call | tf_op jit(solution)/shard_map/layer/pallas_call | solution.py:1527
  101.7 33.6 %reduce_outputs.1 = (f32[4,512,128]{2,1,0:T(8,128)}, f32[8,512]{1,0:T(8,128)}, f32[4,48,128]{2,1,0:T(8,128)}, f32[16,128]{1,0:T(8,128)}) custom-call(f32[1488,128]{1,0:T(8,128)} %get-tuple-element.51.gpar_h, f32[4,512,128]{2,1,0:T(8,128)} %get-tuple-element.52.g_halo, f32[8,512]{1,0:T(8,128)} %get-tuple-element.53.gp_halo, f32[5920]{0:T(1024)} %par.1, ...), custom_call_target="tpu_custom_call" | custom-call | tf_op jit(solution)/shard_map/reduce_outputs/pallas_call | solution.py:1545
  135.3 3.4 %finish.1 = (f32[512,128]{1,0:T(8,128)}, f32[3,512,128]{2,1,0:T(8,128)}, f32[3,512]{1,0:T(4,128)}, f32[100]{0:T(128)}, f32[1]{0:T(128)}, /*index=5*/f32[5920]{0:...) custom-call(f32[4,512,128]{2,1,0:T(8,128)} %get-tuple-element.54.bac, ...), custom_call_target="tpu_custom_call" | custom-call | tf_op jit(solution)/shard_map/finish/pallas_call | solution.py:1561
